TPU v7x, 256 devices: a whole 4x4x8 slice. The times are simulated.
256 devices in a mesh: step: 8 (over x, core), frame: 32 (over z, y).
Axes of the slice: x: 4, y: 4, z: 8, core: 2. Of those that a mesh axis runs over, the one named last changes fastest.
Arguments:
- latents: bfloat16 [8, 8192, 1536], P('step', 'frame')
- anchor: float32 [8192, 1536], P('frame'), may hold values from -6 to 6
- step_index: int32 [8], replicated, may hold values from 0 to 49, as said below
- modulation: float32 [50, 3, 1536], replicated, may hold values from -3 to 3
- step_sizes: float32 [50], replicated, may hold values from 0.02 to 0.2
- input_weight: bfloat16 [1536, 2304], P(('step', 'frame'))
- output_weight: bfloat16 [768, 1536], P(('step', 'frame')), may hold values from -0.21875 to 0.21875
- norm_gain: float32 [2, 768], replicated, may hold values from 1 to 8, as said below
- block_mask: int32 [64, 64], P('frame'), may hold values from 0 to 1, as said below
Outputs:
- velocity: bfloat16 [8, 8192, 1536], P('step', 'frame')
- advanced: float32 [8, 8192, 1536], P('step', 'frame')
Inputs may be any that keep to these rules, and one draw needn't show every extreme that they name: `step_index`: the 8 values are distinct; 0 and 49 are always among them. `norm_gain`: positive. A frame slab is 2 consecutive blocks. block_mask[b, b] = 1 for every block b, and block_mask[a, b] = 0 unless the slabs of a and b are equal or a power of two apart.
All inputs are finite; a program needn't handle non-finite values.
Results may differ from a plain program's by a relative error of at most 0.0068.
Values may be sent and summed in bfloat16 or wider, within the bound.
No kernel may reach another device: no remote copies, remote signals or barrier semaphores. Data moves between devices by JAX's collectives and lax.ppermute only.
A program may use at most 64 MiB of HBM per device.

v0:
```python
import functools
import math

import jax
import jax.numpy as jnp
from jax import lax
from jax.experimental import pallas as pl
from jax.experimental.pallas import tpu as pltpu
from jax.sharding import PartitionSpec as P

HD = 128
BLK = 128
NX, NY, NZ = 4, 4, 8
NORM_EPS = 1e-06
F32 = jnp.float32
BF16 = jnp.bfloat16
VMEM_LIMIT = 56 * 1024 * 1024


def y_shift(block, distance):
    pairs = [(4 * z + y, 4 * z + (y + distance) % NY) for z in range(NZ) for y in range(NY)]
    return lax.ppermute(block, "frame", pairs)


def z_shift(block, distance):
    pairs = [(4 * z + y, 4 * ((z + distance) % NZ) + y) for z in range(NZ) for y in range(NY)]
    return lax.ppermute(block, "frame", pairs)


def x_shift(block, distance):
    pairs = [(2 * x + c, 2 * ((x + distance) % NX) + c) for x in range(NX) for c in range(2)]
    return lax.ppermute(block, "step", pairs)


def x_later(block, distance):
    pairs = [(2 * x + c, 2 * (x + distance) + c) for x in range(NX - distance) for c in range(2)]
    return lax.ppermute(block, "step", pairs)


def core_swap(block):
    return lax.ppermute(block, "step", [(i, i ^ 1) for i in range(2 * NX)])


def modulate_kernel(where_ref, index_ref, latent_ref, table_ref, out_ref, row_s, sem):
    own = index_ref[where_ref[0]]
    copies = [
        pltpu.make_async_copy(table_ref.at[i, pl.ds(own, 1)], row_s.at[i], sem.at[i])
        for i in range(2)
    ]
    for copy in copies:
        copy.start()
    value = latent_ref[...].astype(F32)
    centered = value - jnp.mean(value, axis=-1, keepdims=True)
    variance = jnp.mean(centered * centered, axis=-1, keepdims=True)
    normed = centered * lax.rsqrt(variance + NORM_EPS)
    for copy in copies:
        copy.wait()
    out_ref[...] = (normed * (1.0 + row_s[1]) + row_s[0]).astype(BF16)


def modulate(where, step_index, latent, table):
    rows, width = latent.shape
    return pl.pallas_call(
        modulate_kernel,
        in_specs=[
            pl.BlockSpec(memory_space=pltpu.SMEM),
            pl.BlockSpec(memory_space=pltpu.SMEM),
            pl.BlockSpec(memory_space=pltpu.VMEM),
            pl.BlockSpec(memory_space=pl.ANY),
        ],
        out_specs=pl.BlockSpec(memory_space=pltpu.VMEM),
        out_shape=jax.ShapeDtypeStruct((rows, width), BF16),
        scratch_shapes=[pltpu.VMEM((2, 1, width), F32), pltpu.SemaphoreType.DMA((2,))],
        name="modulate",
    )(where, step_index, latent, table)


N_SLABS = 10


def attend_kernel(
    where_ref,
    mask_ref,
    gain_ref,
    *refs,
):
    slabs = refs[:9]
    z4_top, z4_bottom = refs[9:11]
    pieces = refs[11:21]
    keep_ref, send_ref = refs[21:23]
    m_s, w_s, k_s, v_s, q_s, bias_s, m_sem, w_sem = refs[23:]
    x, core, frame = where_ref[1], where_ref[2], where_ref[3]
    rows = q_s.shape[0]
    feats = q_s.shape[1]
    half = rows // 2

    copies_m = []
    for i in range(9):
        copies_m.append(pltpu.make_async_copy(slabs[i], m_s.at[pl.ds(i * rows, rows)], m_sem.at[i]))
    copies_m.append(pltpu.make_async_copy(z4_top, m_s.at[pl.ds(9 * rows, half)], m_sem.at[9]))
    copies_m.append(
        pltpu.make_async_copy(z4_bottom, m_s.at[pl.ds(9 * rows + half, half)], m_sem.at[10])
    )
    depth = w_s.shape[0] // (2 * NX)
    copies_w = []
    for who in range(2):
        for i, distance in enumerate((0, -1, 1, 2, 2)):
            piece = pieces[who * 5 + i]
            from_x = lax.rem(x + distance + NX, NX)
            from_core = core if who == 0 else 1 - core
            start = (2 * from_x + from_core) * depth
            if i == 4:
                start = start + depth // 2
            start = pl.multiple_of(start, 16)
            copies_w.append(
                pltpu.make_async_copy(
                    piece, w_s.at[pl.ds(start, piece.shape[0])], w_sem.at[who * 5 + i]
                )
            )
    copies_m[0].start()
    for copy in copies_w:
        copy.start()
    for copy in copies_m[1:]:
        copy.start()

    low = lax.rem(frame, NY) < 2
    two_a = jnp.where(low, 2, -2)
    offsets = (0, -4, 4, two_a, -8, 8, -1, 1, -two_a)
    for i in range(N_SLABS):
        if i < 9:
            source = frame + offsets[i]
        else:
            source = lax.rem(frame + 16, 32)
        inside = jnp.logical_and(source >= 0, source < 32)
        source = jnp.clip(source, 0, 31)
        for q_block in range(2):
            for k_block in range(2):
                ok = jnp.logical_and(inside, mask_ref[q_block, 2 * source + k_block] > 0)
                bias_s[q_block : q_block + 1, pl.ds(i * rows + k_block * BLK, BLK)] = jnp.full(
                    (1, BLK), jnp.where(ok, 0.0, -jnp.inf), F32
                )

    def rms(value, gain):
        square = jnp.mean(value * value, axis=-1, keepdims=True)
        return (value * lax.rsqrt(square + NORM_EPS) * gain).astype(BF16)

    copies_m[0].wait()
    for copy in copies_w:
        copy.wait()
    projected = jnp.dot(m_s[0:rows], w_s[:, 0:feats], preferred_element_type=F32)
    q_s[...] = rms(projected, gain_ref[0:1, :])
    for copy in copies_m[1:]:
        copy.wait()

    span = 2 * rows

    def project(i, carry):
        at = pl.ds(pl.multiple_of(i * span, span), span)
        block = m_s[at]
        keys = jnp.dot(block, w_s[:, feats : 2 * feats], preferred_element_type=F32)
        k_s[at] = rms(keys, gain_ref[1:2, :])
        values = jnp.dot(block, w_s[:, 2 * feats :], preferred_element_type=F32)
        v_s[at] = values.astype(BF16)
        return carry

    lax.fori_loop(0, N_SLABS // 2, project, 0)

    factor = 1.0 / math.sqrt(HD)
    for out_ref, q_block in ((send_ref, 1 - core), (keep_ref, core)):
        at = pl.ds(pl.multiple_of(q_block * BLK, BLK), BLK)
        bias = bias_s[pl.ds(q_block, 1), :]
        for head in range(feats // HD):
            cols = slice(head * HD, (head + 1) * HD)
            scores = lax.dot_general(
                q_s[at, cols], k_s[:, cols], (((1,), (1,)), ((), ())), preferred_element_type=F32
            )
            scores = scores * factor + bias
            peak = jnp.max(scores, axis=-1, keepdims=True)
            terms = jnp.exp(scores - peak)
            total = jnp.sum(terms, axis=-1, keepdims=True)
            mixed = jnp.dot(terms.astype(BF16), v_s[:, cols], preferred_element_type=F32)
            out_ref[:, cols] = (mixed / total).astype(BF16)


def attend(where, block_mask, norm_gain, slabs, pieces):
    rows, width = slabs[0].shape
    feats = norm_gain.shape[1]
    keys = N_SLABS * rows
    any_spec = pl.BlockSpec(memory_space=pl.ANY)
    smem = pl.BlockSpec(memory_space=pltpu.SMEM)
    return pl.pallas_call(
        attend_kernel,
        in_specs=[smem, smem, pl.BlockSpec(memory_space=pltpu.VMEM)]
        + [any_spec] * (len(slabs) + len(pieces)),
        out_specs=[pl.BlockSpec(memory_space=pltpu.VMEM)] * 2,
        out_shape=[jax.ShapeDtypeStruct((BLK, feats), BF16)] * 2,
        scratch_shapes=[
            pltpu.VMEM((keys, width), BF16),
            pltpu.VMEM((width, 3 * feats), BF16),
            pltpu.VMEM((keys, feats), BF16),
            pltpu.VMEM((keys, feats), BF16),
            pltpu.VMEM((rows, feats), BF16),
            pltpu.VMEM((2, keys), F32),
            pltpu.SemaphoreType.DMA((11,)),
            pltpu.SemaphoreType.DMA((10,)),
        ],
        compiler_params=pltpu.CompilerParams(vmem_limit_bytes=VMEM_LIMIT),
        cost_estimate=pl.CostEstimate(
            flops=16_000_000_000, bytes_accessed=16_000_000, transcendentals=4_000_000
        ),
        name="attend",
    )(where, block_mask, norm_gain, *slabs, *pieces)


def output_kernel(where_ref, index_ref, size_ref, keep_ref, got_ref, table_ref, *refs):
    pieces = refs[:4]
    own_ref, other_ref, total_ref, w_s, row_s, sem, row_sem = refs[4:]
    step, x, core = where_ref[0], where_ref[1], where_ref[2]
    own_index = index_ref[step]
    other_index = index_ref[step + 1 - 2 * core]
    depth = w_s.shape[0] // (2 * NX)
    copies = []
    for who in range(2):
        for i, distance in enumerate((0, -1, 1, 2)):
            from_x = lax.rem(x + distance + NX, NX)
            from_core = core if who == 0 else 1 - core
            start = pl.multiple_of((2 * from_x + from_core) * depth, 16)
            copies.append(
                pltpu.make_async_copy(
                    pieces[i].at[who], w_s.at[pl.ds(start, depth)], sem.at[who * 4 + i]
                )
            )
    for i, index in enumerate((own_index, other_index)):
        copies.append(
            pltpu.make_async_copy(table_ref.at[2, pl.ds(index, 1)], row_s.at[i], row_sem.at[i])
        )
    for copy in copies:
        copy.start()
    for copy in copies:
        copy.wait()
    weight = w_s[...]
    own = jnp.dot(keep_ref[...], weight, preferred_element_type=F32)
    own = (row_s[0] * own).astype(BF16)
    other = jnp.dot(got_ref[...], weight, preferred_element_type=F32)
    other = (row_s[1] * other).astype(BF16)
    own_ref[...] = own
    other_ref[...] = other
    total_ref[...] = (
        size_ref[own_index] * own.astype(F32) + size_ref[other_index] * other.astype(F32)
    ).astype(BF16)


def output(where, step_index, step_sizes, keep, got, table, pieces):
    half, feats = keep.shape
    width = table.shape[2]
    any_spec = pl.BlockSpec(memory_space=pl.ANY)
    vmem = pl.BlockSpec(memory_space=pltpu.VMEM)
    smem = pl.BlockSpec(memory_space=pltpu.SMEM)
    return pl.pallas_call(
        output_kernel,
        in_specs=[smem, smem, smem, vmem, vmem] + [any_spec] * 5,
        out_specs=[vmem] * 3,
        scratch_shapes=[
            pltpu.VMEM((feats, width), BF16),
            pltpu.VMEM((2, 1, width), F32),
            pltpu.SemaphoreType.DMA((8,)),
            pltpu.SemaphoreType.DMA((2,)),
        ],
        out_shape=[jax.ShapeDtypeStruct((half, width), BF16)] * 3,
        compiler_params=pltpu.CompilerParams(vmem_limit_bytes=VMEM_LIMIT),
        name="output",
    )(where, step_index, step_sizes, keep, got, table, *pieces)


def earlier_kernel(where_ref, index_ref, size_ref, one_ref, two_ref, three_ref, own_ref, out_ref):
    core = where_ref[2]
    size = jnp.where(core == 0, size_ref[index_ref[where_ref[0]]], 0.0)
    total = one_ref[...].astype(F32) + two_ref[...].astype(F32) + three_ref[...].astype(F32)
    out_ref[...] = (total + size * own_ref[...].astype(F32)).astype(BF16)


def earlier_sum(where, step_index, step_sizes, one, two, three, own):
    vmem = pl.BlockSpec(memory_space=pltpu.VMEM)
    smem = pl.BlockSpec(memory_space=pltpu.SMEM)
    return pl.pallas_call(
        earlier_kernel,
        in_specs=[smem, smem, smem] + [vmem] * 4,
        out_specs=vmem,
        out_shape=jax.ShapeDtypeStruct(own.shape, BF16),
        name="earlier_sum",
    )(where, step_index, step_sizes, one, two, three, own)


def advance_kernel(
    where_ref,
    index_ref,
    size_ref,
    one_ref,
    two_ref,
    three_ref,
    own_ref,
    other_ref,
    before_ref,
    rest_ref,
    anchor_ref,
    velocity_ref,
    advanced_ref,
):
    step, core = where_ref[0], where_ref[2]
    half = own_ref.shape[0]
    size_own = size_ref[index_ref[step]]
    size_other = jnp.where(core == 1, size_ref[index_ref[step + 1 - 2 * core]], 0.0)
    near = pl.ds(pl.multiple_of(core * half, half), half)
    far = pl.ds(pl.multiple_of((1 - core) * half, half), half)
    own = own_ref[...]
    velocity_ref[near] = own
    total = one_ref[...].astype(F32) + two_ref[...].astype(F32) + three_ref[...].astype(F32)
    total = total + size_other * other_ref[...].astype(F32) + size_own * own.astype(F32)
    advanced_ref[near] = anchor_ref[near] + total
    rest = rest_ref[...]
    velocity_ref[far] = rest
    advanced_ref[far] = (
        anchor_ref[far] + before_ref[...].astype(F32) + size_own * rest.astype(F32)
    )


def advance(where, step_index, step_sizes, one, two, three, own, other, before, rest, anchor):
    vmem = pl.BlockSpec(memory_space=pltpu.VMEM)
    smem = pl.BlockSpec(memory_space=pltpu.SMEM)
    return pl.pallas_call(
        advance_kernel,
        in_specs=[smem, smem, smem] + [vmem] * 8,
        out_specs=[vmem] * 2,
        out_shape=[
            jax.ShapeDtypeStruct(anchor.shape, BF16),
            jax.ShapeDtypeStruct(anchor.shape, F32),
        ],
        name="advance",
    )(where, step_index, step_sizes, one, two, three, own, other, before, rest, anchor)


def placed_y(parts, own):
    result = jnp.zeros((NZ, NY, 8, parts[0].shape[1]), BF16)
    for i, part in enumerate(parts):
        part = part.reshape(NZ, 1, 8, -1)
        result = lax.dynamic_update_slice_in_dim(result, part, lax.rem(own + i, NY), 1)
    return result


def on_device(
    latents,
    anchor,
    step_index,
    modulation,
    step_sizes,
    input_weight,
    output_weight,
    norm_gain,
    block_mask,
):
    latent = latents[0]
    rows, width = latent.shape
    step = lax.axis_index("step")
    frame = lax.axis_index("frame")
    x, core = step // 2, lax.rem(step, 2)
    z, y = frame // NY, lax.rem(frame, NY)
    where_am_i = jnp.stack([step, x, core, frame]).astype(jnp.int32)

    table = jnp.transpose(modulation, (1, 0, 2))

    out_width = output_weight.shape[1]
    packed = jnp.concatenate([input_weight, output_weight.reshape(2, -1)], axis=0)
    modulated = modulate(where_am_i, step_index, latent, table)
    packed, modulated = lax.optimization_barrier((packed, modulated))
    zp, zm = z_shift(modulated, 1), z_shift(modulated, -1)
    two_a = y_shift(modulated, 2)
    columns_z = [[NY * i + j for i in range(NZ)] for j in range(NY)]
    column = lax.all_to_all(
        jnp.broadcast_to(packed[None], (NZ,) + packed.shape),
        "frame",
        0,
        0,
        axis_index_groups=columns_z,
    ).reshape(8 * NZ, -1)
    column, zp, zm, two_a = lax.optimization_barrier((column, zp, zm, two_a))

    zp2, zm2 = z_shift(zp, 1), z_shift(zm, -1)
    plane = placed_y([column] + [y_shift(column, -d) for d in range(1, NY)], y)
    plane, zp2, zm2 = lax.optimization_barrier((plane, zp2, zm2))
    in_rows = plane[:, :, :6].reshape(192, -1)
    out_rows = plane[:, :, 6:].reshape(96, out_width)

    left, right = x_shift(in_rows, 1), x_shift(in_rows, -1)

    before = y_shift(jnp.where(y == NY - 1, zp, modulated), 1)
    after = y_shift(jnp.where(y == 0, zm, modulated), -1)
    z4_top = z_shift(zp2[: rows // 2], 2)
    in_rows, out_rows, left, right, before, after, z4_top, zm2, zp, zm = lax.optimization_barrier(
        (in_rows, out_rows, left, right, before, after, z4_top, zm2, zp, zm)
    )
    far_top = x_shift(left[:96], 1)
    far_bottom = x_shift(right[96:], -1)
    z4_bottom = z_shift(zm2[rows // 2 :], -2)
    two_b = y_shift(jnp.where(y >= 2, zp, zm), 2)
    near = [core_swap(piece) for piece in (in_rows, left, right)]
    out_rows = jnp.stack([out_rows, core_swap(out_rows)])
    far_top, far_bottom, z4_bottom, two_b, out_rows = lax.optimization_barrier(
        (far_top, far_bottom, z4_bottom, two_b, out_rows)
    )
    slabs = [modulated, zp, zm, two_a, zp2, zm2, before, after, two_b, z4_top, z4_bottom]
    pieces = [in_rows, left, right, far_top, far_bottom]
    pieces = pieces + near + [core_swap(far_top), core_swap(far_bottom)]

    out_pieces = [out_rows, x_shift(out_rows, 1), x_shift(out_rows, -1), x_shift(out_rows, 2)]
    keep, send = attend(where_am_i, block_mask, norm_gain, slabs, pieces)

    got = core_swap(send)
    own, other, total = output(
        where_am_i, step_index, step_sizes, keep, got, table, out_pieces
    )
    one = x_later(total, 1)
    three = x_later(total, 3)
    two = x_later(one, 1)
    rest = core_swap(other)
    sums = earlier_sum(where_am_i, step_index, step_sizes, one, two, three, own)
    before = core_swap(sums)
    velocity, advanced = advance(
        where_am_i, step_index, step_sizes, one, two, three, own, other, before, rest, anchor
    )
    return (velocity[None], advanced[None])


def solution(mesh):
    placed = (
        P("step", "frame", None),
        P("frame", None),
        P(),
        P(),
        P(),
        P(("step", "frame"), None),
        P(("step", "frame"), None),
        P(),
        P("frame", None),
    )
    return jax.shard_map(
        on_device,
        mesh=mesh,
        in_specs=placed,
        out_specs=(P("step", "frame", None), P("step", "frame", None)),
        check_vma=False,
    )
```

profile of v0, /device:TPU:3, one launch (start us, length us, event | category | flops | bytes accessed | tf_op | source)
XLA Modules:
  0.0 185.1 jit_solution(16849211619721894301)
XLA Ops:
  0.6 0.7 reshape.29
  1.4 0.8 pad_maximum_fusion.1
  2.2 0.7 pad_add_fusion.where_ref
  2.9 2.9 %modulate.1.refs_0_ = bf16[256,1536]{1,0:T(8,128)(2,1)} custom-call(s32[4]{0:T(128)} %pad_add_fusion.where_ref, s32[8]{0:T(128)} %index_ref.7, bf16[256,1536]{1,0:T(8,128)(2,1)} %bitcast.28, f32[3,50,1536]{2,1,0:T(8,128)} %bitcast.21), custom_call_target="tpu_custom_call" | custom-call | tf_op jit(solution)/shard_map/modulate/pallas_call | solution.py:63
  5.7 1.7 collective-permute-start
  7.5 4.0 %collective-permute-start.1 = (bf16[256,1536]{1,0:T(8,128)(2,1)}, bf16[256,1536]{1,0:T(8,128)(2,1)S(1)}, u32[]{:S(2)}, u32[]{:S(2)}) collective-permute-start(bf16[256,1536]{1,0:T(8,128)(2,1)} %modulate.1.refs_0_), channel_id=1, source_target_pairs={{0,28},{1,29},{2,30},{3,31},{4,0},{5,1},{6,2},{7,3},{8,4},{9,5},{1... | collective-permute-start | bytes 2359304 | tf_op jit(solution)/shard_map/ppermute | solution.py:27
  11.5 2.9 %collective-permute-start.2 = (bf16[256,1536]{1,0:T(8,128)(2,1)}, bf16[256,1536]{1,0:T(8,128)(2,1)S(1)}, u32[]{:S(2)}, u32[]{:S(2)}) collective-permute-start(bf16[256,1536]{1,0:T(8,128)(2,1)} %modulate.1.refs_0_), channel_id=1, source_target_pairs={{0,2},{1,3},{2,0},{3,1},{4,6},{5,7},{6,4},{7,5},{8,10},{9,11},{10,... | collective-permute-start | bytes 2359304 | tf_op jit(solution)/shard_map/ppermute | solution.py:22
  14.4 0.7 broadcast_in_dim.16
  15.1 5.2 %all-to-all-start = ((bf16[8,8,2304]{2,1,0:T(8,128)(2,1)}), bf16[8,8,2304]{2,1,0:T(8,128)(2,1)S(1)}, u32[]{:S(2)}, u32[]{:S(2)}) async-start(bf16[8,8,2304]{2,1,0:T(8,128)(2,1)} %broadcast_in_dim.16), calls=%async_computation | async-start | bytes 589824 | tf_op jit(solution)/shard_map/all_to_all | solution.py:378
  20.3 13.8 %all-to-all-done = bf16[8,8,2304]{2,1,0:T(8,128)(2,1)S(1)} async-done(((bf16[8,8,2304]{2,1,0:T(8,128)(2,1)}), bf16[8,8,2304]{2,1,0:T(8,128)(2,1)S(1)}, u32[]{:S(2)}, u32[]{:S(2)}) %all-to-all-start) | async-done | bytes 294944 | tf_op jit(solution)/shard_map/all_to_all | solution.py:378
  34.1 2.8 %collective-permute-start.3 = (bf16[64,2304]{1,0:T(8,128)(2,1)S(1)}, bf16[64,2304]{1,0:T(8,128)(2,1)S(1)}, u32[]{:S(2)}, u32[]{:S(2)}) collective-permute-start(bf16[64,2304]{1,0:T(8,128)(2,1)S(1)} %bitcast.23), channel_id=1, source_target_pairs={{0,3},{1,0},{2,1},{3,2},{4,7},{5,4},{6,5},{7,6},{8,11},{9,8},{10,9... | collective-permute-start | bytes 884744 | tf_op jit(solution)/shard_map/ppermute | solution.py:22
  36.9 0.3 collective-permute-start.4
  37.3 0.7 collective-permute-start.5
  38.0 2.6 %collective-permute-start.6 = (bf16[256,1536]{1,0:T(8,128)(2,1)S(1)}, bf16[256,1536]{1,0:T(8,128)(2,1)S(1)}, u32[]{:S(2)}, u32[]{:S(2)}) collective-permute-start(bf16[256,1536]{1,0:T(8,128)(2,1)S(1)} %collective-permute-done.refs_1_), channel_id=1, source_target_pairs={{0,4},{1,5},{2,6},{3,7},{4,8},{5,9},{6,10},{7,11},{8,12},{9,13},{1... | collective-permute-start | bytes 2359304 | tf_op jit(solution)/shard_map/ppermute | solution.py:27
  40.8 2.5 %collective-permute-done.3 = bf16[64,2304]{1,0:T(8,128)(2,1)S(1)} collective-permute-done((bf16[64,2304]{1,0:T(8,128)(2,1)S(1)}, bf16[64,2304]{1,0:T(8,128)(2,1)S(1)}, u32[]{:S(2)}, u32[]{:S(2)}) %collective-permute-start.3) | collective-permute-done | bytes 294944 | tf_op jit(solution)/shard_map/ppermute | solution.py:22
  43.3 0.9 collective-permute-done.4
  44.2 9.1 %collective-permute-done.5 = bf16[64,2304]{1,0:T(8,128)(2,1)S(1)} collective-permute-done((bf16[64,2304]{1,0:T(8,128)(2,1)S(1)}, bf16[64,2304]{1,0:T(8,128)(2,1)S(1)}, u32[]{:S(2)}, u32[]{:S(2)}) %collective-permute-start.5) | collective-permute-done | bytes 294944 | tf_op jit(solution)/shard_map/ppermute | solution.py:22
  53.3 1.4 collective-permute-done.6.refs_4_
  54.7 0.9 copy-done.14
  55.6 1.0 copy-done.16
  56.6 1.2 reshape.35.refs_11_
  57.8 1.2 collective-permute-start.8
  59.0 0.3 collective-permute-start.9
  59.2 1.3 broadcast_select_fusion.1
  60.5 1.6 collective-permute-start.10
  62.1 1.1 collective-permute-start.11
  63.2 2.0 %collective-permute-start.12 = (bf16[128,1536]{1,0:T(8,128)(2,1)S(1)}, bf16[128,1536]{1,0:T(8,128)(2,1)}, u32[]{:S(2)}, u32[]{:S(2)}) collective-permute-start(bf16[128,1536]{1,0:T(8,128)(2,1)S(1)} %slice.20), channel_id=1, source_target_pairs={{0,8},{1,9},{2,10},{3,11},{4,12},{5,13},{6,14},{7,15},{8,16},{9,17... | collective-permute-start | bytes 1179656 | tf_op jit(solution)/shard_map/ppermute | solution.py:27
  65.3 0.3 slice.19
  65.6 0.2 reshape.36
  65.8 9.8 %collective-permute-done.10.refs_6_ = bf16[256,1536]{1,0:T(8,128)(2,1)} collective-permute-done((bf16[256,1536]{1,0:T(8,128)(2,1)}, bf16[256,1536]{1,0:T(8,128)(2,1)}, u32[]{:S(2)}, u32[]{:S(2)}) %collective-permute-start.10) | collective-permute-done | bytes 786464 | tf_op jit(solution)/shard_map/ppermute | solution.py:22
  75.7 6.5 %collective-permute-done.12.refs_9_ = bf16[128,1536]{1,0:T(8,128)(2,1)} collective-permute-done((bf16[128,1536]{1,0:T(8,128)(2,1)S(1)}, bf16[128,1536]{1,0:T(8,128)(2,1)}, u32[]{:S(2)}, u32[]{:S(2)}) %collective-permute-start.12) | collective-permute-done | bytes 393248 | tf_op jit(solution)/shard_map/ppermute | solution.py:27
  82.2 1.0 slice.21
  83.3 1.5 collective-permute-start.13
  84.8 2.6 %collective-permute-start.15 = (bf16[128,1536]{1,0:T(8,128)(2,1)S(1)}, bf16[128,1536]{1,0:T(8,128)(2,1)}, u32[]{:S(2)}, u32[]{:S(2)}) collective-permute-start(bf16[128,1536]{1,0:T(8,128)(2,1)S(1)} %slice.23), channel_id=1, source_target_pairs={{0,24},{1,25},{2,26},{3,27},{4,28},{5,29},{6,30},{7,31},{8,0},{9,1... | collective-permute-start | bytes 1179656 | tf_op jit(solution)/shard_map/ppermute | solution.py:27
  87.5 2.6 %collective-permute-start.16 = (bf16[256,1536]{1,0:T(8,128)(2,1)S(1)}, bf16[256,1536]{1,0:T(8,128)(2,1)S(1)}, u32[]{:S(2)}, u32[]{:S(2)}) collective-permute-start(bf16[256,1536]{1,0:T(8,128)(2,1)S(1)} %broadcast_select_fusion), channel_id=1, source_target_pairs={{0,2},{1,3},{2,0},{3,1},{4,6},{5,7},{6,4},{7,5},{8,10},{9,11},{10,... | collective-permute-start | bytes 2359304 | tf_op jit(solution)/shard_map/ppermute | solution.py:22
  90.1 2.7 %collective-permute-start.17 = (bf16[96,1536]{1,0:T(8,128)(2,1)S(1)}, bf16[96,1536]{1,0:T(8,128)(2,1)S(1)}, u32[]{:S(2)}, u32[]{:S(2)}) collective-permute-start(bf16[96,1536]{1,0:T(8,128)(2,1)S(1)} %reshape.36), channel_id=1, source_target_pairs={{0,32},{32,0},{64,96},{96,64},{128,160},{160,128},{192,224},{224,1... | collective-permute-start | bytes 884744 | tf_op jit(solution)/shard_map/ppermute | solution.py:41
  92.8 1.0 slice.22
  94.0 0.3 collective-permute-start.14
  94.3 5.9 %collective-permute-done.15.refs_10_ = bf16[128,1536]{1,0:T(8,128)(2,1)} collective-permute-done((bf16[128,1536]{1,0:T(8,128)(2,1)S(1)}, bf16[128,1536]{1,0:T(8,128)(2,1)}, u32[]{:S(2)}, u32[]{:S(2)}) %collective-permute-start.15) | collective-permute-done | bytes 393248 | tf_op jit(solution)/shard_map/ppermute | solution.py:27
  100.2 1.6 collective-permute-start.19
  102.0 3.4 %collective-permute-done.14.refs_15_ = bf16[96,2304]{1,0:T(8,128)(2,1)S(1)} collective-permute-done((bf16[96,2304]{1,0:T(8,128)(2,1)S(1)}, bf16[96,2304]{1,0:T(8,128)(2,1)S(1)}, u32[]{:S(2)}, u32[]{:S(2)}) %collective-permute-start.14) | collective-permute-done | bytes 442400 | tf_op jit(solution)/shard_map/ppermute | solution.py:32
  105.4 3.7 %collective-permute-start.21 = (bf16[96,2304]{1,0:T(8,128)(2,1)S(1)}, bf16[96,2304]{1,0:T(8,128)(2,1)S(1)}, u32[]{:S(2)}, u32[]{:S(2)}) collective-permute-start(bf16[96,2304]{1,0:T(8,128)(2,1)S(1)} %collective-permute-done.13.refs_14_), channel_id=1, source_target_pairs={{0,32},{32,0},{64,96},{96,64},{128,160},{160,128},{192,224},{224,1... | collective-permute-start | bytes 1327112 | tf_op jit(solution)/shard_map/ppermute | solution.py:41
  109.1 1.0 collective-permute-start.24
  110.1 0.6 collective-permute-start.25
  110.6 2.0 %collective-permute-start.26 = (bf16[2,96,1536]{2,1,0:T(8,128)(2,1)S(1)}, bf16[2,96,1536]{2,1,0:T(8,128)(2,1)S(1)}, u32[]{:S(2)}, u32[]{:S(2)}) collective-permute-start(bf16[2,96,1536]{2,1,0:T(8,128)(2,1)S(1)} %pad_maximum_fusion.refs_0_), channel_id=1, source_target_pairs={{0,128},{32,160},{64,192},{96,224},{128,0},{160,32},{192,64},{224,... | collective-permute-start | bytes 1769480 | tf_op jit(solution)/shard_map/ppermute | solution.py:32
  112.7 0.7 copy-done.25
  113.5 0.8 copy-done.26
  114.2 27.8 %attend.1 = (bf16[128,768]{1,0:T(8,128)(2,1)}, bf16[128,768]{1,0:T(8,128)(2,1)}) custom-call(s32[4]{0:T(128)} %pad_add_fusion.where_ref, s32[2,64]{1,0:T(2,128)} %mask_ref.1, f32[2,768]{1,0:T(2,128)} %gain_ref.1, bf16[256,1536]{1,0:T(8,128)(2,1)} %modulate.1.refs_0_, bf16[256,1536]{1,0:T(8,128)(2,1)} %copy-done, bf16[256,1536]{1,0:T(8,128)(2,1)} %copy-done.1, ...), custom_call_target="tpu_custom_call" | custom-call | flops 16000000000 | bytes 16000000 | tf_op jit(solution)/shard_map/attend/pallas_call | solution.py:191
  142.0 1.4 collective-permute-start.23
  143.4 1.2 collective-permute-done.23.got_ref
  144.7 0.7 copy-done.13
  145.4 4.5 %output.1 = (bf16[128,1536]{1,0:T(8,128)(2,1)}, bf16[128,1536]{1,0:T(8,128)(2,1)}, bf16[128,1536]{1,0:T(8,128)(2,1)}) custom-call(s32[4]{0:T(128)} %pad_add_fusion.where_ref, s32[8]{0:T(128)} %index_ref.7, f32[50]{0:T(128)} %size_ref.5, bf16[128,768]{1,0:T(8,128)(2,1)} %get-tuple-element.56.keep_ref, bf16[128,768]{1,0:T(8,128)(2,1)} %copy-done.13, ...), custom_call_target="tpu_custom_call" | custom-call | tf_op jit(solution)/shard_map/output/pallas_call | solution.py:259
  149.8 2.5 %collective-permute-start.27 = (bf16[128,1536]{1,0:T(8,128)(2,1)}, bf16[128,1536]{1,0:T(8,128)(2,1)S(1)}, u32[]{:S(2)}, u32[]{:S(2)}) collective-permute-start(bf16[128,1536]{1,0:T(8,128)(2,1)} %get-tuple-element.59), channel_id=1, source_target_pairs={{0,64},{32,96},{64,128},{96,160},{128,192},{160,224},{1,65},{33,97... | collective-permute-start | bytes 1179656 | tf_op jit(solution)/shard_map/ppermute | solution.py:37
  152.4 0.7 collective-permute-start.29
  153.1 9.2 %collective-permute-done.27.one_ref = bf16[128,1536]{1,0:T(8,128)(2,1)S(1)} collective-permute-done((bf16[128,1536]{1,0:T(8,128)(2,1)}, bf16[128,1536]{1,0:T(8,128)(2,1)S(1)}, u32[]{:S(2)}, u32[]{:S(2)}) %collective-permute-start.27) | collective-permute-done | bytes 393248 | tf_op jit(solution)/shard_map/ppermute | solution.py:37
  162.3 2.5 %collective-permute-start.28 = (bf16[128,1536]{1,0:T(8,128)(2,1)S(1)}, bf16[128,1536]{1,0:T(8,128)(2,1)S(1)}, u32[]{:S(2)}, u32[]{:S(2)}) collective-permute-start(bf16[128,1536]{1,0:T(8,128)(2,1)S(1)} %collective-permute-done.27.one_ref), channel_id=1, source_target_pairs={{0,64},{32,96},{64,128},{96,160},{128,192},{160,224},{1,65},{33,97... | collective-permute-start | bytes 1179656 | tf_op jit(solution)/shard_map/ppermute | solution.py:37
  164.8 1.6 collective-permute-start.31
  166.4 7.2 %collective-permute-done.28.two_ref = bf16[128,1536]{1,0:T(8,128)(2,1)S(1)} collective-permute-done((bf16[128,1536]{1,0:T(8,128)(2,1)S(1)}, bf16[128,1536]{1,0:T(8,128)(2,1)S(1)}, u32[]{:S(2)}, u32[]{:S(2)}) %collective-permute-start.28) | collective-permute-done | bytes 393248 | tf_op jit(solution)/shard_map/ppermute | solution.py:37
  173.6 0.8 copy-done.6
  174.3 2.3 %earlier_sum.1 = bf16[128,1536]{1,0:T(8,128)(2,1)} custom-call(s32[4]{0:T(128)} %pad_add_fusion.where_ref, s32[8]{0:T(128)} %index_ref.7, f32[50]{0:T(128)} %size_ref.5, bf16[128,1536]{1,0:T(8,128)(2,1)} %copy-done.4, bf16[128,1536]{1,0:T(8,128)(2,1)} %copy-done.6, bf16[128,1536]{1,0:T(8,128)(2,1)} %copy-done.5, bf16[128,1536]{1,0:T(8,128)(2,1)} %get-tuple-element.60.own_ref), custom_call_target="tpu_custom_call" | custom-call | tf_op jit(solution)/shard_map/earlier_sum/pallas_call | solution.py:285
  176.6 2.1 %collective-permute-start.30 = (bf16[128,1536]{1,0:T(8,128)(2,1)}, bf16[128,1536]{1,0:T(8,128)(2,1)S(1)}, u32[]{:S(2)}, u32[]{:S(2)}) collective-permute-start(bf16[128,1536]{1,0:T(8,128)(2,1)} %earlier_sum.1), channel_id=1, source_target_pairs={{0,32},{32,0},{64,96},{96,64},{128,160},{160,128},{192,224},{224,1... | collective-permute-start | bytes 1179656 | tf_op jit(solution)/shard_map/ppermute | solution.py:41
  178.8 1.6 collective-permute-done.30.before_ref
  180.3 0.7 copy-done.12
  181.1 4.1 %advance.1 = (bf16[256,1536]{1,0:T(8,128)(2,1)}, f32[256,1536]{1,0:T(8,128)}) custom-call(s32[4]{0:T(128)} %pad_add_fusion.where_ref, s32[8]{0:T(128)} %index_ref.7, f32[50]{0:T(128)} %size_ref.5, bf16[128,1536]{1,0:T(8,128)(2,1)} %copy-done.4, bf16[128,1536]{1,0:T(8,128)(2,1)} %copy-done.6, bf16[128,1536]{1,0:T(8,128)(2,1)} %copy-done.5, ...), custom_call_target="tpu_custom_call" | custom-call | tf_op jit(solution)/shard_map/advance/pallas_call | solution.py:330
  (80 shorter events, 1.0 us)
Async XLA Ops:
  5.7 28.3 %collective-permute-start = (bf16[256,1536]{1,0:T(8,128)(2,1)}, bf16[256,1536]{1,0:T(8,128)(2,1)S(1)}, u32[]{:S(2)}, u32[]{:S(2)}) collective-permute-start(bf16[256,1536]{1,0:T(8,128)(2,1)} %modulate.1.refs_0_), channel_id=1, source_target_pairs={{0,4},{1,5},{2,6},{3,7},{4,8},{5,9},{6,10},{7,11},{8,12},{9,13},{1... | collective-permute-start | bytes 2359304 | tf_op jit(solution)/shard_map/ppermute | solution.py:27
  7.5 26.6 %collective-permute-start.1 = (bf16[256,1536]{1,0:T(8,128)(2,1)}, bf16[256,1536]{1,0:T(8,128)(2,1)S(1)}, u32[]{:S(2)}, u32[]{:S(2)}) collective-permute-start(bf16[256,1536]{1,0:T(8,128)(2,1)} %modulate.1.refs_0_), channel_id=1, source_target_pairs={{0,28},{1,29},{2,30},{3,31},{4,0},{5,1},{6,2},{7,3},{8,4},{9,5},{1... | collective-permute-start | bytes 2359304 | tf_op jit(solution)/shard_map/ppermute | solution.py:27
  11.5 22.6 %collective-permute-start.2 = (bf16[256,1536]{1,0:T(8,128)(2,1)}, bf16[256,1536]{1,0:T(8,128)(2,1)S(1)}, u32[]{:S(2)}, u32[]{:S(2)}) collective-permute-start(bf16[256,1536]{1,0:T(8,128)(2,1)} %modulate.1.refs_0_), channel_id=1, source_target_pairs={{0,2},{1,3},{2,0},{3,1},{4,6},{5,7},{6,4},{7,5},{8,10},{9,11},{10,... | collective-permute-start | bytes 2359304 | tf_op jit(solution)/shard_map/ppermute | solution.py:22
  15.1 19.0 %all-to-all-start = ((bf16[8,8,2304]{2,1,0:T(8,128)(2,1)}), bf16[8,8,2304]{2,1,0:T(8,128)(2,1)S(1)}, u32[]{:S(2)}, u32[]{:S(2)}) async-start(bf16[8,8,2304]{2,1,0:T(8,128)(2,1)} %broadcast_in_dim.16), calls=%async_computation | async-start | bytes 589824 | tf_op jit(solution)/shard_map/all_to_all | solution.py:378
  34.1 53.3 %copy-start = (bf16[256,1536]{1,0:T(8,128)(2,1)}, bf16[256,1536]{1,0:T(8,128)(2,1)S(1)}, u32[]{:S(2)}) copy-start(bf16[256,1536]{1,0:T(8,128)(2,1)S(1)} %collective-permute-done.refs_1_) | copy-start | bytes 2359300
  34.1 53.3 %copy-start.1 = (bf16[256,1536]{1,0:T(8,128)(2,1)}, bf16[256,1536]{1,0:T(8,128)(2,1)S(1)}, u32[]{:S(2)}) copy-start(bf16[256,1536]{1,0:T(8,128)(2,1)S(1)} %collective-permute-done.1.refs_2_) | copy-start | bytes 2359300
  34.1 6.4 %copy-start.21 = (bf16[256,1536]{1,0:T(8,128)(2,1)}, bf16[256,1536]{1,0:T(8,128)(2,1)S(1)}, u32[]{:S(2)}) copy-start(bf16[256,1536]{1,0:T(8,128)(2,1)S(1)} %collective-permute-done.2.refs_3_) | copy-start | bytes 2359300
  34.1 9.1 %collective-permute-start.3 = (bf16[64,2304]{1,0:T(8,128)(2,1)S(1)}, bf16[64,2304]{1,0:T(8,128)(2,1)S(1)}, u32[]{:S(2)}, u32[]{:S(2)}) collective-permute-start(bf16[64,2304]{1,0:T(8,128)(2,1)S(1)} %bitcast.23), channel_id=1, source_target_pairs={{0,3},{1,0},{2,1},{3,2},{4,7},{5,4},{6,5},{7,6},{8,11},{9,8},{10,9... | collective-permute-start | bytes 884744 | tf_op jit(solution)/shard_map/ppermute | solution.py:22
  36.9 7.2 %collective-permute-start.4 = (bf16[64,2304]{1,0:T(8,128)(2,1)S(1)}, bf16[64,2304]{1,0:T(8,128)(2,1)S(1)}, u32[]{:S(2)}, u32[]{:S(2)}) collective-permute-start(bf16[64,2304]{1,0:T(8,128)(2,1)S(1)} %bitcast.24), channel_id=1, source_target_pairs={{0,2},{1,3},{2,0},{3,1},{4,6},{5,7},{6,4},{7,5},{8,10},{9,11},{10,... | collective-permute-start | bytes 884744 | tf_op jit(solution)/shard_map/ppermute | solution.py:22
  37.3 15.9 %collective-permute-start.5 = (bf16[64,2304]{1,0:T(8,128)(2,1)S(1)}, bf16[64,2304]{1,0:T(8,128)(2,1)S(1)}, u32[]{:S(2)}, u32[]{:S(2)}) collective-permute-start(bf16[64,2304]{1,0:T(8,128)(2,1)S(1)} %bitcast.25), channel_id=1, source_target_pairs={{0,1},{1,2},{2,3},{3,0},{4,5},{5,6},{6,7},{7,4},{8,9},{9,10},{10,1... | collective-permute-start | bytes 884744 | tf_op jit(solution)/shard_map/ppermute | solution.py:22
  38.0 16.7 %collective-permute-start.6 = (bf16[256,1536]{1,0:T(8,128)(2,1)S(1)}, bf16[256,1536]{1,0:T(8,128)(2,1)S(1)}, u32[]{:S(2)}, u32[]{:S(2)}) collective-permute-start(bf16[256,1536]{1,0:T(8,128)(2,1)S(1)} %collective-permute-done.refs_1_), channel_id=1, source_target_pairs={{0,4},{1,5},{2,6},{3,7},{4,8},{5,9},{6,10},{7,11},{8,12},{9,13},{1... | collective-permute-start | bytes 2359304 | tf_op jit(solution)/shard_map/ppermute | solution.py:27
  40.5 14.1 %collective-permute-start.7 = (bf16[256,1536]{1,0:T(8,128)(2,1)S(1)}, bf16[256,1536]{1,0:T(8,128)(2,1)S(1)}, u32[]{:S(2)}, u32[]{:S(2)}) collective-permute-start(bf16[256,1536]{1,0:T(8,128)(2,1)S(1)} %collective-permute-done.1.refs_2_), channel_id=1, source_target_pairs={{0,28},{1,29},{2,30},{3,31},{4,0},{5,1},{6,2},{7,3},{8,4},{9,5},{1... | collective-permute-start | bytes 2359304 | tf_op jit(solution)/shard_map/ppermute | solution.py:27
  53.3 6.0 %copy-start.2 = (bf16[256,1536]{1,0:T(8,128)(2,1)S(1)}, bf16[256,1536]{1,0:T(8,128)(2,1)}, u32[]{:S(2)}) copy-start(bf16[256,1536]{1,0:T(8,128)(2,1)} %modulate.1.refs_0_) | copy-start | bytes 2359300
  54.7 0.9 copy-start.14
  55.6 1.0 copy-start.16
  57.8 5.4 %copy-start.15 = (bf16[256,1536]{1,0:T(8,128)(2,1)S(1)}, bf16[256,1536]{1,0:T(8,128)(2,1)}, u32[]{:S(2)}) copy-start(bf16[256,1536]{1,0:T(8,128)(2,1)} %copy-done.14) | copy-start | bytes 2359300
  57.8 24.4 %collective-permute-start.8 = (bf16[192,2304]{1,0:T(8,128)(2,1)}, bf16[192,2304]{1,0:T(8,128)(2,1)}, u32[]{:S(2)}, u32[]{:S(2)}) collective-permute-start(bf16[192,2304]{1,0:T(8,128)(2,1)} %reshape.35.refs_11_), channel_id=1, source_target_pairs={{0,64},{32,96},{64,128},{96,160},{128,192},{160,224},{192,0},{224,... | collective-permute-start | bytes 2654216 | tf_op jit(solution)/shard_map/ppermute | solution.py:32
  59.0 23.2 %collective-permute-start.9 = (bf16[192,2304]{1,0:T(8,128)(2,1)}, bf16[192,2304]{1,0:T(8,128)(2,1)}, u32[]{:S(2)}, u32[]{:S(2)}) collective-permute-start(bf16[192,2304]{1,0:T(8,128)(2,1)} %reshape.35.refs_11_), channel_id=1, source_target_pairs={{0,192},{32,224},{64,0},{96,32},{128,64},{160,96},{192,128},{224,1... | collective-permute-start | bytes 2654216 | tf_op jit(solution)/shard_map/ppermute | solution.py:32
  60.5 15.1 %collective-permute-start.10 = (bf16[256,1536]{1,0:T(8,128)(2,1)}, bf16[256,1536]{1,0:T(8,128)(2,1)}, u32[]{:S(2)}, u32[]{:S(2)}) collective-permute-start(bf16[256,1536]{1,0:T(8,128)(2,1)} %get-tuple-element.65), channel_id=1, source_target_pairs={{0,1},{1,2},{2,3},{3,0},{4,5},{5,6},{6,7},{7,4},{8,9},{9,10},{10,1... | collective-permute-start | bytes 2359304 | tf_op jit(solution)/shard_map/ppermute | solution.py:22
  62.1 13.6 %collective-permute-start.11 = (bf16[256,1536]{1,0:T(8,128)(2,1)}, bf16[256,1536]{1,0:T(8,128)(2,1)}, u32[]{:S(2)}, u32[]{:S(2)}) collective-permute-start(bf16[256,1536]{1,0:T(8,128)(2,1)} %get-tuple-element.64), channel_id=1, source_target_pairs={{0,3},{1,0},{2,1},{3,2},{4,7},{5,4},{6,5},{7,6},{8,11},{9,8},{10,9... | collective-permute-start | bytes 2359304 | tf_op jit(solution)/shard_map/ppermute | solution.py:22
  63.2 19.0 %collective-permute-start.12 = (bf16[128,1536]{1,0:T(8,128)(2,1)S(1)}, bf16[128,1536]{1,0:T(8,128)(2,1)}, u32[]{:S(2)}, u32[]{:S(2)}) collective-permute-start(bf16[128,1536]{1,0:T(8,128)(2,1)S(1)} %slice.20), channel_id=1, source_target_pairs={{0,8},{1,9},{2,10},{3,11},{4,12},{5,13},{6,14},{7,15},{8,16},{9,17... | collective-permute-start | bytes 1179656 | tf_op jit(solution)/shard_map/ppermute | solution.py:27
  65.6 19.2 %copy-start.17 = (bf16[256,1536]{1,0:T(8,128)(2,1)S(1)}, bf16[256,1536]{1,0:T(8,128)(2,1)}, u32[]{:S(2)}) copy-start(bf16[256,1536]{1,0:T(8,128)(2,1)} %copy-done.16) | copy-start | bytes 2359300
  83.3 18.5 %collective-permute-start.13 = (bf16[96,2304]{1,0:T(8,128)(2,1)S(1)}, bf16[96,2304]{1,0:T(8,128)(2,1)S(1)}, u32[]{:S(2)}, u32[]{:S(2)}) collective-permute-start(bf16[96,2304]{1,0:T(8,128)(2,1)S(1)} %slice.21), channel_id=1, source_target_pairs={{0,64},{32,96},{64,128},{96,160},{128,192},{160,224},{192,0},{224,... | collective-permute-start | bytes 1327112 | tf_op jit(solution)/shard_map/ppermute | solution.py:32
  84.8 9.1 %copy-start.7 = (bf16[192,2304]{1,0:T(8,128)(2,1)S(1)}, bf16[192,2304]{1,0:T(8,128)(2,1)}, u32[]{:S(2)}) copy-start(bf16[192,2304]{1,0:T(8,128)(2,1)} %reshape.35.refs_11_) | copy-start | bytes 2654212
  84.8 15.4 %collective-permute-start.15 = (bf16[128,1536]{1,0:T(8,128)(2,1)S(1)}, bf16[128,1536]{1,0:T(8,128)(2,1)}, u32[]{:S(2)}, u32[]{:S(2)}) collective-permute-start(bf16[128,1536]{1,0:T(8,128)(2,1)S(1)} %slice.23), channel_id=1, source_target_pairs={{0,24},{1,25},{2,26},{3,27},{4,28},{5,29},{6,30},{7,31},{8,0},{9,1... | collective-permute-start | bytes 1179656 | tf_op jit(solution)/shard_map/ppermute | solution.py:27
  87.5 17.9 %collective-permute-start.16 = (bf16[256,1536]{1,0:T(8,128)(2,1)S(1)}, bf16[256,1536]{1,0:T(8,128)(2,1)S(1)}, u32[]{:S(2)}, u32[]{:S(2)}) collective-permute-start(bf16[256,1536]{1,0:T(8,128)(2,1)S(1)} %broadcast_select_fusion), channel_id=1, source_target_pairs={{0,2},{1,3},{2,0},{3,1},{4,6},{5,7},{6,4},{7,5},{8,10},{9,11},{10,... | collective-permute-start | bytes 2359304 | tf_op jit(solution)/shard_map/ppermute | solution.py:22
  90.1 3.9 %collective-permute-start.17 = (bf16[96,1536]{1,0:T(8,128)(2,1)S(1)}, bf16[96,1536]{1,0:T(8,128)(2,1)S(1)}, u32[]{:S(2)}, u32[]{:S(2)}) collective-permute-start(bf16[96,1536]{1,0:T(8,128)(2,1)S(1)} %reshape.36), channel_id=1, source_target_pairs={{0,32},{32,0},{64,96},{96,64},{128,160},{160,128},{192,224},{224,1... | collective-permute-start | bytes 884744 | tf_op jit(solution)/shard_map/ppermute | solution.py:41
  93.9 15.2 %collective-permute-start.18 = (bf16[192,2304]{1,0:T(8,128)(2,1)S(1)}, bf16[192,2304]{1,0:T(8,128)(2,1)S(1)}, u32[]{:S(2)}, u32[]{:S(2)}) collective-permute-start(bf16[192,2304]{1,0:T(8,128)(2,1)S(1)} %copy-done.7), channel_id=1, source_target_pairs={{0,32},{32,0},{64,96},{96,64},{128,160},{160,128},{192,224},{224,1... | collective-permute-start | bytes 2654216 | tf_op jit(solution)/shard_map/ppermute | solution.py:41
  94.0 11.4 %collective-permute-start.14 = (bf16[96,2304]{1,0:T(8,128)(2,1)S(1)}, bf16[96,2304]{1,0:T(8,128)(2,1)S(1)}, u32[]{:S(2)}, u32[]{:S(2)}) collective-permute-start(bf16[96,2304]{1,0:T(8,128)(2,1)S(1)} %slice.22), channel_id=1, source_target_pairs={{0,192},{32,224},{64,0},{96,32},{128,64},{160,96},{192,128},{224,1... | collective-permute-start | bytes 1327112 | tf_op jit(solution)/shard_map/ppermute | solution.py:32
  100.2 9.9 %collective-permute-start.19 = (bf16[192,2304]{1,0:T(8,128)(2,1)}, bf16[192,2304]{1,0:T(8,128)(2,1)S(1)}, u32[]{:S(2)}, u32[]{:S(2)}) collective-permute-start(bf16[192,2304]{1,0:T(8,128)(2,1)} %collective-permute-done.8.refs_12_), channel_id=1, source_target_pairs={{0,32},{32,0},{64,96},{96,64},{128,160},{160,128},{192,224},{224,1... | collective-permute-start | bytes 2654216 | tf_op jit(solution)/shard_map/ppermute | solution.py:41
  101.8 10.9 %copy-start.23 = (bf16[96,2304]{1,0:T(8,128)(2,1)}, bf16[96,2304]{1,0:T(8,128)(2,1)S(1)}, u32[]{:S(2)}) copy-start(bf16[96,2304]{1,0:T(8,128)(2,1)S(1)} %collective-permute-done.13.refs_14_) | copy-start | bytes 1327108
  101.8 8.8 %collective-permute-start.20 = (bf16[192,2304]{1,0:T(8,128)(2,1)}, bf16[192,2304]{1,0:T(8,128)(2,1)S(1)}, u32[]{:S(2)}, u32[]{:S(2)}) collective-permute-start(bf16[192,2304]{1,0:T(8,128)(2,1)} %collective-permute-done.9.refs_13_), channel_id=1, source_target_pairs={{0,32},{32,0},{64,96},{96,64},{128,160},{160,128},{192,224},{224,1... | collective-permute-start | bytes 2654216 | tf_op jit(solution)/shard_map/ppermute | solution.py:41
  101.9 40.1 %copy-start.3 = (bf16[2,96,1536]{2,1,0:T(8,128)(2,1)}, bf16[2,96,1536]{2,1,0:T(8,128)(2,1)S(1)}, u32[]{:S(2)}) copy-start(bf16[2,96,1536]{2,1,0:T(8,128)(2,1)S(1)} %pad_maximum_fusion.refs_0_) | copy-start | bytes 1769476
  105.4 7.3 %copy-start.24 = (bf16[96,2304]{1,0:T(8,128)(2,1)}, bf16[96,2304]{1,0:T(8,128)(2,1)S(1)}, u32[]{:S(2)}) copy-start(bf16[96,2304]{1,0:T(8,128)(2,1)S(1)} %collective-permute-done.14.refs_15_) | copy-start | bytes 1327108
  105.4 7.3 %copy-start.22 = (bf16[256,1536]{1,0:T(8,128)(2,1)}, bf16[256,1536]{1,0:T(8,128)(2,1)S(1)}, u32[]{:S(2)}) copy-start(bf16[256,1536]{1,0:T(8,128)(2,1)S(1)} %collective-permute-done.16.refs_8_) | copy-start | bytes 2359300
  105.4 7.3 %collective-permute-start.21 = (bf16[96,2304]{1,0:T(8,128)(2,1)S(1)}, bf16[96,2304]{1,0:T(8,128)(2,1)S(1)}, u32[]{:S(2)}, u32[]{:S(2)}) collective-permute-start(bf16[96,2304]{1,0:T(8,128)(2,1)S(1)} %collective-permute-done.13.refs_14_), channel_id=1, source_target_pairs={{0,32},{32,0},{64,96},{96,64},{128,160},{160,128},{192,224},{224,1... | collective-permute-start | bytes 1327112 | tf_op jit(solution)/shard_map/ppermute | solution.py:41
  109.1 3.6 %collective-permute-start.22 = (bf16[96,2304]{1,0:T(8,128)(2,1)S(1)}, bf16[96,2304]{1,0:T(8,128)(2,1)S(1)}, u32[]{:S(2)}, u32[]{:S(2)}) collective-permute-start(bf16[96,2304]{1,0:T(8,128)(2,1)S(1)} %collective-permute-done.14.refs_15_), channel_id=1, source_target_pairs={{0,32},{32,0},{64,96},{96,64},{128,160},{160,128},{192,224},{224,1... | collective-permute-start | bytes 1327112 | tf_op jit(solution)/shard_map/ppermute | solution.py:41
  109.1 3.6 %copy-start.18 = (bf16[192,2304]{1,0:T(8,128)(2,1)}, bf16[192,2304]{1,0:T(8,128)(2,1)S(1)}, u32[]{:S(2)}) copy-start(bf16[192,2304]{1,0:T(8,128)(2,1)S(1)} %collective-permute-done.18.refs_16_) | copy-start | bytes 2654212
  109.1 34.3 %collective-permute-start.24 = (bf16[2,96,1536]{2,1,0:T(8,128)(2,1)S(1)}, bf16[2,96,1536]{2,1,0:T(8,128)(2,1)S(1)}, u32[]{:S(2)}, u32[]{:S(2)}) collective-permute-start(bf16[2,96,1536]{2,1,0:T(8,128)(2,1)S(1)} %pad_maximum_fusion.refs_0_), channel_id=1, source_target_pairs={{0,64},{32,96},{64,128},{96,160},{128,192},{160,224},{192,0},{224,... | collective-permute-start | bytes 1769480 | tf_op jit(solution)/shard_map/ppermute | solution.py:32
  110.1 2.6 %copy-start.19 = (bf16[192,2304]{1,0:T(8,128)(2,1)}, bf16[192,2304]{1,0:T(8,128)(2,1)S(1)}, u32[]{:S(2)}) copy-start(bf16[192,2304]{1,0:T(8,128)(2,1)S(1)} %collective-permute-done.19.refs_17_) | copy-start | bytes 2654212
  110.1 33.3 %collective-permute-start.25 = (bf16[2,96,1536]{2,1,0:T(8,128)(2,1)S(1)}, bf16[2,96,1536]{2,1,0:T(8,128)(2,1)S(1)}, u32[]{:S(2)}, u32[]{:S(2)}) collective-permute-start(bf16[2,96,1536]{2,1,0:T(8,128)(2,1)S(1)} %pad_maximum_fusion.refs_0_), channel_id=1, source_target_pairs={{0,192},{32,224},{64,0},{96,32},{128,64},{160,96},{192,128},{224,1... | collective-permute-start | bytes 1769480 | tf_op jit(solution)/shard_map/ppermute | solution.py:32
  110.6 2.1 %copy-start.20 = (bf16[192,2304]{1,0:T(8,128)(2,1)}, bf16[192,2304]{1,0:T(8,128)(2,1)S(1)}, u32[]{:S(2)}) copy-start(bf16[192,2304]{1,0:T(8,128)(2,1)S(1)} %collective-permute-done.20.refs_18_) | copy-start | bytes 2654212
  110.6 32.8 %collective-permute-start.26 = (bf16[2,96,1536]{2,1,0:T(8,128)(2,1)S(1)}, bf16[2,96,1536]{2,1,0:T(8,128)(2,1)S(1)}, u32[]{:S(2)}, u32[]{:S(2)}) collective-permute-start(bf16[2,96,1536]{2,1,0:T(8,128)(2,1)S(1)} %pad_maximum_fusion.refs_0_), channel_id=1, source_target_pairs={{0,128},{32,160},{64,192},{96,224},{128,0},{160,32},{192,64},{224,... | collective-permute-start | bytes 1769480 | tf_op jit(solution)/shard_map/ppermute | solution.py:32
  112.7 0.8 copy-start.25
  113.5 0.8 copy-start.26
  142.0 2.6 %collective-permute-start.23 = (bf16[128,768]{1,0:T(8,128)(2,1)}, bf16[128,768]{1,0:T(8,128)(2,1)S(1)}, u32[]{:S(2)}, u32[]{:S(2)}) collective-permute-start(bf16[128,768]{1,0:T(8,128)(2,1)} %get-tuple-element.57), channel_id=1, source_target_pairs={{0,32},{32,0},{64,96},{96,64},{128,160},{160,128},{192,224},{224,1... | collective-permute-start | bytes 589832 | tf_op jit(solution)/shard_map/ppermute | solution.py:41
  143.4 1.3 copy-start.8
  143.4 1.3 copy-start.9
  143.4 1.3 copy-start.10
  144.7 0.7 copy-start.13
  149.8 12.4 %collective-permute-start.27 = (bf16[128,1536]{1,0:T(8,128)(2,1)}, bf16[128,1536]{1,0:T(8,128)(2,1)S(1)}, u32[]{:S(2)}, u32[]{:S(2)}) collective-permute-start(bf16[128,1536]{1,0:T(8,128)(2,1)} %get-tuple-element.59), channel_id=1, source_target_pairs={{0,64},{32,96},{64,128},{96,160},{128,192},{160,224},{1,65},{33,97... | collective-permute-start | bytes 1179656 | tf_op jit(solution)/shard_map/ppermute | solution.py:37
  152.4 14.0 %collective-permute-start.29 = (bf16[128,1536]{1,0:T(8,128)(2,1)}, bf16[128,1536]{1,0:T(8,128)(2,1)S(1)}, u32[]{:S(2)}, u32[]{:S(2)}) collective-permute-start(bf16[128,1536]{1,0:T(8,128)(2,1)} %get-tuple-element.59), channel_id=1, source_target_pairs={{0,192},{32,224},{1,193},{33,225},{2,194},{34,226},{3,195},{35,227... | collective-permute-start | bytes 1179656 | tf_op jit(solution)/shard_map/ppermute | solution.py:37
  162.3 11.3 %copy-start.4 = (bf16[128,1536]{1,0:T(8,128)(2,1)}, bf16[128,1536]{1,0:T(8,128)(2,1)S(1)}, u32[]{:S(2)}) copy-start(bf16[128,1536]{1,0:T(8,128)(2,1)S(1)} %collective-permute-done.27.one_ref) | copy-start | bytes 1179652
  162.3 11.3 %collective-permute-start.28 = (bf16[128,1536]{1,0:T(8,128)(2,1)S(1)}, bf16[128,1536]{1,0:T(8,128)(2,1)S(1)}, u32[]{:S(2)}, u32[]{:S(2)}) collective-permute-start(bf16[128,1536]{1,0:T(8,128)(2,1)S(1)} %collective-permute-done.27.one_ref), channel_id=1, source_target_pairs={{0,64},{32,96},{64,128},{96,160},{128,192},{160,224},{1,65},{33,97... | collective-permute-start | bytes 1179656 | tf_op jit(solution)/shard_map/ppermute | solution.py:37
  164.8 14.0 %collective-permute-start.31 = (bf16[128,1536]{1,0:T(8,128)(2,1)}, bf16[128,1536]{1,0:T(8,128)(2,1)S(1)}, u32[]{:S(2)}, u32[]{:S(2)}) collective-permute-start(bf16[128,1536]{1,0:T(8,128)(2,1)} %get-tuple-element.61.other_ref), channel_id=1, source_target_pairs={{0,32},{32,0},{64,96},{96,64},{128,160},{160,128},{192,224},{224,1... | collective-permute-start | bytes 1179656 | tf_op jit(solution)/shard_map/ppermute | solution.py:41
  166.4 7.2 %copy-start.5 = (bf16[128,1536]{1,0:T(8,128)(2,1)}, bf16[128,1536]{1,0:T(8,128)(2,1)S(1)}, u32[]{:S(2)}) copy-start(bf16[128,1536]{1,0:T(8,128)(2,1)S(1)} %collective-permute-done.29.three_ref) | copy-start | bytes 1179652
  173.6 0.8 copy-start.6
  176.6 3.7 %collective-permute-start.30 = (bf16[128,1536]{1,0:T(8,128)(2,1)}, bf16[128,1536]{1,0:T(8,128)(2,1)S(1)}, u32[]{:S(2)}, u32[]{:S(2)}) collective-permute-start(bf16[128,1536]{1,0:T(8,128)(2,1)} %earlier_sum.1), channel_id=1, source_target_pairs={{0,32},{32,0},{64,96},{96,64},{128,160},{160,128},{192,224},{224,1... | collective-permute-start | bytes 1179656 | tf_op jit(solution)/shard_map/ppermute | solution.py:41
  178.8 1.6 copy-start.11
  180.3 0.7 copy-start.12
where the time goes:
time: 186 us; the launch traced here: 185 us
  waiting for transfers between devices  72.5 us (39%)
  starting transfers between devices  56.1 us (30%)
  Pallas kernels  41.5 us (22%)
  local copies, waits for them, and re-layouts  11.1 us (6%)
  other arithmetic  2.89 us (2%)
    pallas_call x1, Pallas kernels, attend(): pl.pallas_call(attend_kernel, in_specs=[smem, smem, pl.BlockSpec(memory_s...  27.8 us
    ppermute x7, waiting for transfers between devices, y_shift(): return lax.ppermute(block, 'frame', pairs)  22.3 us
    ppermute x3, waiting for transfers between devices, x_later(): return lax.ppermute(block, 'step', pairs)  16.4 us
    ppermute x6, waiting for transfers between devices, z_shift(): return lax.ppermute(block, 'frame', pairs)  13.8 us
    all_to_all x1, waiting for transfers between devices, on_device(): lax.all_to_all(jnp.broadcast_to(packed[None], (NZ,) + packed.shape), 'fra...  13.8 us
    ppermute x9, starting transfers between devices, core_swap(): return lax.ppermute(block, 'step', [(i, i ^ 1) for i in range(2 * NX)])  13.3 us
    ppermute x6, starting transfers between devices, z_shift(): return lax.ppermute(block, 'frame', pairs)  13.1 us
    ppermute x7, starting transfers between devices, y_shift(): return lax.ppermute(block, 'frame', pairs)  12 us
  transfers between devices with their start and end apart: 33, of which 15 were waited for; matrix products, arithmetic and copies ran while one was open for 2% of the time, Pallas kernels for 16%

commit v1 on v0

--- a/solution.py
+++ b/solution.py
@@ -86,9 +86,9 @@
 ):
     slabs = refs[:9]
     z4_top, z4_bottom = refs[9:11]
-    pieces = refs[11:21]
-    keep_ref, send_ref = refs[21:23]
-    m_s, w_s, k_s, v_s, q_s, bias_s, m_sem, w_sem = refs[23:]
+    pieces = refs[11:19]
+    keep_ref, send_ref = refs[19:21]
+    m_s, w_s, k_s, v_s, q_s, bias_s, m_sem, w_sem = refs[21:]
     x, core, frame = where_ref[1], where_ref[2], where_ref[3]
     rows = q_s.shape[0]
     feats = q_s.shape[1]
@@ -104,17 +104,14 @@
     depth = w_s.shape[0] // (2 * NX)
     copies_w = []
     for who in range(2):
-        for i, distance in enumerate((0, -1, 1, 2, 2)):
-            piece = pieces[who * 5 + i]
+        for i, distance in enumerate((0, -1, 1, 2)):
+            piece = pieces[who * 4 + i]
             from_x = lax.rem(x + distance + NX, NX)
             from_core = core if who == 0 else 1 - core
-            start = (2 * from_x + from_core) * depth
-            if i == 4:
-                start = start + depth // 2
-            start = pl.multiple_of(start, 16)
+            start = pl.multiple_of((2 * from_x + from_core) * depth, 16)
             copies_w.append(
                 pltpu.make_async_copy(
-                    piece, w_s.at[pl.ds(start, piece.shape[0])], w_sem.at[who * 5 + i]
+                    piece, w_s.at[pl.ds(start, depth)], w_sem.at[who * 4 + i]
                 )
             )
     copies_m[0].start()
@@ -202,7 +199,7 @@
             pltpu.VMEM((rows, feats), BF16),
             pltpu.VMEM((2, keys), F32),
             pltpu.SemaphoreType.DMA((11,)),
-            pltpu.SemaphoreType.DMA((10,)),
+            pltpu.SemaphoreType.DMA((8,)),
         ],
         compiler_params=pltpu.CompilerParams(vmem_limit_bytes=VMEM_LIMIT),
         cost_estimate=pl.CostEstimate(
@@ -238,11 +235,11 @@
         copy.start()
     for copy in copies:
         copy.wait()
-    weight = w_s[...]
-    own = jnp.dot(keep_ref[...], weight, preferred_element_type=F32)
-    own = (row_s[0] * own).astype(BF16)
-    other = jnp.dot(got_ref[...], weight, preferred_element_type=F32)
-    other = (row_s[1] * other).astype(BF16)
+    both = jnp.concatenate([keep_ref[...], got_ref[...]], axis=0)
+    both = jnp.dot(both, w_s[...], preferred_element_type=F32)
+    half = keep_ref.shape[0]
+    own = (row_s[0] * both[:half]).astype(BF16)
+    other = (row_s[1] * both[half:]).astype(BF16)
     own_ref[...] = own
     other_ref[...] = other
     total_ref[...] = (
@@ -272,71 +269,78 @@
     )(where, step_index, step_sizes, keep, got, table, *pieces)
 
 
-def earlier_kernel(where_ref, index_ref, size_ref, one_ref, two_ref, three_ref, own_ref, out_ref):
-    core = where_ref[2]
-    size = jnp.where(core == 0, size_ref[index_ref[where_ref[0]]], 0.0)
-    total = one_ref[...].astype(F32) + two_ref[...].astype(F32) + three_ref[...].astype(F32)
-    out_ref[...] = (total + size * own_ref[...].astype(F32)).astype(BF16)
-
-
-def earlier_sum(where, step_index, step_sizes, one, two, three, own):
-    vmem = pl.BlockSpec(memory_space=pltpu.VMEM)
-    smem = pl.BlockSpec(memory_space=pltpu.SMEM)
-    return pl.pallas_call(
-        earlier_kernel,
-        in_specs=[smem, smem, smem] + [vmem] * 4,
-        out_specs=vmem,
-        out_shape=jax.ShapeDtypeStruct(own.shape, BF16),
-        name="earlier_sum",
-    )(where, step_index, step_sizes, one, two, three, own)
-
-
-def advance_kernel(
+def base_kernel(
     where_ref,
     index_ref,
     size_ref,
-    one_ref,
-    two_ref,
-    three_ref,
     own_ref,
     other_ref,
-    before_ref,
     rest_ref,
     anchor_ref,
     velocity_ref,
-    advanced_ref,
+    base_ref,
 ):
     step, core = where_ref[0], where_ref[2]
-    half = own_ref.shape[0]
+    near = pl.program_id(0) == core
     size_own = size_ref[index_ref[step]]
-    size_other = jnp.where(core == 1, size_ref[index_ref[step + 1 - 2 * core]], 0.0)
-    near = pl.ds(pl.multiple_of(core * half, half), half)
-    far = pl.ds(pl.multiple_of((1 - core) * half, half), half)
-    own = own_ref[...]
-    velocity_ref[near] = own
-    total = one_ref[...].astype(F32) + two_ref[...].astype(F32) + three_ref[...].astype(F32)
-    total = total + size_other * other_ref[...].astype(F32) + size_own * own.astype(F32)
-    advanced_ref[near] = anchor_ref[near] + total
-    rest = rest_ref[...]
-    velocity_ref[far] = rest
-    advanced_ref[far] = (
-        anchor_ref[far] + before_ref[...].astype(F32) + size_own * rest.astype(F32)
-    )
-
-
-def advance(where, step_index, step_sizes, one, two, three, own, other, before, rest, anchor):
-    vmem = pl.BlockSpec(memory_space=pltpu.VMEM)
+    size_other = jnp.where(
+        jnp.logical_and(near, core == 1), size_ref[index_ref[step + 1 - 2 * core]], 0.0
+    )
+    value = jnp.where(near, own_ref[...].astype(F32), rest_ref[...].astype(F32))
+    velocity_ref[...] = value.astype(BF16)
+    base_ref[...] = (
+        anchor_ref[...] + size_other * other_ref[...].astype(F32) + size_own * value
+    )
+
+
+def base(where, step_index, step_sizes, own, other, rest, anchor):
+    half, width = own.shape
     smem = pl.BlockSpec(memory_space=pltpu.SMEM)
+    part = pl.BlockSpec((half // 2, width), lambda i, j: (j, 0))
+    whole = pl.BlockSpec((half // 2, width), lambda i, j: (2 * i + j, 0))
     return pl.pallas_call(
-        advance_kernel,
-        in_specs=[smem, smem, smem] + [vmem] * 8,
-        out_specs=[vmem] * 2,
+        base_kernel,
+        grid=(2, 2),
+        in_specs=[smem, smem, smem, part, part, part, whole],
+        out_specs=[whole, whole],
         out_shape=[
             jax.ShapeDtypeStruct(anchor.shape, BF16),
             jax.ShapeDtypeStruct(anchor.shape, F32),
         ],
-        name="advance",
-    )(where, step_index, step_sizes, one, two, three, own, other, before, rest, anchor)
+        cost_estimate=pl.CostEstimate(
+            flops=3_000_000, bytes_accessed=6_000_000, transcendentals=0
+        ),
+        name="base",
+    )(where, step_index, step_sizes, own, other, rest, anchor)
+
+
+def add_kernel(where_ref, *refs):
+    value = refs[0][...]
+    for part_ref in refs[1:-1]:
+        value = value + part_ref[...].astype(F32)
+    refs[-1][...] = value
+
+
+def add_half(where, near, value, parts, name):
+    half, width = parts[0].shape
+
+    def place(i, where):
+        core = where[2] if near else 1 - where[2]
+        return (2 * core + i, 0)
+
+    return pl.pallas_call(
+        add_kernel,
+        grid_spec=pltpu.PrefetchScalarGridSpec(
+            num_scalar_prefetch=1,
+            grid=(2,),
+            in_specs=[pl.BlockSpec((half // 2, width), place)]
+            + [pl.BlockSpec((half // 2, width), lambda i, where: (i, 0))] * len(parts),
+            out_specs=pl.BlockSpec((half // 2, width), place),
+        ),
+        out_shape=jax.ShapeDtypeStruct(value.shape, F32),
+        input_output_aliases={1: 0},
+        name=name,
+    )(where, value, *parts)
 
 
 def placed_y(parts, own):
@@ -368,12 +372,11 @@
 
     table = jnp.transpose(modulation, (1, 0, 2))
 
+    size_own = step_sizes[step_index[step]]
+    size_even = jnp.where(core == 0, size_own, 0.0)
+
     out_width = output_weight.shape[1]
     packed = jnp.concatenate([input_weight, output_weight.reshape(2, -1)], axis=0)
-    modulated = modulate(where_am_i, step_index, latent, table)
-    packed, modulated = lax.optimization_barrier((packed, modulated))
-    zp, zm = z_shift(modulated, 1), z_shift(modulated, -1)
-    two_a = y_shift(modulated, 2)
     columns_z = [[NY * i + j for i in range(NZ)] for j in range(NY)]
     column = lax.all_to_all(
         jnp.broadcast_to(packed[None], (NZ,) + packed.shape),
@@ -382,34 +385,36 @@
         0,
         axis_index_groups=columns_z,
     ).reshape(8 * NZ, -1)
-    column, zp, zm, two_a = lax.optimization_barrier((column, zp, zm, two_a))
-
-    zp2, zm2 = z_shift(zp, 1), z_shift(zm, -1)
-    plane = placed_y([column] + [y_shift(column, -d) for d in range(1, NY)], y)
-    plane, zp2, zm2 = lax.optimization_barrier((plane, zp2, zm2))
+    modulated = modulate(where_am_i, step_index, latent, table)
+    two_a = y_shift(modulated, 2)
+    column, modulated, size_even = lax.optimization_barrier((column, modulated, size_even))
+
+    zp, zm = z_shift(modulated, 1), z_shift(modulated, -1)
+    later, two_a = lax.optimization_barrier((column, two_a))
+    plane = placed_y([column, y_shift(column, -1), y_shift(later, 2), y_shift(column, 1)], y)
+    plane, zp, zm = lax.optimization_barrier((plane, zp, zm))
     in_rows = plane[:, :, :6].reshape(192, -1)
     out_rows = plane[:, :, 6:].reshape(96, out_width)
 
-    left, right = x_shift(in_rows, 1), x_shift(in_rows, -1)
-
+    left = x_shift(in_rows, 1)
+    zp2, zm2 = z_shift(zp, 1), z_shift(zm, -1)
     before = y_shift(jnp.where(y == NY - 1, zp, modulated), 1)
     after = y_shift(jnp.where(y == 0, zm, modulated), -1)
+    in_rows, out_rows, left, zp2, zm2, zp, zm, before, after = lax.optimization_barrier(
+        (in_rows, out_rows, left, zp2, zm2, zp, zm, before, after)
+    )
+
+    right, far = x_shift(in_rows, -1), x_shift(left, 1)
     z4_top = z_shift(zp2[: rows // 2], 2)
-    in_rows, out_rows, left, right, before, after, z4_top, zm2, zp, zm = lax.optimization_barrier(
-        (in_rows, out_rows, left, right, before, after, z4_top, zm2, zp, zm)
-    )
-    far_top = x_shift(left[:96], 1)
-    far_bottom = x_shift(right[96:], -1)
     z4_bottom = z_shift(zm2[rows // 2 :], -2)
     two_b = y_shift(jnp.where(y >= 2, zp, zm), 2)
-    near = [core_swap(piece) for piece in (in_rows, left, right)]
+    near = [core_swap(piece) for piece in (in_rows, left)]
     out_rows = jnp.stack([out_rows, core_swap(out_rows)])
-    far_top, far_bottom, z4_bottom, two_b, out_rows = lax.optimization_barrier(
-        (far_top, far_bottom, z4_bottom, two_b, out_rows)
+    right, far, z4_top, z4_bottom, two_b, out_rows = lax.optimization_barrier(
+        (right, far, z4_top, z4_bottom, two_b, out_rows)
     )
     slabs = [modulated, zp, zm, two_a, zp2, zm2, before, after, two_b, z4_top, z4_bottom]
-    pieces = [in_rows, left, right, far_top, far_bottom]
-    pieces = pieces + near + [core_swap(far_top), core_swap(far_bottom)]
+    pieces = [in_rows, left, right, far] + near + [core_swap(right), core_swap(far)]
 
     out_pieces = [out_rows, x_shift(out_rows, 1), x_shift(out_rows, -1), x_shift(out_rows, 2)]
     keep, send = attend(where_am_i, block_mask, norm_gain, slabs, pieces)
@@ -422,11 +427,12 @@
     three = x_later(total, 3)
     two = x_later(one, 1)
     rest = core_swap(other)
-    sums = earlier_sum(where_am_i, step_index, step_sizes, one, two, three, own)
-    before = core_swap(sums)
-    velocity, advanced = advance(
-        where_am_i, step_index, step_sizes, one, two, three, own, other, before, rest, anchor
-    )
+    velocity, advanced = base(where_am_i, step_index, step_sizes, own, other, rest, anchor)
+    two, velocity, advanced = lax.optimization_barrier((two, velocity, advanced))
+    sums = one.astype(F32) + two.astype(F32) + three.astype(F32) + size_even * own.astype(F32)
+    earlier = core_swap(sums.astype(BF16))
+    advanced = add_half(where_am_i, True, advanced, [one, two, three], "add_near")
+    advanced = add_half(where_am_i, False, advanced, [earlier], "add_far")
     return (velocity[None], advanced[None])
 
 

time: 186 us -> 184 us (0.989)
  the two profiles are of different devices: /device:TPU:3 before, /device:TPU:79 now
where the time goes in v1:
time: 184 us; the launch traced here: 183 us
  waiting for transfers between devices  78.2 us (42%)
  Pallas kernels  45.3 us (25%)
  starting transfers between devices  42.5 us (23%)
  local copies, waits for them, and re-layouts  10 us (5%)
  between operations  3.56 us (2%)
  other arithmetic  3.09 us (2%)
    ppermute x7, waiting for transfers between devices, y_shift(): return lax.ppermute(block, 'frame', pairs)  36.3 us
    pallas_call x1, Pallas kernels, attend(): pl.pallas_call(attend_kernel, in_specs=[smem, smem, pl.BlockSpec(memory_s...  27.9 us
    ppermute x6, waiting for transfers between devices, z_shift(): return lax.ppermute(block, 'frame', pairs)  21.9 us
    ppermute x3, waiting for transfers between devices, x_later(): return lax.ppermute(block, 'step', pairs)  17 us
    ppermute x7, starting transfers between devices, y_shift(): return lax.ppermute(block, 'frame', pairs)  10.6 us
    ppermute x8, starting transfers between devices, core_swap(): return lax.ppermute(block, 'step', [(i, i ^ 1) for i in range(2 * NX)])  9.83 us
    all_to_all x1, starting transfers between devices, on_device(): lax.all_to_all(jnp.broadcast_to(packed[None], (NZ,) + packed.shape), 'fra...  7.55 us
    pallas_call x2, Pallas kernels, add_half(): pl.pallas_call(add_kernel, grid_spec=pltpu.PrefetchScalarGridSpec(num_sca...  5.74 us
  transfers between devices with their start and end apart: 31, of which 14 were waited for; matrix products, arithmetic and copies ran while one was open for 3% of the time, Pallas kernels for 21%

profile of v1, /device:TPU:79, one launch (start us, length us, event | category | flops | bytes accessed | tf_op | source)
XLA Modules:
  0.0 182.7 jit_solution(2983386315225074411)
XLA Ops:
  0.6 0.7 reshape.29
  1.4 0.8 pad_maximum_fusion.1
  2.2 0.7 broadcast_in_dim.15
  2.9 7.6 %all-to-all-start = ((bf16[8,8,2304]{2,1,0:T(8,128)(2,1)}), bf16[8,8,2304]{2,1,0:T(8,128)(2,1)S(1)}, u32[]{:S(2)}, u32[]{:S(2)}) async-start(bf16[8,8,2304]{2,1,0:T(8,128)(2,1)} %broadcast_in_dim.15), calls=%async_computation | async-start | bytes 589824 | tf_op jit(solution)/shard_map/all_to_all | solution.py:381
  10.4 0.7 pad_add_fusion.where_ref
  11.1 2.9 %modulate.1.refs_0_ = bf16[256,1536]{1,0:T(8,128)(2,1)} custom-call(s32[4]{0:T(128)} %pad_add_fusion.where_ref, s32[8]{0:T(128)} %index_ref.5, bf16[256,1536]{1,0:T(8,128)(2,1)} %bitcast.31, f32[3,50,1536]{2,1,0:T(8,128)} %bitcast.24), custom_call_target="tpu_custom_call" | custom-call | tf_op jit(solution)/shard_map/modulate/pallas_call | solution.py:63
  14.0 2.1 %collective-permute-start.1 = (bf16[256,1536]{1,0:T(8,128)(2,1)}, bf16[256,1536]{1,0:T(8,128)(2,1)}, u32[]{:S(2)}, u32[]{:S(2)}) collective-permute-start(bf16[256,1536]{1,0:T(8,128)(2,1)} %modulate.1.refs_0_), channel_id=1, source_target_pairs={{0,2},{1,3},{2,0},{3,1},{4,6},{5,7},{6,4},{7,5},{8,10},{9,11},{10,... | collective-permute-start | bytes 2359304 | tf_op jit(solution)/shard_map/ppermute | solution.py:22
  16.1 0.6 dynamic_slice.6
  18.7 0.6 dynamic_slice.7
  19.9 1.1 collective-permute-start
  21.1 0.4 collective-permute-start.3
  21.5 1.2 collective-permute-start.4
  22.7 0.3 collective-permute-start.5
  23.1 10.7 %collective-permute-done.1.refs_3_ = bf16[256,1536]{1,0:T(8,128)(2,1)} collective-permute-done((bf16[256,1536]{1,0:T(8,128)(2,1)}, bf16[256,1536]{1,0:T(8,128)(2,1)}, u32[]{:S(2)}, u32[]{:S(2)}) %collective-permute-start.1) | collective-permute-done | bytes 786464 | tf_op jit(solution)/shard_map/ppermute | solution.py:22
  33.8 2.0 %collective-permute-start.2 = (bf16[64,2304]{1,0:T(8,128)(2,1)S(1)}, bf16[64,2304]{1,0:T(8,128)(2,1)S(1)}, u32[]{:S(2)}, u32[]{:S(2)}) collective-permute-start(bf16[64,2304]{1,0:T(8,128)(2,1)S(1)} %bitcast.29), channel_id=1, source_target_pairs={{0,2},{1,3},{2,0},{3,1},{4,6},{5,7},{6,4},{7,5},{8,10},{9,11},{10,... | collective-permute-start | bytes 884744 | tf_op jit(solution)/shard_map/ppermute | solution.py:22
  35.8 7.4 %collective-permute-done = bf16[64,2304]{1,0:T(8,128)(2,1)S(1)} collective-permute-done((bf16[64,2304]{1,0:T(8,128)(2,1)S(1)}, bf16[64,2304]{1,0:T(8,128)(2,1)S(1)}, u32[]{:S(2)}, u32[]{:S(2)}) %collective-permute-start) | collective-permute-done | bytes 294944 | tf_op jit(solution)/shard_map/ppermute | solution.py:22
  43.3 3.0 %collective-permute-done.2 = bf16[64,2304]{1,0:T(8,128)(2,1)S(1)} collective-permute-done((bf16[64,2304]{1,0:T(8,128)(2,1)S(1)}, bf16[64,2304]{1,0:T(8,128)(2,1)S(1)}, u32[]{:S(2)}, u32[]{:S(2)}) %collective-permute-start.2) | collective-permute-done | bytes 294944 | tf_op jit(solution)/shard_map/ppermute | solution.py:22
  46.4 1.2 reshape.35.refs_11_
  47.6 0.2 collective-permute-start.6
  47.8 0.2 copy-done.2
  48.0 1.3 broadcast_select_fusion.1
  49.5 1.3 collective-permute-start.9
  50.8 1.2 collective-permute-start.7
  51.9 0.3 collective-permute-start.8
  52.2 0.3 slice.13
  52.5 0.2 reshape.36
  52.7 13.6 %collective-permute-done.10.refs_7_ = bf16[256,1536]{1,0:T(8,128)(2,1)} collective-permute-done((bf16[256,1536]{1,0:T(8,128)(2,1)}, bf16[256,1536]{1,0:T(8,128)(2,1)}, u32[]{:S(2)}, u32[]{:S(2)}) %collective-permute-start.10) | collective-permute-done | bytes 786464 | tf_op jit(solution)/shard_map/ppermute | solution.py:22
  66.4 1.4 collective-permute-done.9.refs_6_
  67.8 1.4 collective-permute-done.8.refs_5_
  69.2 0.9 collective-permute-start.11
  70.1 1.8 collective-permute-start.12
  72.0 3.5 %collective-permute-start.15 = (bf16[256,1536]{1,0:T(8,128)(2,1)S(1)}, bf16[256,1536]{1,0:T(8,128)(2,1)S(1)}, u32[]{:S(2)}, u32[]{:S(2)}) collective-permute-start(bf16[256,1536]{1,0:T(8,128)(2,1)S(1)} %broadcast_select_fusion), channel_id=1, source_target_pairs={{0,2},{1,3},{2,0},{3,1},{4,6},{5,7},{6,4},{7,5},{8,10},{9,11},{10,... | collective-permute-start | bytes 2359304 | tf_op jit(solution)/shard_map/ppermute | solution.py:22
  75.5 4.6 %collective-permute-start.16 = (bf16[96,1536]{1,0:T(8,128)(2,1)S(1)}, bf16[96,1536]{1,0:T(8,128)(2,1)S(1)}, u32[]{:S(2)}, u32[]{:S(2)}) collective-permute-start(bf16[96,1536]{1,0:T(8,128)(2,1)S(1)} %reshape.36), channel_id=1, source_target_pairs={{0,32},{32,0},{64,96},{96,64},{128,160},{160,128},{192,224},{224,1... | collective-permute-start | bytes 884744 | tf_op jit(solution)/shard_map/ppermute | solution.py:41
  80.0 1.0 slice.14
  81.1 2.5 %collective-permute-start.13 = (bf16[128,1536]{1,0:T(8,128)(2,1)S(1)}, bf16[128,1536]{1,0:T(8,128)(2,1)}, u32[]{:S(2)}, u32[]{:S(2)}) collective-permute-start(bf16[128,1536]{1,0:T(8,128)(2,1)S(1)} %slice.14), channel_id=1, source_target_pairs={{0,8},{1,9},{2,10},{3,11},{4,12},{5,13},{6,14},{7,15},{8,16},{9,17... | collective-permute-start | bytes 1179656 | tf_op jit(solution)/shard_map/ppermute | solution.py:27
  83.6 1.0 slice.15
  84.8 11.3 %collective-permute-done.13.refs_9_ = bf16[128,1536]{1,0:T(8,128)(2,1)} collective-permute-done((bf16[128,1536]{1,0:T(8,128)(2,1)S(1)}, bf16[128,1536]{1,0:T(8,128)(2,1)}, u32[]{:S(2)}, u32[]{:S(2)}) %collective-permute-start.13) | collective-permute-done | bytes 393248 | tf_op jit(solution)/shard_map/ppermute | solution.py:27
  96.0 0.7 collective-permute-start.17
  96.7 9.3 %collective-permute-done.14.refs_10_ = bf16[128,1536]{1,0:T(8,128)(2,1)} collective-permute-done((bf16[128,1536]{1,0:T(8,128)(2,1)S(1)}, bf16[128,1536]{1,0:T(8,128)(2,1)}, u32[]{:S(2)}, u32[]{:S(2)}) %collective-permute-start.14) | collective-permute-done | bytes 393248 | tf_op jit(solution)/shard_map/ppermute | solution.py:27
  106.0 0.9 collective-permute-start.18
  107.0 0.5 collective-permute-start.20
  107.5 1.5 collective-permute-start.23
  109.1 0.8 collective-permute-start.24
  110.0 1.5 collective-permute-done.19.refs_17_
  111.5 1.0 copy-done.21
  112.5 27.9 %attend.1 = (bf16[128,768]{1,0:T(8,128)(2,1)}, bf16[128,768]{1,0:T(8,128)(2,1)}) custom-call(s32[4]{0:T(128)} %pad_add_fusion.where_ref, s32[2,64]{1,0:T(2,128)} %mask_ref.1, f32[2,768]{1,0:T(2,128)} %gain_ref.1, bf16[256,1536]{1,0:T(8,128)(2,1)} %modulate.1.refs_0_, bf16[256,1536]{1,0:T(8,128)(2,1)} %copy-done, bf16[256,1536]{1,0:T(8,128)(2,1)} %copy-done.1, ...), custom_call_target="tpu_custom_call" | custom-call | flops 16000000000 | bytes 16000000 | tf_op jit(solution)/shard_map/attend/pallas_call | solution.py:188
  140.3 0.4 collective-permute-start.21
  140.8 1.2 collective-permute-done.21.got_ref
  142.1 0.7 copy-done.14
  142.8 4.5 %output.1 = (bf16[128,1536]{1,0:T(8,128)(2,1)}, bf16[128,1536]{1,0:T(8,128)(2,1)}, bf16[128,1536]{1,0:T(8,128)(2,1)}) custom-call(s32[4]{0:T(128)} %pad_add_fusion.where_ref, s32[8]{0:T(128)} %index_ref.5, f32[50]{0:T(128)} %size_ref.3, bf16[128,768]{1,0:T(8,128)(2,1)} %get-tuple-element.56.keep_ref, bf16[128,768]{1,0:T(8,128)(2,1)} %copy-done.14, ...), custom_call_target="tpu_custom_call" | custom-call | tf_op jit(solution)/shard_map/output/pallas_call | solution.py:256
  147.3 1.3 collective-permute-start.25
  148.6 0.4 collective-permute-start.27
  149.0 10.7 %collective-permute-done.25.refs_1_ = bf16[128,1536]{1,0:T(8,128)(2,1)S(1)} collective-permute-done((bf16[128,1536]{1,0:T(8,128)(2,1)}, bf16[128,1536]{1,0:T(8,128)(2,1)S(1)}, u32[]{:S(2)}, u32[]{:S(2)}) %collective-permute-start.25) | collective-permute-done | bytes 393248 | tf_op jit(solution)/shard_map/ppermute | solution.py:37
  159.7 1.3 collective-permute-start.26
  161.0 1.3 collective-permute-start.28
  162.3 0.8 copy-done.12
  163.1 4.3 %base.1 = (bf16[256,1536]{1,0:T(8,128)(2,1)}, f32[256,1536]{1,0:T(8,128)}) custom-call(s32[4]{0:T(128)} %pad_add_fusion.where_ref, s32[8]{0:T(128)} %index_ref.5, f32[50]{0:T(128)} %size_ref.3, bf16[128,1536]{1,0:T(8,128)(2,1)} %get-tuple-element.60.own_ref, bf16[128,1536]{1,0:T(8,128)(2,1)} %get-tuple-element.61.other_ref, bf16[128,1536]{1,0:T(8,128)(2,1)} %copy-done.12, ...), custom_call_target="tpu_custom_call" | custom-call | flops 3000000 | bytes 6000000 | tf_op jit(solution)/shard_map/base/pallas_call | solution.py:301
  167.4 3.6 %collective-permute-done.26.refs_2_ = bf16[128,1536]{1,0:T(8,128)(2,1)S(1)} collective-permute-done((bf16[128,1536]{1,0:T(8,128)(2,1)S(1)}, bf16[128,1536]{1,0:T(8,128)(2,1)S(1)}, u32[]{:S(2)}, u32[]{:S(2)}) %collective-permute-start.26) | collective-permute-done | bytes 393248 | tf_op jit(solution)/shard_map/ppermute | solution.py:37
  171.0 2.7 %collective-permute-done.28.refs_3_ = bf16[128,1536]{1,0:T(8,128)(2,1)S(1)} collective-permute-done((bf16[128,1536]{1,0:T(8,128)(2,1)}, bf16[128,1536]{1,0:T(8,128)(2,1)S(1)}, u32[]{:S(2)}, u32[]{:S(2)}) %collective-permute-start.28) | collective-permute-done | bytes 393248 | tf_op jit(solution)/shard_map/ppermute | solution.py:37
  173.8 0.2 add_convert_fusion
  174.0 2.2 %collective-permute-start.29 = (bf16[128,1536]{1,0:T(8,128)(2,1)S(1)}, bf16[128,1536]{1,0:T(8,128)(2,1)S(1)}, u32[]{:S(2)}, u32[]{:S(2)}) collective-permute-start(bf16[128,1536]{1,0:T(8,128)(2,1)S(1)} %add_convert_fusion), channel_id=1, source_target_pairs={{0,32},{32,0},{64,96},{96,64},{128,160},{160,128},{192,224},{224,1... | collective-permute-start | bytes 1179656 | tf_op jit(solution)/shard_map/ppermute | solution.py:41
  176.2 3.0 %add_near.1.refs_0_ = f32[256,1536]{1,0:T(8,128)} custom-call(s32[4]{0:T(128)} %pad_add_fusion.where_ref, f32[256,1536]{1,0:T(8,128)} %get-tuple-element.65.refs_0_, bf16[128,1536]{1,0:T(8,128)(2,1)} %copy-done.4, bf16[128,1536]{1,0:T(8,128)(2,1)} %copy-done.5, bf16[128,1536]{1,0:T(8,128)(2,1)} %copy-done.6), custom_call_target="tpu_custom_call", output_to_operand_aliasing={{}: (1, {})} | custom-call | tf_op jit(solution)/shard_map/add_near/pallas_call | solution.py:331
  179.2 0.8 copy-done.13
  180.0 2.7 %add_far.1 = f32[256,1536]{1,0:T(8,128)} custom-call(s32[4]{0:T(128)} %pad_add_fusion.where_ref, f32[256,1536]{1,0:T(8,128)} %add_near.1.refs_0_, bf16[128,1536]{1,0:T(8,128)(2,1)} %copy-done.13), custom_call_target="tpu_custom_call", output_to_operand_aliasing={{}: (1, {})} | custom-call | tf_op jit(solution)/shard_map/add_far/pallas_call | solution.py:331
  (70 shorter events, 0.9 us)
Async XLA Ops:
  2.9 17.0 %all-to-all-start = ((bf16[8,8,2304]{2,1,0:T(8,128)(2,1)}), bf16[8,8,2304]{2,1,0:T(8,128)(2,1)S(1)}, u32[]{:S(2)}, u32[]{:S(2)}) async-start(bf16[8,8,2304]{2,1,0:T(8,128)(2,1)} %broadcast_in_dim.15), calls=%async_computation | async-start | bytes 589824 | tf_op jit(solution)/shard_map/all_to_all | solution.py:381
  11.1 5.0 %copy-start.15 = (s32[8]{0:T(128)S(1)}, s32[8]{0:T(128)}, u32[]{:S(2)}) copy-start(s32[8]{0:T(128)} %index_ref.5) | copy-start | bytes 100
  11.1 7.6 %copy-start.16 = (f32[50]{0:T(128)S(1)}, f32[50]{0:T(128)}, u32[]{:S(2)}) copy-start(f32[50]{0:T(128)} %size_ref.3) | copy-start | bytes 604
  14.0 19.7 %collective-permute-start.1 = (bf16[256,1536]{1,0:T(8,128)(2,1)}, bf16[256,1536]{1,0:T(8,128)(2,1)}, u32[]{:S(2)}, u32[]{:S(2)}) collective-permute-start(bf16[256,1536]{1,0:T(8,128)(2,1)} %modulate.1.refs_0_), channel_id=1, source_target_pairs={{0,2},{1,3},{2,0},{3,1},{4,6},{5,7},{6,4},{7,5},{8,10},{9,11},{10,... | collective-permute-start | bytes 2359304 | tf_op jit(solution)/shard_map/ppermute | solution.py:22
  19.9 23.3 %collective-permute-start = (bf16[64,2304]{1,0:T(8,128)(2,1)S(1)}, bf16[64,2304]{1,0:T(8,128)(2,1)S(1)}, u32[]{:S(2)}, u32[]{:S(2)}) collective-permute-start(bf16[64,2304]{1,0:T(8,128)(2,1)S(1)} %bitcast.26), channel_id=1, source_target_pairs={{0,3},{1,0},{2,1},{3,2},{4,7},{5,4},{6,5},{7,6},{8,11},{9,8},{10,9... | collective-permute-start | bytes 884744 | tf_op jit(solution)/shard_map/ppermute | solution.py:22
  21.1 25.2 %collective-permute-start.3 = (bf16[64,2304]{1,0:T(8,128)(2,1)S(1)}, bf16[64,2304]{1,0:T(8,128)(2,1)S(1)}, u32[]{:S(2)}, u32[]{:S(2)}) collective-permute-start(bf16[64,2304]{1,0:T(8,128)(2,1)S(1)} %bitcast.27), channel_id=1, source_target_pairs={{0,1},{1,2},{2,3},{3,0},{4,5},{5,6},{6,7},{7,4},{8,9},{9,10},{10,1... | collective-permute-start | bytes 884744 | tf_op jit(solution)/shard_map/ppermute | solution.py:22
  21.5 24.9 %collective-permute-start.4 = (bf16[256,1536]{1,0:T(8,128)(2,1)}, bf16[256,1536]{1,0:T(8,128)(2,1)S(1)}, u32[]{:S(2)}, u32[]{:S(2)}) collective-permute-start(bf16[256,1536]{1,0:T(8,128)(2,1)} %modulate.1.refs_0_), channel_id=1, source_target_pairs={{0,4},{1,5},{2,6},{3,7},{4,8},{5,9},{6,10},{7,11},{8,12},{9,13},{1... | collective-permute-start | bytes 2359304 | tf_op jit(solution)/shard_map/ppermute | solution.py:27
  22.7 23.7 %collective-permute-start.5 = (bf16[256,1536]{1,0:T(8,128)(2,1)}, bf16[256,1536]{1,0:T(8,128)(2,1)S(1)}, u32[]{:S(2)}, u32[]{:S(2)}) collective-permute-start(bf16[256,1536]{1,0:T(8,128)(2,1)} %modulate.1.refs_0_), channel_id=1, source_target_pairs={{0,28},{1,29},{2,30},{3,31},{4,0},{5,1},{6,2},{7,3},{8,4},{9,5},{1... | collective-permute-start | bytes 2359304 | tf_op jit(solution)/shard_map/ppermute | solution.py:27
  33.8 12.5 %collective-permute-start.2 = (bf16[64,2304]{1,0:T(8,128)(2,1)S(1)}, bf16[64,2304]{1,0:T(8,128)(2,1)S(1)}, u32[]{:S(2)}, u32[]{:S(2)}) collective-permute-start(bf16[64,2304]{1,0:T(8,128)(2,1)S(1)} %bitcast.29), channel_id=1, source_target_pairs={{0,2},{1,3},{2,0},{3,1},{4,6},{5,7},{6,4},{7,5},{8,10},{9,11},{10,... | collective-permute-start | bytes 884744 | tf_op jit(solution)/shard_map/ppermute | solution.py:22
  46.4 1.6 copy-start.2
  46.4 25.5 %copy-start = (bf16[256,1536]{1,0:T(8,128)(2,1)}, bf16[256,1536]{1,0:T(8,128)(2,1)S(1)}, u32[]{:S(2)}) copy-start(bf16[256,1536]{1,0:T(8,128)(2,1)S(1)} %collective-permute-done.4.refs_1_) | copy-start | bytes 2359300
  46.4 25.4 %copy-start.1 = (bf16[256,1536]{1,0:T(8,128)(2,1)}, bf16[256,1536]{1,0:T(8,128)(2,1)S(1)}, u32[]{:S(2)}) copy-start(bf16[256,1536]{1,0:T(8,128)(2,1)S(1)} %collective-permute-done.5.refs_2_) | copy-start | bytes 2359300
  47.6 21.6 %collective-permute-start.6 = (bf16[192,2304]{1,0:T(8,128)(2,1)}, bf16[192,2304]{1,0:T(8,128)(2,1)}, u32[]{:S(2)}, u32[]{:S(2)}) collective-permute-start(bf16[192,2304]{1,0:T(8,128)(2,1)} %reshape.35.refs_11_), channel_id=1, source_target_pairs={{0,64},{32,96},{64,128},{96,160},{128,192},{160,224},{192,0},{224,... | collective-permute-start | bytes 2654216 | tf_op jit(solution)/shard_map/ppermute | solution.py:32
  49.3 17.1 %collective-permute-start.10 = (bf16[256,1536]{1,0:T(8,128)(2,1)}, bf16[256,1536]{1,0:T(8,128)(2,1)}, u32[]{:S(2)}, u32[]{:S(2)}) collective-permute-start(bf16[256,1536]{1,0:T(8,128)(2,1)} %get-tuple-element.68), channel_id=1, source_target_pairs={{0,3},{1,0},{2,1},{3,2},{4,7},{5,4},{6,5},{7,6},{8,11},{9,8},{10,9... | collective-permute-start | bytes 2359304 | tf_op jit(solution)/shard_map/ppermute | solution.py:22
  49.5 18.4 %collective-permute-start.9 = (bf16[256,1536]{1,0:T(8,128)(2,1)}, bf16[256,1536]{1,0:T(8,128)(2,1)}, u32[]{:S(2)}, u32[]{:S(2)}) collective-permute-start(bf16[256,1536]{1,0:T(8,128)(2,1)} %get-tuple-element.69), channel_id=1, source_target_pairs={{0,1},{1,2},{2,3},{3,0},{4,5},{5,6},{6,7},{7,4},{8,9},{9,10},{10,1... | collective-permute-start | bytes 2359304 | tf_op jit(solution)/shard_map/ppermute | solution.py:22
  50.8 17.1 %collective-permute-start.7 = (bf16[256,1536]{1,0:T(8,128)(2,1)S(1)}, bf16[256,1536]{1,0:T(8,128)(2,1)}, u32[]{:S(2)}, u32[]{:S(2)}) collective-permute-start(bf16[256,1536]{1,0:T(8,128)(2,1)S(1)} %collective-permute-done.4.refs_1_), channel_id=1, source_target_pairs={{0,4},{1,5},{2,6},{3,7},{4,8},{5,9},{6,10},{7,11},{8,12},{9,13},{1... | collective-permute-start | bytes 2359304 | tf_op jit(solution)/shard_map/ppermute | solution.py:27
  51.9 17.2 %collective-permute-start.8 = (bf16[256,1536]{1,0:T(8,128)(2,1)S(1)}, bf16[256,1536]{1,0:T(8,128)(2,1)}, u32[]{:S(2)}, u32[]{:S(2)}) collective-permute-start(bf16[256,1536]{1,0:T(8,128)(2,1)S(1)} %collective-permute-done.5.refs_2_), channel_id=1, source_target_pairs={{0,28},{1,29},{2,30},{3,31},{4,0},{5,1},{6,2},{7,3},{8,4},{9,5},{1... | collective-permute-start | bytes 2359304 | tf_op jit(solution)/shard_map/ppermute | solution.py:27
  69.2 37.7 %collective-permute-start.11 = (bf16[192,2304]{1,0:T(8,128)(2,1)}, bf16[192,2304]{1,0:T(8,128)(2,1)S(1)}, u32[]{:S(2)}, u32[]{:S(2)}) collective-permute-start(bf16[192,2304]{1,0:T(8,128)(2,1)} %reshape.35.refs_11_), channel_id=1, source_target_pairs={{0,192},{32,224},{64,0},{96,32},{128,64},{160,96},{192,128},{224,1... | collective-permute-start | bytes 2654216 | tf_op jit(solution)/shard_map/ppermute | solution.py:32
  70.1 36.8 %collective-permute-start.12 = (bf16[192,2304]{1,0:T(8,128)(2,1)}, bf16[192,2304]{1,0:T(8,128)(2,1)S(1)}, u32[]{:S(2)}, u32[]{:S(2)}) collective-permute-start(bf16[192,2304]{1,0:T(8,128)(2,1)} %collective-permute-done.6.refs_12_), channel_id=1, source_target_pairs={{0,64},{32,96},{64,128},{96,160},{128,192},{160,224},{192,0},{224,... | collective-permute-start | bytes 2654216 | tf_op jit(solution)/shard_map/ppermute | solution.py:32
  72.0 34.9 %collective-permute-start.15 = (bf16[256,1536]{1,0:T(8,128)(2,1)S(1)}, bf16[256,1536]{1,0:T(8,128)(2,1)S(1)}, u32[]{:S(2)}, u32[]{:S(2)}) collective-permute-start(bf16[256,1536]{1,0:T(8,128)(2,1)S(1)} %broadcast_select_fusion), channel_id=1, source_target_pairs={{0,2},{1,3},{2,0},{3,1},{4,6},{5,7},{6,4},{7,5},{8,10},{9,11},{10,... | collective-permute-start | bytes 2359304 | tf_op jit(solution)/shard_map/ppermute | solution.py:22
  75.5 9.1 %collective-permute-start.16 = (bf16[96,1536]{1,0:T(8,128)(2,1)S(1)}, bf16[96,1536]{1,0:T(8,128)(2,1)S(1)}, u32[]{:S(2)}, u32[]{:S(2)}) collective-permute-start(bf16[96,1536]{1,0:T(8,128)(2,1)S(1)} %reshape.36), channel_id=1, source_target_pairs={{0,32},{32,0},{64,96},{96,64},{128,160},{160,128},{192,224},{224,1... | collective-permute-start | bytes 884744 | tf_op jit(solution)/shard_map/ppermute | solution.py:41
  81.1 15.0 %copy-start.8 = (bf16[192,2304]{1,0:T(8,128)(2,1)S(1)}, bf16[192,2304]{1,0:T(8,128)(2,1)}, u32[]{:S(2)}) copy-start(bf16[192,2304]{1,0:T(8,128)(2,1)} %reshape.35.refs_11_) | copy-start | bytes 2654212
  81.1 14.9 %collective-permute-start.13 = (bf16[128,1536]{1,0:T(8,128)(2,1)S(1)}, bf16[128,1536]{1,0:T(8,128)(2,1)}, u32[]{:S(2)}, u32[]{:S(2)}) collective-permute-start(bf16[128,1536]{1,0:T(8,128)(2,1)S(1)} %slice.14), channel_id=1, source_target_pairs={{0,8},{1,9},{2,10},{3,11},{4,12},{5,13},{6,14},{7,15},{8,16},{9,17... | collective-permute-start | bytes 1179656 | tf_op jit(solution)/shard_map/ppermute | solution.py:27
  84.6 21.4 %collective-permute-start.14 = (bf16[128,1536]{1,0:T(8,128)(2,1)S(1)}, bf16[128,1536]{1,0:T(8,128)(2,1)}, u32[]{:S(2)}, u32[]{:S(2)}) collective-permute-start(bf16[128,1536]{1,0:T(8,128)(2,1)S(1)} %slice.15), channel_id=1, source_target_pairs={{0,24},{1,25},{2,26},{3,27},{4,28},{5,29},{6,30},{7,31},{8,0},{9,1... | collective-permute-start | bytes 1179656 | tf_op jit(solution)/shard_map/ppermute | solution.py:27
  84.7 55.6 %copy-start.3 = (bf16[2,96,1536]{2,1,0:T(8,128)(2,1)}, bf16[2,96,1536]{2,1,0:T(8,128)(2,1)S(1)}, u32[]{:S(2)}) copy-start(bf16[2,96,1536]{2,1,0:T(8,128)(2,1)S(1)} %pad_maximum_fusion.refs_0_) | copy-start | bytes 1769476
  96.0 11.5 %collective-permute-start.17 = (bf16[192,2304]{1,0:T(8,128)(2,1)S(1)}, bf16[192,2304]{1,0:T(8,128)(2,1)S(1)}, u32[]{:S(2)}, u32[]{:S(2)}) collective-permute-start(bf16[192,2304]{1,0:T(8,128)(2,1)S(1)} %copy-done.8), channel_id=1, source_target_pairs={{0,32},{32,0},{64,96},{96,64},{128,160},{160,128},{192,224},{224,1... | collective-permute-start | bytes 2654216 | tf_op jit(solution)/shard_map/ppermute | solution.py:41
  106.0 3.1 %collective-permute-start.18 = (bf16[192,2304]{1,0:T(8,128)(2,1)}, bf16[192,2304]{1,0:T(8,128)(2,1)S(1)}, u32[]{:S(2)}, u32[]{:S(2)}) collective-permute-start(bf16[192,2304]{1,0:T(8,128)(2,1)} %collective-permute-done.6.refs_12_), channel_id=1, source_target_pairs={{0,32},{32,0},{64,96},{96,64},{128,160},{160,128},{192,224},{224,1... | collective-permute-start | bytes 2654216 | tf_op jit(solution)/shard_map/ppermute | solution.py:41
  106.9 5.5 %copy-start.22 = (bf16[256,1536]{1,0:T(8,128)(2,1)}, bf16[256,1536]{1,0:T(8,128)(2,1)S(1)}, u32[]{:S(2)}) copy-start(bf16[256,1536]{1,0:T(8,128)(2,1)S(1)} %collective-permute-done.15.refs_8_) | copy-start | bytes 2359300
  106.9 5.5 %copy-start.17 = (bf16[192,2304]{1,0:T(8,128)(2,1)}, bf16[192,2304]{1,0:T(8,128)(2,1)S(1)}, u32[]{:S(2)}) copy-start(bf16[192,2304]{1,0:T(8,128)(2,1)S(1)} %collective-permute-done.11.refs_13_) | copy-start | bytes 2654212
  106.9 5.5 %copy-start.18 = (bf16[192,2304]{1,0:T(8,128)(2,1)}, bf16[192,2304]{1,0:T(8,128)(2,1)S(1)}, u32[]{:S(2)}) copy-start(bf16[192,2304]{1,0:T(8,128)(2,1)S(1)} %collective-permute-done.12.refs_14_) | copy-start | bytes 2654212
  106.9 4.5 %collective-permute-start.19 = (bf16[192,2304]{1,0:T(8,128)(2,1)S(1)}, bf16[192,2304]{1,0:T(8,128)(2,1)S(1)}, u32[]{:S(2)}, u32[]{:S(2)}) collective-permute-start(bf16[192,2304]{1,0:T(8,128)(2,1)S(1)} %collective-permute-done.11.refs_13_), channel_id=1, source_target_pairs={{0,32},{32,0},{64,96},{96,64},{128,160},{160,128},{192,224},{224,1... | collective-permute-start | bytes 2654216 | tf_op jit(solution)/shard_map/ppermute | solution.py:41
  107.0 5.4 %collective-permute-start.20 = (bf16[192,2304]{1,0:T(8,128)(2,1)S(1)}, bf16[192,2304]{1,0:T(8,128)(2,1)}, u32[]{:S(2)}, u32[]{:S(2)}) collective-permute-start(bf16[192,2304]{1,0:T(8,128)(2,1)S(1)} %collective-permute-done.12.refs_14_), channel_id=1, source_target_pairs={{0,32},{32,0},{64,96},{96,64},{128,160},{160,128},{192,224},{224,1... | collective-permute-start | bytes 2654216 | tf_op jit(solution)/shard_map/ppermute | solution.py:41
  107.5 33.3 %collective-permute-start.22 = (bf16[2,96,1536]{2,1,0:T(8,128)(2,1)S(1)}, bf16[2,96,1536]{2,1,0:T(8,128)(2,1)S(1)}, u32[]{:S(2)}, u32[]{:S(2)}) collective-permute-start(bf16[2,96,1536]{2,1,0:T(8,128)(2,1)S(1)} %pad_maximum_fusion.refs_0_), channel_id=1, source_target_pairs={{0,64},{32,96},{64,128},{96,160},{128,192},{160,224},{192,0},{224,... | collective-permute-start | bytes 1769480 | tf_op jit(solution)/shard_map/ppermute | solution.py:32
  107.5 4.9 %copy-start.19 = (bf16[192,2304]{1,0:T(8,128)(2,1)}, bf16[192,2304]{1,0:T(8,128)(2,1)S(1)}, u32[]{:S(2)}) copy-start(bf16[192,2304]{1,0:T(8,128)(2,1)S(1)} %collective-permute-done.17.refs_15_) | copy-start | bytes 2654212
  107.5 33.3 %collective-permute-start.23 = (bf16[2,96,1536]{2,1,0:T(8,128)(2,1)S(1)}, bf16[2,96,1536]{2,1,0:T(8,128)(2,1)S(1)}, u32[]{:S(2)}, u32[]{:S(2)}) collective-permute-start(bf16[2,96,1536]{2,1,0:T(8,128)(2,1)S(1)} %pad_maximum_fusion.refs_0_), channel_id=1, source_target_pairs={{0,192},{32,224},{64,0},{96,32},{128,64},{160,96},{192,128},{224,1... | collective-permute-start | bytes 1769480 | tf_op jit(solution)/shard_map/ppermute | solution.py:32
  109.1 3.3 %copy-start.20 = (bf16[192,2304]{1,0:T(8,128)(2,1)}, bf16[192,2304]{1,0:T(8,128)(2,1)S(1)}, u32[]{:S(2)}) copy-start(bf16[192,2304]{1,0:T(8,128)(2,1)S(1)} %collective-permute-done.18.refs_16_) | copy-start | bytes 2654212
  109.1 31.7 %collective-permute-start.24 = (bf16[2,96,1536]{2,1,0:T(8,128)(2,1)S(1)}, bf16[2,96,1536]{2,1,0:T(8,128)(2,1)S(1)}, u32[]{:S(2)}, u32[]{:S(2)}) collective-permute-start(bf16[2,96,1536]{2,1,0:T(8,128)(2,1)S(1)} %pad_maximum_fusion.refs_0_), channel_id=1, source_target_pairs={{0,128},{32,160},{64,192},{96,224},{128,0},{160,32},{192,64},{224,... | collective-permute-start | bytes 1769480 | tf_op jit(solution)/shard_map/ppermute | solution.py:32
  111.5 1.0 copy-start.21
  140.3 1.7 collective-permute-start.21
  140.8 1.3 copy-start.9
  140.8 1.3 copy-start.10
  140.8 1.3 copy-start.11
  142.1 0.7 copy-start.14
  147.3 12.4 %collective-permute-start.25 = (bf16[128,1536]{1,0:T(8,128)(2,1)}, bf16[128,1536]{1,0:T(8,128)(2,1)S(1)}, u32[]{:S(2)}, u32[]{:S(2)}) collective-permute-start(bf16[128,1536]{1,0:T(8,128)(2,1)} %get-tuple-element.59), channel_id=1, source_target_pairs={{0,64},{32,96},{64,128},{96,160},{128,192},{160,224},{1,65},{33,97... | collective-permute-start | bytes 1179656 | tf_op jit(solution)/shard_map/ppermute | solution.py:37
  148.6 13.7 %collective-permute-start.27 = (bf16[128,1536]{1,0:T(8,128)(2,1)}, bf16[128,1536]{1,0:T(8,128)(2,1)S(1)}, u32[]{:S(2)}, u32[]{:S(2)}) collective-permute-start(bf16[128,1536]{1,0:T(8,128)(2,1)} %get-tuple-element.61.other_ref), channel_id=1, source_target_pairs={{0,32},{32,0},{64,96},{96,64},{128,160},{160,128},{192,224},{224,1... | collective-permute-start | bytes 1179656 | tf_op jit(solution)/shard_map/ppermute | solution.py:41
  159.7 14.0 %copy-start.4 = (bf16[128,1536]{1,0:T(8,128)(2,1)}, bf16[128,1536]{1,0:T(8,128)(2,1)S(1)}, u32[]{:S(2)}) copy-start(bf16[128,1536]{1,0:T(8,128)(2,1)S(1)} %collective-permute-done.25.refs_1_) | copy-start | bytes 1179652
  159.7 11.3 %collective-permute-start.26 = (bf16[128,1536]{1,0:T(8,128)(2,1)S(1)}, bf16[128,1536]{1,0:T(8,128)(2,1)S(1)}, u32[]{:S(2)}, u32[]{:S(2)}) collective-permute-start(bf16[128,1536]{1,0:T(8,128)(2,1)S(1)} %collective-permute-done.25.refs_1_), channel_id=1, source_target_pairs={{0,64},{32,96},{64,128},{96,160},{128,192},{160,224},{1,65},{33,97... | collective-permute-start | bytes 1179656 | tf_op jit(solution)/shard_map/ppermute | solution.py:37
  161.0 12.7 %collective-permute-start.28 = (bf16[128,1536]{1,0:T(8,128)(2,1)}, bf16[128,1536]{1,0:T(8,128)(2,1)S(1)}, u32[]{:S(2)}, u32[]{:S(2)}) collective-permute-start(bf16[128,1536]{1,0:T(8,128)(2,1)} %get-tuple-element.59), channel_id=1, source_target_pairs={{0,192},{32,224},{1,193},{33,225},{2,194},{34,226},{3,195},{35,227... | collective-permute-start | bytes 1179656 | tf_op jit(solution)/shard_map/ppermute | solution.py:37
  162.3 0.8 copy-start.12
  163.1 10.7 %copy-start.7 = (bf16[128,1536]{1,0:T(8,128)(2,1)S(1)}, bf16[128,1536]{1,0:T(8,128)(2,1)}, u32[]{:S(2)}) copy-start(bf16[128,1536]{1,0:T(8,128)(2,1)} %get-tuple-element.60.own_ref) | copy-start | bytes 1179652
  171.0 5.2 %copy-start.5 = (bf16[128,1536]{1,0:T(8,128)(2,1)}, bf16[128,1536]{1,0:T(8,128)(2,1)S(1)}, u32[]{:S(2)}) copy-start(bf16[128,1536]{1,0:T(8,128)(2,1)S(1)} %collective-permute-done.26.refs_2_) | copy-start | bytes 1179652
  173.8 2.4 %copy-start.6 = (bf16[128,1536]{1,0:T(8,128)(2,1)}, bf16[128,1536]{1,0:T(8,128)(2,1)S(1)}, u32[]{:S(2)}) copy-start(bf16[128,1536]{1,0:T(8,128)(2,1)S(1)} %collective-permute-done.28.refs_3_) | copy-start | bytes 1179652
  174.0 5.2 %collective-permute-start.29 = (bf16[128,1536]{1,0:T(8,128)(2,1)S(1)}, bf16[128,1536]{1,0:T(8,128)(2,1)S(1)}, u32[]{:S(2)}, u32[]{:S(2)}) collective-permute-start(bf16[128,1536]{1,0:T(8,128)(2,1)S(1)} %add_convert_fusion), channel_id=1, source_target_pairs={{0,32},{32,0},{64,96},{96,64},{128,160},{160,128},{192,224},{224,1... | collective-permute-start | bytes 1179656 | tf_op jit(solution)/shard_map/ppermute | solution.py:41
  179.2 0.8 copy-start.13

commit v2 on v0

--- a/solution.py
+++ b/solution.py
@@ -19,6 +19,12 @@
 
 def y_shift(block, distance):
     pairs = [(4 * z + y, 4 * z + (y + distance) % NY) for z in range(NZ) for y in range(NY)]
+    return lax.ppermute(block, "frame", pairs)
+
+
+def y_step(block, distance, edge):
+    pairs = [(4 * z + y, 4 * z + (y + distance) % NY) for z in range(NZ) for y in range(NY)]
+    pairs = [(i, j) for i, j in pairs if (i + distance != j) == edge]
     return lax.ppermute(block, "frame", pairs)
 
 
@@ -85,10 +91,10 @@
     *refs,
 ):
     slabs = refs[:9]
-    z4_top, z4_bottom = refs[9:11]
-    pieces = refs[11:21]
-    keep_ref, send_ref = refs[21:23]
-    m_s, w_s, k_s, v_s, q_s, bias_s, m_sem, w_sem = refs[23:]
+    z4_top, z4_bottom, before_edge, after_edge = refs[9:13]
+    pieces = refs[13:23]
+    keep_ref, send_ref = refs[23:25]
+    m_s, w_s, k_s, v_s, q_s, bias_s, m_sem, w_sem = refs[25:]
     x, core, frame = where_ref[1], where_ref[2], where_ref[3]
     rows = q_s.shape[0]
     feats = q_s.shape[1]
@@ -120,8 +126,23 @@
     copies_m[0].start()
     for copy in copies_w:
         copy.start()
-    for copy in copies_m[1:]:
-        copy.start()
+    row_y = lax.rem(frame, NY)
+    for i, edge_ref, at_edge in ((6, before_edge, 0), (7, after_edge, NY - 1)):
+        edge_copy = pltpu.make_async_copy(
+            edge_ref, m_s.at[pl.ds(i * rows, rows)], m_sem.at[i]
+        )
+
+        @pl.when(row_y == at_edge)
+        def _():
+            edge_copy.start()
+
+        @pl.when(row_y != at_edge)
+        def _():
+            copies_m[i].start()
+
+    for i, copy in enumerate(copies_m):
+        if i not in (0, 6, 7):
+            copy.start()
 
     low = lax.rem(frame, NY) < 2
     two_a = jnp.where(low, 2, -2)
@@ -238,11 +259,11 @@
         copy.start()
     for copy in copies:
         copy.wait()
-    weight = w_s[...]
-    own = jnp.dot(keep_ref[...], weight, preferred_element_type=F32)
-    own = (row_s[0] * own).astype(BF16)
-    other = jnp.dot(got_ref[...], weight, preferred_element_type=F32)
-    other = (row_s[1] * other).astype(BF16)
+    both = jnp.concatenate([keep_ref[...], got_ref[...]], axis=0)
+    both = jnp.dot(both, w_s[...], preferred_element_type=F32)
+    half = keep_ref.shape[0]
+    own = (row_s[0] * both[:half]).astype(BF16)
+    other = (row_s[1] * both[half:]).astype(BF16)
     own_ref[...] = own
     other_ref[...] = other
     total_ref[...] = (
@@ -272,81 +293,6 @@
     )(where, step_index, step_sizes, keep, got, table, *pieces)
 
 
-def earlier_kernel(where_ref, index_ref, size_ref, one_ref, two_ref, three_ref, own_ref, out_ref):
-    core = where_ref[2]
-    size = jnp.where(core == 0, size_ref[index_ref[where_ref[0]]], 0.0)
-    total = one_ref[...].astype(F32) + two_ref[...].astype(F32) + three_ref[...].astype(F32)
-    out_ref[...] = (total + size * own_ref[...].astype(F32)).astype(BF16)
-
-
-def earlier_sum(where, step_index, step_sizes, one, two, three, own):
-    vmem = pl.BlockSpec(memory_space=pltpu.VMEM)
-    smem = pl.BlockSpec(memory_space=pltpu.SMEM)
-    return pl.pallas_call(
-        earlier_kernel,
-        in_specs=[smem, smem, smem] + [vmem] * 4,
-        out_specs=vmem,
-        out_shape=jax.ShapeDtypeStruct(own.shape, BF16),
-        name="earlier_sum",
-    )(where, step_index, step_sizes, one, two, three, own)
-
-
-def advance_kernel(
-    where_ref,
-    index_ref,
-    size_ref,
-    one_ref,
-    two_ref,
-    three_ref,
-    own_ref,
-    other_ref,
-    before_ref,
-    rest_ref,
-    anchor_ref,
-    velocity_ref,
-    advanced_ref,
-):
-    step, core = where_ref[0], where_ref[2]
-    half = own_ref.shape[0]
-    size_own = size_ref[index_ref[step]]
-    size_other = jnp.where(core == 1, size_ref[index_ref[step + 1 - 2 * core]], 0.0)
-    near = pl.ds(pl.multiple_of(core * half, half), half)
-    far = pl.ds(pl.multiple_of((1 - core) * half, half), half)
-    own = own_ref[...]
-    velocity_ref[near] = own
-    total = one_ref[...].astype(F32) + two_ref[...].astype(F32) + three_ref[...].astype(F32)
-    total = total + size_other * other_ref[...].astype(F32) + size_own * own.astype(F32)
-    advanced_ref[near] = anchor_ref[near] + total
-    rest = rest_ref[...]
-    velocity_ref[far] = rest
-    advanced_ref[far] = (
-        anchor_ref[far] + before_ref[...].astype(F32) + size_own * rest.astype(F32)
-    )
-
-
-def advance(where, step_index, step_sizes, one, two, three, own, other, before, rest, anchor):
-    vmem = pl.BlockSpec(memory_space=pltpu.VMEM)
-    smem = pl.BlockSpec(memory_space=pltpu.SMEM)
-    return pl.pallas_call(
-        advance_kernel,
-        in_specs=[smem, smem, smem] + [vmem] * 8,
-        out_specs=[vmem] * 2,
-        out_shape=[
-            jax.ShapeDtypeStruct(anchor.shape, BF16),
-            jax.ShapeDtypeStruct(anchor.shape, F32),
-        ],
-        name="advance",
-    )(where, step_index, step_sizes, one, two, three, own, other, before, rest, anchor)
-
-
-def placed_y(parts, own):
-    result = jnp.zeros((NZ, NY, 8, parts[0].shape[1]), BF16)
-    for i, part in enumerate(parts):
-        part = part.reshape(NZ, 1, 8, -1)
-        result = lax.dynamic_update_slice_in_dim(result, part, lax.rem(own + i, NY), 1)
-    return result
-
-
 def on_device(
     latents,
     anchor,
@@ -368,12 +314,19 @@
 
     table = jnp.transpose(modulation, (1, 0, 2))
 
+    size_own = step_sizes[step_index[step]]
+    size_other = step_sizes[step_index[step + 1 - 2 * core]]
+
     out_width = output_weight.shape[1]
+    modulated = modulate(where_am_i, step_index, latent, table)
+    input_weight, output_weight, modulated = lax.optimization_barrier(
+        (input_weight, output_weight, modulated)
+    )
+    zp, zm = z_shift(modulated, 1), z_shift(modulated, -1)
+    before = y_step(modulated, 1, False)
+    after = y_step(modulated, -1, False)
+    two_a = y_shift(modulated, 2)
     packed = jnp.concatenate([input_weight, output_weight.reshape(2, -1)], axis=0)
-    modulated = modulate(where_am_i, step_index, latent, table)
-    packed, modulated = lax.optimization_barrier((packed, modulated))
-    zp, zm = z_shift(modulated, 1), z_shift(modulated, -1)
-    two_a = y_shift(modulated, 2)
     columns_z = [[NY * i + j for i in range(NZ)] for j in range(NY)]
     column = lax.all_to_all(
         jnp.broadcast_to(packed[None], (NZ,) + packed.shape),
@@ -381,33 +334,44 @@
         0,
         0,
         axis_index_groups=columns_z,
-    ).reshape(8 * NZ, -1)
-    column, zp, zm, two_a = lax.optimization_barrier((column, zp, zm, two_a))
+    )
+    column, zp, zm, before, after, two_a, size_own, size_other = lax.optimization_barrier(
+        (column, zp, zm, before, after, two_a, size_own, size_other)
+    )
 
     zp2, zm2 = z_shift(zp, 1), z_shift(zm, -1)
-    plane = placed_y([column] + [y_shift(column, -d) for d in range(1, NY)], y)
-    plane, zp2, zm2 = lax.optimization_barrier((plane, zp2, zm2))
+    before_edge = y_step(zp, 1, True)
+    after_edge = y_step(zm, -1, True)
+    rows_y = [[NY * i + j for j in range(NY)] for i in range(NZ)]
+    plane = lax.all_to_all(
+        jnp.broadcast_to(column[None], (NY,) + column.shape),
+        "frame",
+        0,
+        0,
+        axis_index_groups=rows_y,
+    )
+    plane, before_edge, after_edge, zp, zm = lax.optimization_barrier(
+        (plane, before_edge, after_edge, zp, zm)
+    )
+    plane = jnp.transpose(plane, (1, 0, 2, 3))
     in_rows = plane[:, :, :6].reshape(192, -1)
     out_rows = plane[:, :, 6:].reshape(96, out_width)
 
     left, right = x_shift(in_rows, 1), x_shift(in_rows, -1)
-
-    before = y_shift(jnp.where(y == NY - 1, zp, modulated), 1)
-    after = y_shift(jnp.where(y == 0, zm, modulated), -1)
     z4_top = z_shift(zp2[: rows // 2], 2)
-    in_rows, out_rows, left, right, before, after, z4_top, zm2, zp, zm = lax.optimization_barrier(
-        (in_rows, out_rows, left, right, before, after, z4_top, zm2, zp, zm)
-    )
+    z4_bottom = z_shift(zm2[rows // 2 :], -2)
+    two_b = y_shift(jnp.where(y >= 2, zp, zm), 2)
+    in_rows, out_rows, left, right, z4_top, z4_bottom, two_b = lax.optimization_barrier(
+        (in_rows, out_rows, left, right, z4_top, z4_bottom, two_b)
+    )
+
     far_top = x_shift(left[:96], 1)
     far_bottom = x_shift(right[96:], -1)
-    z4_bottom = z_shift(zm2[rows // 2 :], -2)
-    two_b = y_shift(jnp.where(y >= 2, zp, zm), 2)
     near = [core_swap(piece) for piece in (in_rows, left, right)]
     out_rows = jnp.stack([out_rows, core_swap(out_rows)])
-    far_top, far_bottom, z4_bottom, two_b, out_rows = lax.optimization_barrier(
-        (far_top, far_bottom, z4_bottom, two_b, out_rows)
-    )
+    far_top, far_bottom, out_rows = lax.optimization_barrier((far_top, far_bottom, out_rows))
     slabs = [modulated, zp, zm, two_a, zp2, zm2, before, after, two_b, z4_top, z4_bottom]
+    slabs = slabs + [before_edge, after_edge]
     pieces = [in_rows, left, right, far_top, far_bottom]
     pieces = pieces + near + [core_swap(far_top), core_swap(far_bottom)]
 
@@ -422,11 +386,18 @@
     three = x_later(total, 3)
     two = x_later(one, 1)
     rest = core_swap(other)
-    sums = earlier_sum(where_am_i, step_index, step_sizes, one, two, three, own)
-    before = core_swap(sums)
-    velocity, advanced = advance(
-        where_am_i, step_index, step_sizes, one, two, three, own, other, before, rest, anchor
-    )
+    parts = (2, rows // 2, width)
+    near_half = (jnp.arange(2, dtype=jnp.int32) == core)[:, None, None]
+    own32 = own.astype(F32)
+    velocity = jnp.where(near_half, own[None], rest[None]).reshape(rows, width)
+    sums = one.astype(F32) + two.astype(F32) + three.astype(F32)
+    even = jnp.where(core == 0, size_own, 0.0)
+    earlier = core_swap((sums + even * own32).astype(BF16))
+    odd = jnp.where(core == 1, size_other, 0.0)
+    own_part = sums + odd * other.astype(F32) + size_own * own32
+    rest_part = earlier.astype(F32) + size_own * rest.astype(F32)
+    advanced = anchor.reshape(parts) + jnp.where(near_half, own_part[None], rest_part[None])
+    advanced = advanced.reshape(rows, width)
     return (velocity[None], advanced[None])
 
 

time: 186 us -> 209 us (1.12)
  the two profiles are of different devices: /device:TPU:3 before, /device:TPU:79 now
where the time goes in v2:
time: 209 us; the launch traced here: 206 us
  waiting for transfers between devices  78.8 us (38%)
  starting transfers between devices  67.7 us (32%)
  Pallas kernels  35.3 us (17%)
  local copies, waits for them, and re-layouts  11.9 us (6%)
  other arithmetic  7.15 us (3%)
  between operations  5.56 us (3%)
    pallas_call x1, Pallas kernels, attend(): pl.pallas_call(attend_kernel, in_specs=[smem, smem, pl.BlockSpec(memory_s...  27.8 us
    ppermute x2, starting transfers between devices, y_shift(): return lax.ppermute(block, 'frame', pairs)  21.8 us
    ppermute x6, waiting for transfers between devices, z_shift(): return lax.ppermute(block, 'frame', pairs)  20.4 us
    ppermute x3, waiting for transfers between devices, x_later(): return lax.ppermute(block, 'step', pairs)  17.8 us
    ppermute x2, waiting for transfers between devices, y_shift(): return lax.ppermute(block, 'frame', pairs)  13.3 us
    ppermute x7, waiting for transfers between devices, x_shift(): return lax.ppermute(block, 'step', pairs)  10.1 us
    ppermute x6, starting transfers between devices, z_shift(): return lax.ppermute(block, 'frame', pairs)  9.9 us
    all_to_all x1, starting transfers between devices, on_device(): lax.all_to_all(jnp.broadcast_to(packed[None], (NZ,) + packed.shape), 'fra...  8.59 us
  transfers between devices with their start and end apart: 33, of which 13 were waited for; matrix products, arithmetic and copies ran while one was open for 6% of the time, Pallas kernels for 13%

profile of v2, /device:TPU:79, one launch (start us, length us, event | category | flops | bytes accessed | tf_op | source)
XLA Modules:
  0.0 206.5 jit_solution(620946676741652926)
XLA Ops:
  0.7 0.7 pad_add_fusion.where_ref
  1.3 2.9 %modulate.1.refs_0_ = bf16[256,1536]{1,0:T(8,128)(2,1)} custom-call(s32[4]{0:T(128)} %pad_add_fusion.where_ref, s32[8]{0:T(128)} %index_ref.3, bf16[256,1536]{1,0:T(8,128)(2,1)} %bitcast.37, f32[3,50,1536]{2,1,0:T(8,128)} %bitcast.31), custom_call_target="tpu_custom_call" | custom-call | tf_op jit(solution)/shard_map/modulate/pallas_call | solution.py:69
  4.3 1.7 collective-permute-start
  6.0 3.2 %collective-permute-start.2 = (bf16[256,1536]{1,0:T(8,128)(2,1)}, bf16[256,1536]{1,0:T(8,128)(2,1)S(1)}, u32[]{:S(2)}, u32[]{:S(2)}) collective-permute-start(bf16[256,1536]{1,0:T(8,128)(2,1)} %modulate.1.refs_0_), channel_id=1, source_target_pairs={{0,1},{1,2},{2,3},{4,5},{5,6},{6,7},{8,9},{9,10},{10,11},{12,13},{... | collective-permute-start | bytes 2359304 | tf_op jit(solution)/shard_map/ppermute | solution.py:28
  9.2 2.1 %collective-permute-start.3 = (bf16[256,1536]{1,0:T(8,128)(2,1)}, bf16[256,1536]{1,0:T(8,128)(2,1)S(1)}, u32[]{:S(2)}, u32[]{:S(2)}) collective-permute-start(bf16[256,1536]{1,0:T(8,128)(2,1)} %modulate.1.refs_0_), channel_id=1, source_target_pairs={{1,0},{2,1},{3,2},{5,4},{6,5},{7,6},{9,8},{10,9},{11,10},{13,12},{... | collective-permute-start | bytes 2359304 | tf_op jit(solution)/shard_map/ppermute | solution.py:28
  11.3 2.1 %collective-permute-start.4 = (bf16[256,1536]{1,0:T(8,128)(2,1)}, bf16[256,1536]{1,0:T(8,128)(2,1)S(1)}, u32[]{:S(2)}, u32[]{:S(2)}) collective-permute-start(bf16[256,1536]{1,0:T(8,128)(2,1)} %modulate.1.refs_0_), channel_id=1, source_target_pairs={{0,2},{1,3},{2,0},{3,1},{4,6},{5,7},{6,4},{7,5},{8,10},{9,11},{10,... | collective-permute-start | bytes 2359304 | tf_op jit(solution)/shard_map/ppermute | solution.py:22
  13.5 0.7 broadcast_in_dim.80
  14.2 8.6 %all-to-all-start = ((bf16[8,8,2304]{2,1,0:T(8,128)(2,1)}), bf16[8,8,2304]{2,1,0:T(8,128)(2,1)S(1)}, u32[]{:S(2)}, u32[]{:S(2)}) async-start(bf16[8,8,2304]{2,1,0:T(8,128)(2,1)} %broadcast_in_dim.80), calls=%async_computation | async-start | bytes 589824 | tf_op jit(solution)/shard_map/all_to_all | solution.py:331
  22.8 0.6 fusion.5
  26.8 0.6 fusion.4
  27.4 5.9 %all-to-all-done = bf16[8,8,2304]{2,1,0:T(8,128)(2,1)S(1)} async-done(((bf16[8,8,2304]{2,1,0:T(8,128)(2,1)}), bf16[8,8,2304]{2,1,0:T(8,128)(2,1)S(1)}, u32[]{:S(2)}, u32[]{:S(2)}) %all-to-all-start) | async-done | bytes 294944 | tf_op jit(solution)/shard_map/all_to_all | solution.py:331
  33.3 13.3 %collective-permute-done.4.refs_3_ = bf16[256,1536]{1,0:T(8,128)(2,1)S(1)} collective-permute-done((bf16[256,1536]{1,0:T(8,128)(2,1)}, bf16[256,1536]{1,0:T(8,128)(2,1)S(1)}, u32[]{:S(2)}, u32[]{:S(2)}) %collective-permute-start.4) | collective-permute-done | bytes 786464 | tf_op jit(solution)/shard_map/ppermute | solution.py:22
  46.6 1.2 broadcast_in_dim.81
  47.9 3.5 %all-to-all-start.1 = ((bf16[4,8,8,2304]{3,2,1,0:T(8,128)(2,1)}), bf16[4,8,8,2304]{3,2,1,0:T(8,128)(2,1)S(1)}, u32[]{:S(2)}, u32[]{:S(2)}) async-start(bf16[4,8,8,2304]{3,2,1,0:T(8,128)(2,1)} %broadcast_in_dim.81), calls=%async_computation.1 | async-start | bytes 2359296 | tf_op jit(solution)/shard_map/all_to_all | solution.py:346
  51.4 0.7 collective-permute-start.5
  52.1 0.7 collective-permute-start.6
  52.9 3.0 %collective-permute-start.7 = (bf16[256,1536]{1,0:T(8,128)(2,1)}, bf16[256,1536]{1,0:T(8,128)(2,1)}, u32[]{:S(2)}, u32[]{:S(2)}) collective-permute-start(bf16[256,1536]{1,0:T(8,128)(2,1)} %collective-permute-done.refs_1_), channel_id=1, source_target_pairs={{0,4},{1,5},{2,6},{3,7},{4,8},{5,9},{6,10},{7,11},{8,12},{9,13},{1... | collective-permute-start | bytes 2359304 | tf_op jit(solution)/shard_map/ppermute | solution.py:33
  55.9 7.9 %all-to-all-done.1 = bf16[4,8,8,2304]{3,2,1,0:T(8,128)(2,1)S(1)} async-done(((bf16[4,8,8,2304]{3,2,1,0:T(8,128)(2,1)}), bf16[4,8,8,2304]{3,2,1,0:T(8,128)(2,1)S(1)}, u32[]{:S(2)}, u32[]{:S(2)}) %all-to-all-start.1) | async-done | bytes 1179680 | tf_op jit(solution)/shard_map/all_to_all | solution.py:346
  64.0 0.3 reshape.80.refs_13_
  64.3 0.6 collective-permute-start.10
  64.9 2.1 %collective-permute-start.9 = (bf16[192,2304]{1,0:T(8,128)(2,1)S(1)}, bf16[192,2304]{1,0:T(8,128)(2,1)}, u32[]{:S(2)}, u32[]{:S(2)}) collective-permute-start(bf16[192,2304]{1,0:T(8,128)(2,1)S(1)} %reshape.80.refs_13_), channel_id=1, source_target_pairs={{0,64},{32,96},{64,128},{96,160},{128,192},{160,224},{192,0},{224,... | collective-permute-start | bytes 2654216 | tf_op jit(solution)/shard_map/ppermute | solution.py:38
  67.0 1.2 broadcast_select_fusion
  68.3 19.7 %collective-permute-start.13 = (bf16[256,1536]{1,0:T(8,128)(2,1)S(1)}, bf16[256,1536]{1,0:T(8,128)(2,1)}, u32[]{:S(2)}, u32[]{:S(2)}) collective-permute-start(bf16[256,1536]{1,0:T(8,128)(2,1)S(1)} %broadcast_select_fusion), channel_id=1, source_target_pairs={{0,2},{1,3},{2,0},{3,1},{4,6},{5,7},{6,4},{7,5},{8,10},{9,11},{10,... | collective-permute-start | bytes 2359304 | tf_op jit(solution)/shard_map/ppermute | solution.py:22
  88.0 1.0 slice.26
  89.0 5.1 %collective-permute-start.11 = (bf16[128,1536]{1,0:T(8,128)(2,1)S(1)}, bf16[128,1536]{1,0:T(8,128)(2,1)}, u32[]{:S(2)}, u32[]{:S(2)}) collective-permute-start(bf16[128,1536]{1,0:T(8,128)(2,1)S(1)} %slice.26), channel_id=1, source_target_pairs={{0,8},{1,9},{2,10},{3,11},{4,12},{5,13},{6,14},{7,15},{8,16},{9,17... | collective-permute-start | bytes 1179656 | tf_op jit(solution)/shard_map/ppermute | solution.py:33
  94.1 1.8 slice.27
  95.9 0.3 slice.25
  96.2 0.2 copy.12
  96.4 0.2 reshape.81
  96.6 13.3 %collective-permute-done.11.refs_9_ = bf16[128,1536]{1,0:T(8,128)(2,1)} collective-permute-done((bf16[128,1536]{1,0:T(8,128)(2,1)S(1)}, bf16[128,1536]{1,0:T(8,128)(2,1)}, u32[]{:S(2)}, u32[]{:S(2)}) %collective-permute-start.11) | collective-permute-done | bytes 393248 | tf_op jit(solution)/shard_map/ppermute | solution.py:33
  109.9 7.2 %collective-permute-done.12.refs_10_ = bf16[128,1536]{1,0:T(8,128)(2,1)} collective-permute-done((bf16[128,1536]{1,0:T(8,128)(2,1)}, bf16[128,1536]{1,0:T(8,128)(2,1)}, u32[]{:S(2)}, u32[]{:S(2)}) %collective-permute-start.12) | collective-permute-done | bytes 393248 | tf_op jit(solution)/shard_map/ppermute | solution.py:33
  117.1 0.6 collective-permute-start.16
  117.6 1.0 slice.22
  118.8 1.0 slice.23
  119.8 1.7 collective-permute-start.15
  121.5 0.6 collective-permute-start.17
  122.1 0.5 collective-permute-start.19
  122.7 7.9 %collective-permute-done.14.refs_16_ = bf16[96,2304]{1,0:T(8,128)(2,1)S(1)} collective-permute-done((bf16[96,2304]{1,0:T(8,128)(2,1)S(1)}, bf16[96,2304]{1,0:T(8,128)(2,1)S(1)}, u32[]{:S(2)}, u32[]{:S(2)}) %collective-permute-start.14) | collective-permute-done | bytes 442400 | tf_op jit(solution)/shard_map/ppermute | solution.py:38
  130.5 2.2 %collective-permute-done.15.refs_17_ = bf16[96,2304]{1,0:T(8,128)(2,1)S(1)} collective-permute-done((bf16[96,2304]{1,0:T(8,128)(2,1)S(1)}, bf16[96,2304]{1,0:T(8,128)(2,1)S(1)}, u32[]{:S(2)}, u32[]{:S(2)}) %collective-permute-start.15) | collective-permute-done | bytes 442400 | tf_op jit(solution)/shard_map/ppermute | solution.py:38
  132.8 1.1 collective-permute-start.20
  133.9 1.4 collective-permute-done.20.refs_21_
  135.3 0.6 collective-permute-done.21.refs_22_
  135.9 0.8 collective-permute-start.24
  136.8 0.7 collective-permute-start.25
  137.5 0.2 copy-done.12
  137.7 0.7 copy-done.13
  138.4 0.9 copy-done.14
  139.3 27.8 %attend.1 = (bf16[128,768]{1,0:T(8,128)(2,1)}, bf16[128,768]{1,0:T(8,128)(2,1)}) custom-call(s32[4]{0:T(128)} %pad_add_fusion.where_ref, s32[2,64]{1,0:T(2,128)} %mask_ref.1, f32[2,768]{1,0:T(2,128)} %gain_ref.1, bf16[256,1536]{1,0:T(8,128)(2,1)} %modulate.1.refs_0_, bf16[256,1536]{1,0:T(8,128)(2,1)} %collective-permute-done.refs_1_, ...), custom_call_target="tpu_custom_call" | custom-call | flops 16000000000 | bytes 16000000 | tf_op jit(solution)/shard_map/attend/pallas_call | solution.py:212
  167.1 1.2 collective-permute-start.22
  168.4 1.2 collective-permute-done.22.got_ref
  169.6 0.6 copy-done.7
  170.3 4.5 %output.1 = (bf16[128,1536]{1,0:T(8,128)(2,1)}, bf16[128,1536]{1,0:T(8,128)(2,1)}, bf16[128,1536]{1,0:T(8,128)(2,1)}) custom-call(s32[4]{0:T(128)} %pad_add_fusion.where_ref, s32[8]{0:T(128)} %index_ref.3, f32[50]{0:T(128)} %size_ref.1, bf16[128,768]{1,0:T(8,128)(2,1)} %get-tuple-element.56.keep_ref, bf16[128,768]{1,0:T(8,128)(2,1)} %copy-done.7, ...), custom_call_target="tpu_custom_call" | custom-call | tf_op jit(solution)/shard_map/output/pallas_call | solution.py:280
  174.8 1.3 collective-permute-start.27
  176.1 1.3 collective-permute-start.29
  177.4 10.0 %collective-permute-done.27 = bf16[128,1536]{1,0:T(8,128)(2,1)S(1)} collective-permute-done((bf16[128,1536]{1,0:T(8,128)(2,1)}, bf16[128,1536]{1,0:T(8,128)(2,1)S(1)}, u32[]{:S(2)}, u32[]{:S(2)}) %collective-permute-start.27) | collective-permute-done | bytes 393248 | tf_op jit(solution)/shard_map/ppermute | solution.py:43
  187.4 1.3 collective-permute-start.28
  189.9 1.2 collective-permute-start.26
  191.1 7.7 %collective-permute-done.28 = bf16[128,1536]{1,0:T(8,128)(2,1)S(1)} collective-permute-done((bf16[128,1536]{1,0:T(8,128)(2,1)S(1)}, bf16[128,1536]{1,0:T(8,128)(2,1)S(1)}, u32[]{:S(2)}, u32[]{:S(2)}) %collective-permute-start.28) | collective-permute-done | bytes 393248 | tf_op jit(solution)/shard_map/ppermute | solution.py:43
  198.8 2.1 %fusion.1 = (f32[128,1536]{1,0:T(8,128)S(1)}, bf16[128,1536]{1,0:T(8,128)(2,1)S(1)}) fusion(bf16[128,1536]{1,0:T(8,128)(2,1)} %get-tuple-element.59, bf16[128,1536]{1,0:T(8,128)(2,1)} %get-tuple-element.60, bf16[128,1536]{1,0:T(8,128)(2,1)S(1)} %collective-permute-done.29, bf16[128,1536]{1,0:T(8,128)(2,1)S(1)} %collective-permute-done.28, ...), kind=kLoop, calls=%fused_computation.4 | loop fusion | flops 2752512 | bytes 3145740 | tf_op jit(solution)/shard_map/add | solution.py:397
  200.9 2.1 %collective-permute-start.30 = (bf16[128,1536]{1,0:T(8,128)(2,1)S(1)}, bf16[128,1536]{1,0:T(8,128)(2,1)S(1)}, u32[]{:S(2)}, u32[]{:S(2)}) collective-permute-start(bf16[128,1536]{1,0:T(8,128)(2,1)S(1)} %get-tuple-element.65), channel_id=1, source_target_pairs={{0,32},{32,0},{64,96},{96,64},{128,160},{160,128},{192,224},{224,1... | collective-permute-start | bytes 1179656 | tf_op jit(solution)/shard_map/ppermute | solution.py:47
  203.2 1.0 bitcast_select_fusion.1
  204.2 0.2 collective-permute-done.30
  204.4 0.7 multiply_add_fusion
  205.0 1.4 fusion
  (79 shorter events, 0.8 us)
Async XLA Ops:
  0.6 12.8 %copy-start.8 = (bf16[6,2304]{1,0:T(8,128)(2,1)S(1)}, bf16[6,2304]{1,0:T(8,128)(2,1)}, u32[]{:S(2)}) copy-start(bf16[6,2304]{1,0:T(8,128)(2,1)} %param.14) | copy-start | bytes 82948
  0.6 12.8 %copy-start.9 = (bf16[3,1536]{1,0:T(4,128)(2,1)S(1)}, bf16[3,1536]{1,0:T(4,128)(2,1)}, u32[]{:S(2)}) copy-start(bf16[3,1536]{1,0:T(4,128)(2,1)} %param.15) | copy-start | bytes 27652
  1.3 21.5 %copy-start.10 = (s32[8]{0:T(128)S(1)}, s32[8]{0:T(128)}, u32[]{:S(2)}) copy-start(s32[8]{0:T(128)} %index_ref.3) | copy-start | bytes 100
  1.3 25.4 %copy-start.11 = (f32[50]{0:T(128)S(1)}, f32[50]{0:T(128)}, u32[]{:S(2)}) copy-start(f32[50]{0:T(128)} %size_ref.1) | copy-start | bytes 604
  4.3 29.0 %collective-permute-start = (bf16[256,1536]{1,0:T(8,128)(2,1)}, bf16[256,1536]{1,0:T(8,128)(2,1)}, u32[]{:S(2)}, u32[]{:S(2)}) collective-permute-start(bf16[256,1536]{1,0:T(8,128)(2,1)} %modulate.1.refs_0_), channel_id=1, source_target_pairs={{0,4},{1,5},{2,6},{3,7},{4,8},{5,9},{6,10},{7,11},{8,12},{9,13},{1... | collective-permute-start | bytes 2359304 | tf_op jit(solution)/shard_map/ppermute | solution.py:33
  6.0 27.3 %collective-permute-start.1 = (bf16[256,1536]{1,0:T(8,128)(2,1)}, bf16[256,1536]{1,0:T(8,128)(2,1)}, u32[]{:S(2)}, u32[]{:S(2)}) collective-permute-start(bf16[256,1536]{1,0:T(8,128)(2,1)} %modulate.1.refs_0_), channel_id=1, source_target_pairs={{0,28},{1,29},{2,30},{3,31},{4,0},{5,1},{6,2},{7,3},{8,4},{9,5},{1... | collective-permute-start | bytes 2359304 | tf_op jit(solution)/shard_map/ppermute | solution.py:33
  6.0 27.3 %collective-permute-start.2 = (bf16[256,1536]{1,0:T(8,128)(2,1)}, bf16[256,1536]{1,0:T(8,128)(2,1)S(1)}, u32[]{:S(2)}, u32[]{:S(2)}) collective-permute-start(bf16[256,1536]{1,0:T(8,128)(2,1)} %modulate.1.refs_0_), channel_id=1, source_target_pairs={{0,1},{1,2},{2,3},{4,5},{5,6},{6,7},{8,9},{9,10},{10,11},{12,13},{... | collective-permute-start | bytes 2359304 | tf_op jit(solution)/shard_map/ppermute | solution.py:28
  9.2 24.1 %collective-permute-start.3 = (bf16[256,1536]{1,0:T(8,128)(2,1)}, bf16[256,1536]{1,0:T(8,128)(2,1)S(1)}, u32[]{:S(2)}, u32[]{:S(2)}) collective-permute-start(bf16[256,1536]{1,0:T(8,128)(2,1)} %modulate.1.refs_0_), channel_id=1, source_target_pairs={{1,0},{2,1},{3,2},{5,4},{6,5},{7,6},{9,8},{10,9},{11,10},{13,12},{... | collective-permute-start | bytes 2359304 | tf_op jit(solution)/shard_map/ppermute | solution.py:28
  11.3 35.2 %collective-permute-start.4 = (bf16[256,1536]{1,0:T(8,128)(2,1)}, bf16[256,1536]{1,0:T(8,128)(2,1)S(1)}, u32[]{:S(2)}, u32[]{:S(2)}) collective-permute-start(bf16[256,1536]{1,0:T(8,128)(2,1)} %modulate.1.refs_0_), channel_id=1, source_target_pairs={{0,2},{1,3},{2,0},{3,1},{4,6},{5,7},{6,4},{7,5},{8,10},{9,11},{10,... | collective-permute-start | bytes 2359304 | tf_op jit(solution)/shard_map/ppermute | solution.py:22
  14.2 19.0 %all-to-all-start = ((bf16[8,8,2304]{2,1,0:T(8,128)(2,1)}), bf16[8,8,2304]{2,1,0:T(8,128)(2,1)S(1)}, u32[]{:S(2)}, u32[]{:S(2)}) async-start(bf16[8,8,2304]{2,1,0:T(8,128)(2,1)} %broadcast_in_dim.80), calls=%async_computation | async-start | bytes 589824 | tf_op jit(solution)/shard_map/all_to_all | solution.py:331
  33.3 14.5 %copy-start.15 = (bf16[256,1536]{1,0:T(8,128)(2,1)}, bf16[256,1536]{1,0:T(8,128)(2,1)S(1)}, u32[]{:S(2)}) copy-start(bf16[256,1536]{1,0:T(8,128)(2,1)S(1)} %collective-permute-done.2.refs_6_) | copy-start | bytes 2359300
  33.3 14.4 %copy-start.16 = (bf16[256,1536]{1,0:T(8,128)(2,1)}, bf16[256,1536]{1,0:T(8,128)(2,1)S(1)}, u32[]{:S(2)}) copy-start(bf16[256,1536]{1,0:T(8,128)(2,1)S(1)} %collective-permute-done.3.refs_7_) | copy-start | bytes 2359300
  46.6 1.3 copy-start.17
  47.9 16.0 %all-to-all-start.1 = ((bf16[4,8,8,2304]{3,2,1,0:T(8,128)(2,1)}), bf16[4,8,8,2304]{3,2,1,0:T(8,128)(2,1)S(1)}, u32[]{:S(2)}, u32[]{:S(2)}) async-start(bf16[4,8,8,2304]{3,2,1,0:T(8,128)(2,1)} %broadcast_in_dim.81), calls=%async_computation.1 | async-start | bytes 2359296 | tf_op jit(solution)/shard_map/all_to_all | solution.py:346
  51.4 4.5 %collective-permute-start.5 = (bf16[256,1536]{1,0:T(8,128)(2,1)}, bf16[256,1536]{1,0:T(8,128)(2,1)S(1)}, u32[]{:S(2)}, u32[]{:S(2)}) collective-permute-start(bf16[256,1536]{1,0:T(8,128)(2,1)} %collective-permute-done.refs_1_), channel_id=1, source_target_pairs={{3,0},{7,4},{11,8},{15,12},{19,16},{23,20},{27,24},{31,28},{35,32}... | collective-permute-start | bytes 2359304 | tf_op jit(solution)/shard_map/ppermute | solution.py:28
  52.1 3.8 %collective-permute-start.6 = (bf16[256,1536]{1,0:T(8,128)(2,1)}, bf16[256,1536]{1,0:T(8,128)(2,1)S(1)}, u32[]{:S(2)}, u32[]{:S(2)}) collective-permute-start(bf16[256,1536]{1,0:T(8,128)(2,1)} %collective-permute-done.1.refs_2_), channel_id=1, source_target_pairs={{0,3},{4,7},{8,11},{12,15},{16,19},{20,23},{24,27},{28,31},{32,35}... | collective-permute-start | bytes 2359304 | tf_op jit(solution)/shard_map/ppermute | solution.py:28
  52.9 35.1 %collective-permute-start.7 = (bf16[256,1536]{1,0:T(8,128)(2,1)}, bf16[256,1536]{1,0:T(8,128)(2,1)}, u32[]{:S(2)}, u32[]{:S(2)}) collective-permute-start(bf16[256,1536]{1,0:T(8,128)(2,1)} %collective-permute-done.refs_1_), channel_id=1, source_target_pairs={{0,4},{1,5},{2,6},{3,7},{4,8},{5,9},{6,10},{7,11},{8,12},{9,13},{1... | collective-permute-start | bytes 2359304 | tf_op jit(solution)/shard_map/ppermute | solution.py:33
  55.9 38.2 %collective-permute-start.8 = (bf16[256,1536]{1,0:T(8,128)(2,1)}, bf16[256,1536]{1,0:T(8,128)(2,1)}, u32[]{:S(2)}, u32[]{:S(2)}) collective-permute-start(bf16[256,1536]{1,0:T(8,128)(2,1)} %collective-permute-done.1.refs_2_), channel_id=1, source_target_pairs={{0,28},{1,29},{2,30},{3,31},{4,0},{5,1},{6,2},{7,3},{8,4},{9,5},{1... | collective-permute-start | bytes 2359304 | tf_op jit(solution)/shard_map/ppermute | solution.py:33
  55.9 8.0 %copy-start.18 = (bf16[256,1536]{1,0:T(8,128)(2,1)}, bf16[256,1536]{1,0:T(8,128)(2,1)S(1)}, u32[]{:S(2)}) copy-start(bf16[256,1536]{1,0:T(8,128)(2,1)S(1)} %collective-permute-done.5.refs_11_) | copy-start | bytes 2359300
  55.9 8.0 %copy-start.19 = (bf16[256,1536]{1,0:T(8,128)(2,1)}, bf16[256,1536]{1,0:T(8,128)(2,1)S(1)}, u32[]{:S(2)}) copy-start(bf16[256,1536]{1,0:T(8,128)(2,1)S(1)} %collective-permute-done.6.refs_12_) | copy-start | bytes 2359300
  64.3 57.3 %copy-start.3 = (bf16[192,2304]{1,0:T(8,128)(2,1)}, bf16[192,2304]{1,0:T(8,128)(2,1)S(1)}, u32[]{:S(2)}) copy-start(bf16[192,2304]{1,0:T(8,128)(2,1)S(1)} %reshape.80.refs_13_) | copy-start | bytes 2654212
  64.3 52.8 %collective-permute-start.10 = (bf16[192,2304]{1,0:T(8,128)(2,1)S(1)}, bf16[192,2304]{1,0:T(8,128)(2,1)}, u32[]{:S(2)}, u32[]{:S(2)}) collective-permute-start(bf16[192,2304]{1,0:T(8,128)(2,1)S(1)} %reshape.80.refs_13_), channel_id=1, source_target_pairs={{0,192},{32,224},{64,0},{96,32},{128,64},{160,96},{192,128},{224,1... | collective-permute-start | bytes 2654216 | tf_op jit(solution)/shard_map/ppermute | solution.py:38
  64.9 52.1 %collective-permute-start.9 = (bf16[192,2304]{1,0:T(8,128)(2,1)S(1)}, bf16[192,2304]{1,0:T(8,128)(2,1)}, u32[]{:S(2)}, u32[]{:S(2)}) collective-permute-start(bf16[192,2304]{1,0:T(8,128)(2,1)S(1)} %reshape.80.refs_13_), channel_id=1, source_target_pairs={{0,64},{32,96},{64,128},{96,160},{128,192},{160,224},{192,0},{224,... | collective-permute-start | bytes 2654216 | tf_op jit(solution)/shard_map/ppermute | solution.py:38
  68.3 48.8 %collective-permute-start.13 = (bf16[256,1536]{1,0:T(8,128)(2,1)S(1)}, bf16[256,1536]{1,0:T(8,128)(2,1)}, u32[]{:S(2)}, u32[]{:S(2)}) collective-permute-start(bf16[256,1536]{1,0:T(8,128)(2,1)S(1)} %broadcast_select_fusion), channel_id=1, source_target_pairs={{0,2},{1,3},{2,0},{3,1},{4,6},{5,7},{6,4},{7,5},{8,10},{9,11},{10,... | collective-permute-start | bytes 2359304 | tf_op jit(solution)/shard_map/ppermute | solution.py:22
  89.0 20.9 %collective-permute-start.11 = (bf16[128,1536]{1,0:T(8,128)(2,1)S(1)}, bf16[128,1536]{1,0:T(8,128)(2,1)}, u32[]{:S(2)}, u32[]{:S(2)}) collective-permute-start(bf16[128,1536]{1,0:T(8,128)(2,1)S(1)} %slice.26), channel_id=1, source_target_pairs={{0,8},{1,9},{2,10},{3,11},{4,12},{5,13},{6,14},{7,15},{8,16},{9,17... | collective-permute-start | bytes 1179656 | tf_op jit(solution)/shard_map/ppermute | solution.py:33
  95.9 21.1 %collective-permute-start.12 = (bf16[128,1536]{1,0:T(8,128)(2,1)}, bf16[128,1536]{1,0:T(8,128)(2,1)}, u32[]{:S(2)}, u32[]{:S(2)}) collective-permute-start(bf16[128,1536]{1,0:T(8,128)(2,1)} %slice.27), channel_id=1, source_target_pairs={{0,24},{1,25},{2,26},{3,27},{4,28},{5,29},{6,30},{7,31},{8,0},{9,1... | collective-permute-start | bytes 1179656 | tf_op jit(solution)/shard_map/ppermute | solution.py:33
  117.1 5.1 %collective-permute-start.16 = (bf16[96,1536]{1,0:T(8,128)(2,1)S(1)}, bf16[96,1536]{1,0:T(8,128)(2,1)S(1)}, u32[]{:S(2)}, u32[]{:S(2)}) collective-permute-start(bf16[96,1536]{1,0:T(8,128)(2,1)S(1)} %reshape.81), channel_id=1, source_target_pairs={{0,32},{32,0},{64,96},{96,64},{128,160},{160,128},{192,224},{224,1... | collective-permute-start | bytes 884744 | tf_op jit(solution)/shard_map/ppermute | solution.py:47
  118.7 11.9 %collective-permute-start.14 = (bf16[96,2304]{1,0:T(8,128)(2,1)S(1)}, bf16[96,2304]{1,0:T(8,128)(2,1)S(1)}, u32[]{:S(2)}, u32[]{:S(2)}) collective-permute-start(bf16[96,2304]{1,0:T(8,128)(2,1)S(1)} %slice.22), channel_id=1, source_target_pairs={{0,64},{32,96},{64,128},{96,160},{128,192},{160,224},{192,0},{224,... | collective-permute-start | bytes 1327112 | tf_op jit(solution)/shard_map/ppermute | solution.py:38
  119.8 12.9 %collective-permute-start.15 = (bf16[96,2304]{1,0:T(8,128)(2,1)S(1)}, bf16[96,2304]{1,0:T(8,128)(2,1)S(1)}, u32[]{:S(2)}, u32[]{:S(2)}) collective-permute-start(bf16[96,2304]{1,0:T(8,128)(2,1)S(1)} %slice.23), channel_id=1, source_target_pairs={{0,192},{32,224},{64,0},{96,32},{128,64},{160,96},{192,128},{224,1... | collective-permute-start | bytes 1327112 | tf_op jit(solution)/shard_map/ppermute | solution.py:38
  121.5 15.2 %collective-permute-start.17 = (bf16[192,2304]{1,0:T(8,128)(2,1)S(1)}, bf16[192,2304]{1,0:T(8,128)(2,1)S(1)}, u32[]{:S(2)}, u32[]{:S(2)}) collective-permute-start(bf16[192,2304]{1,0:T(8,128)(2,1)S(1)} %reshape.80.refs_13_), channel_id=1, source_target_pairs={{0,32},{32,0},{64,96},{96,64},{128,160},{160,128},{192,224},{224,1... | collective-permute-start | bytes 2654216 | tf_op jit(solution)/shard_map/ppermute | solution.py:47
  122.1 15.3 %collective-permute-start.18 = (bf16[192,2304]{1,0:T(8,128)(2,1)}, bf16[192,2304]{1,0:T(8,128)(2,1)S(1)}, u32[]{:S(2)}, u32[]{:S(2)}) collective-permute-start(bf16[192,2304]{1,0:T(8,128)(2,1)} %collective-permute-done.9.refs_14_), channel_id=1, source_target_pairs={{0,32},{32,0},{64,96},{96,64},{128,160},{160,128},{192,224},{224,1... | collective-permute-start | bytes 2654216 | tf_op jit(solution)/shard_map/ppermute | solution.py:47
  122.1 15.3 %collective-permute-start.19 = (bf16[192,2304]{1,0:T(8,128)(2,1)}, bf16[192,2304]{1,0:T(8,128)(2,1)S(1)}, u32[]{:S(2)}, u32[]{:S(2)}) collective-permute-start(bf16[192,2304]{1,0:T(8,128)(2,1)} %collective-permute-done.10.refs_15_), channel_id=1, source_target_pairs={{0,32},{32,0},{64,96},{96,64},{128,160},{160,128},{192,224},{224,1... | collective-permute-start | bytes 2654216 | tf_op jit(solution)/shard_map/ppermute | solution.py:47
  122.7 44.4 %copy-start = (bf16[2,96,1536]{2,1,0:T(8,128)(2,1)}, bf16[2,96,1536]{2,1,0:T(8,128)(2,1)S(1)}, u32[]{:S(2)}) copy-start(bf16[2,96,1536]{2,1,0:T(8,128)(2,1)S(1)} %pad_maximum_fusion.refs_0_) | copy-start | bytes 1769476
  130.5 6.9 %copy-start.20 = (bf16[96,2304]{1,0:T(8,128)(2,1)}, bf16[96,2304]{1,0:T(8,128)(2,1)S(1)}, u32[]{:S(2)}) copy-start(bf16[96,2304]{1,0:T(8,128)(2,1)S(1)} %collective-permute-done.14.refs_16_) | copy-start | bytes 1327108
  132.8 4.7 %copy-start.21 = (bf16[96,2304]{1,0:T(8,128)(2,1)}, bf16[96,2304]{1,0:T(8,128)(2,1)S(1)}, u32[]{:S(2)}) copy-start(bf16[96,2304]{1,0:T(8,128)(2,1)S(1)} %collective-permute-done.15.refs_17_) | copy-start | bytes 1327108
  132.8 2.5 %collective-permute-start.20 = (bf16[96,2304]{1,0:T(8,128)(2,1)S(1)}, bf16[96,2304]{1,0:T(8,128)(2,1)S(1)}, u32[]{:S(2)}, u32[]{:S(2)}) collective-permute-start(bf16[96,2304]{1,0:T(8,128)(2,1)S(1)} %collective-permute-done.14.refs_16_), channel_id=1, source_target_pairs={{0,32},{32,0},{64,96},{96,64},{128,160},{160,128},{192,224},{224,1... | collective-permute-start | bytes 1327112 | tf_op jit(solution)/shard_map/ppermute | solution.py:47
  133.9 2.1 collective-permute-start.21
  135.3 2.2 %copy-start.22 = (bf16[96,2304]{1,0:T(8,128)(2,1)}, bf16[96,2304]{1,0:T(8,128)(2,1)S(1)}, u32[]{:S(2)}) copy-start(bf16[96,2304]{1,0:T(8,128)(2,1)S(1)} %collective-permute-done.20.refs_21_) | copy-start | bytes 1327108
  135.3 33.0 %collective-permute-start.23 = (bf16[2,96,1536]{2,1,0:T(8,128)(2,1)S(1)}, bf16[2,96,1536]{2,1,0:T(8,128)(2,1)S(1)}, u32[]{:S(2)}, u32[]{:S(2)}) collective-permute-start(bf16[2,96,1536]{2,1,0:T(8,128)(2,1)S(1)} %pad_maximum_fusion.refs_0_), channel_id=1, source_target_pairs={{0,64},{32,96},{64,128},{96,160},{128,192},{160,224},{192,0},{224,... | collective-permute-start | bytes 1769480 | tf_op jit(solution)/shard_map/ppermute | solution.py:38
  135.9 1.6 copy-start.23
  135.9 32.4 %collective-permute-start.24 = (bf16[2,96,1536]{2,1,0:T(8,128)(2,1)S(1)}, bf16[2,96,1536]{2,1,0:T(8,128)(2,1)S(1)}, u32[]{:S(2)}, u32[]{:S(2)}) collective-permute-start(bf16[2,96,1536]{2,1,0:T(8,128)(2,1)S(1)} %pad_maximum_fusion.refs_0_), channel_id=1, source_target_pairs={{0,192},{32,224},{64,0},{96,32},{128,64},{160,96},{192,128},{224,1... | collective-permute-start | bytes 1769480 | tf_op jit(solution)/shard_map/ppermute | solution.py:38
  136.8 0.9 copy-start.12
  136.8 31.6 %collective-permute-start.25 = (bf16[2,96,1536]{2,1,0:T(8,128)(2,1)S(1)}, bf16[2,96,1536]{2,1,0:T(8,128)(2,1)S(1)}, u32[]{:S(2)}, u32[]{:S(2)}) collective-permute-start(bf16[2,96,1536]{2,1,0:T(8,128)(2,1)S(1)} %pad_maximum_fusion.refs_0_), channel_id=1, source_target_pairs={{0,128},{32,160},{64,192},{96,224},{128,0},{160,32},{192,64},{224,... | collective-permute-start | bytes 1769480 | tf_op jit(solution)/shard_map/ppermute | solution.py:38
  137.4 0.9 copy-start.13
  138.4 0.9 copy-start.14
  167.1 2.5 %collective-permute-start.22 = (bf16[128,768]{1,0:T(8,128)(2,1)}, bf16[128,768]{1,0:T(8,128)(2,1)S(1)}, u32[]{:S(2)}, u32[]{:S(2)}) collective-permute-start(bf16[128,768]{1,0:T(8,128)(2,1)} %get-tuple-element.57), channel_id=1, source_target_pairs={{0,32},{32,0},{64,96},{96,64},{128,160},{160,128},{192,224},{224,1... | collective-permute-start | bytes 589832 | tf_op jit(solution)/shard_map/ppermute | solution.py:47
  168.3 1.3 copy-start.4
  168.3 1.3 copy-start.5
  168.4 1.3 copy-start.6
  169.6 0.7 copy-start.7
  174.8 12.6 %collective-permute-start.27 = (bf16[128,1536]{1,0:T(8,128)(2,1)}, bf16[128,1536]{1,0:T(8,128)(2,1)S(1)}, u32[]{:S(2)}, u32[]{:S(2)}) collective-permute-start(bf16[128,1536]{1,0:T(8,128)(2,1)} %get-tuple-element.61), channel_id=1, source_target_pairs={{0,64},{32,96},{64,128},{96,160},{128,192},{160,224},{1,65},{33,97... | collective-permute-start | bytes 1179656 | tf_op jit(solution)/shard_map/ppermute | solution.py:43
  176.1 15.0 %collective-permute-start.29 = (bf16[128,1536]{1,0:T(8,128)(2,1)}, bf16[128,1536]{1,0:T(8,128)(2,1)S(1)}, u32[]{:S(2)}, u32[]{:S(2)}) collective-permute-start(bf16[128,1536]{1,0:T(8,128)(2,1)} %get-tuple-element.61), channel_id=1, source_target_pairs={{0,192},{32,224},{1,193},{33,225},{2,194},{34,226},{3,195},{35,227... | collective-permute-start | bytes 1179656 | tf_op jit(solution)/shard_map/ppermute | solution.py:43
  187.4 11.4 %collective-permute-start.28 = (bf16[128,1536]{1,0:T(8,128)(2,1)S(1)}, bf16[128,1536]{1,0:T(8,128)(2,1)S(1)}, u32[]{:S(2)}, u32[]{:S(2)}) collective-permute-start(bf16[128,1536]{1,0:T(8,128)(2,1)S(1)} %collective-permute-done.27), channel_id=1, source_target_pairs={{0,64},{32,96},{64,128},{96,160},{128,192},{160,224},{1,65},{33,97... | collective-permute-start | bytes 1179656 | tf_op jit(solution)/shard_map/ppermute | solution.py:43
  189.9 13.1 %collective-permute-start.26 = (bf16[128,1536]{1,0:T(8,128)(2,1)}, bf16[128,1536]{1,0:T(8,128)(2,1)S(1)}, u32[]{:S(2)}, u32[]{:S(2)}) collective-permute-start(bf16[128,1536]{1,0:T(8,128)(2,1)} %get-tuple-element.60), channel_id=1, source_target_pairs={{0,32},{32,0},{64,96},{96,64},{128,160},{160,128},{192,224},{224,1... | collective-permute-start | bytes 1179656 | tf_op jit(solution)/shard_map/ppermute | solution.py:47
  198.8 4.2 %copy-start.2 = (bf16[128,1536]{1,0:T(8,128)(2,1)S(1)}, bf16[128,1536]{1,0:T(8,128)(2,1)}, u32[]{:S(2)}) copy-start(bf16[128,1536]{1,0:T(8,128)(2,1)} %get-tuple-element.59) | copy-start | bytes 1179652
  200.9 3.5 %collective-permute-start.30 = (bf16[128,1536]{1,0:T(8,128)(2,1)S(1)}, bf16[128,1536]{1,0:T(8,128)(2,1)S(1)}, u32[]{:S(2)}, u32[]{:S(2)}) collective-permute-start(bf16[128,1536]{1,0:T(8,128)(2,1)S(1)} %get-tuple-element.65), channel_id=1, source_target_pairs={{0,32},{32,0},{64,96},{96,64},{128,160},{160,128},{192,224},{224,1... | collective-permute-start | bytes 1179656 | tf_op jit(solution)/shard_map/ppermute | solution.py:47
  203.1 1.9 copy-start.1

commit v3 on v1

--- a/solution.py
+++ b/solution.py
@@ -269,80 +269,6 @@
     )(where, step_index, step_sizes, keep, got, table, *pieces)
 
 
-def base_kernel(
-    where_ref,
-    index_ref,
-    size_ref,
-    own_ref,
-    other_ref,
-    rest_ref,
-    anchor_ref,
-    velocity_ref,
-    base_ref,
-):
-    step, core = where_ref[0], where_ref[2]
-    near = pl.program_id(0) == core
-    size_own = size_ref[index_ref[step]]
-    size_other = jnp.where(
-        jnp.logical_and(near, core == 1), size_ref[index_ref[step + 1 - 2 * core]], 0.0
-    )
-    value = jnp.where(near, own_ref[...].astype(F32), rest_ref[...].astype(F32))
-    velocity_ref[...] = value.astype(BF16)
-    base_ref[...] = (
-        anchor_ref[...] + size_other * other_ref[...].astype(F32) + size_own * value
-    )
-
-
-def base(where, step_index, step_sizes, own, other, rest, anchor):
-    half, width = own.shape
-    smem = pl.BlockSpec(memory_space=pltpu.SMEM)
-    part = pl.BlockSpec((half // 2, width), lambda i, j: (j, 0))
-    whole = pl.BlockSpec((half // 2, width), lambda i, j: (2 * i + j, 0))
-    return pl.pallas_call(
-        base_kernel,
-        grid=(2, 2),
-        in_specs=[smem, smem, smem, part, part, part, whole],
-        out_specs=[whole, whole],
-        out_shape=[
-            jax.ShapeDtypeStruct(anchor.shape, BF16),
-            jax.ShapeDtypeStruct(anchor.shape, F32),
-        ],
-        cost_estimate=pl.CostEstimate(
-            flops=3_000_000, bytes_accessed=6_000_000, transcendentals=0
-        ),
-        name="base",
-    )(where, step_index, step_sizes, own, other, rest, anchor)
-
-
-def add_kernel(where_ref, *refs):
-    value = refs[0][...]
-    for part_ref in refs[1:-1]:
-        value = value + part_ref[...].astype(F32)
-    refs[-1][...] = value
-
-
-def add_half(where, near, value, parts, name):
-    half, width = parts[0].shape
-
-    def place(i, where):
-        core = where[2] if near else 1 - where[2]
-        return (2 * core + i, 0)
-
-    return pl.pallas_call(
-        add_kernel,
-        grid_spec=pltpu.PrefetchScalarGridSpec(
-            num_scalar_prefetch=1,
-            grid=(2,),
-            in_specs=[pl.BlockSpec((half // 2, width), place)]
-            + [pl.BlockSpec((half // 2, width), lambda i, where: (i, 0))] * len(parts),
-            out_specs=pl.BlockSpec((half // 2, width), place),
-        ),
-        out_shape=jax.ShapeDtypeStruct(value.shape, F32),
-        input_output_aliases={1: 0},
-        name=name,
-    )(where, value, *parts)
-
-
 def placed_y(parts, own):
     result = jnp.zeros((NZ, NY, 8, parts[0].shape[1]), BF16)
     for i, part in enumerate(parts):
@@ -373,9 +299,14 @@
     table = jnp.transpose(modulation, (1, 0, 2))
 
     size_own = step_sizes[step_index[step]]
-    size_even = jnp.where(core == 0, size_own, 0.0)
+    size_other = step_sizes[step_index[step + 1 - 2 * core]]
 
     out_width = output_weight.shape[1]
+    modulated = modulate(where_am_i, step_index, latent, table)
+    input_weight, output_weight, modulated = lax.optimization_barrier(
+        (input_weight, output_weight, modulated)
+    )
+    two_a = y_shift(modulated, 2)
     packed = jnp.concatenate([input_weight, output_weight.reshape(2, -1)], axis=0)
     columns_z = [[NY * i + j for i in range(NZ)] for j in range(NY)]
     column = lax.all_to_all(
@@ -385,13 +316,12 @@
         0,
         axis_index_groups=columns_z,
     ).reshape(8 * NZ, -1)
-    modulated = modulate(where_am_i, step_index, latent, table)
-    two_a = y_shift(modulated, 2)
-    column, modulated, size_even = lax.optimization_barrier((column, modulated, size_even))
+    column, modulated, two_a, size_own, size_other = lax.optimization_barrier(
+        (column, modulated, two_a, size_own, size_other)
+    )
 
     zp, zm = z_shift(modulated, 1), z_shift(modulated, -1)
-    later, two_a = lax.optimization_barrier((column, two_a))
-    plane = placed_y([column, y_shift(column, -1), y_shift(later, 2), y_shift(column, 1)], y)
+    plane = placed_y([column] + [y_shift(column, -d) for d in range(1, NY)], y)
     plane, zp, zm = lax.optimization_barrier((plane, zp, zm))
     in_rows = plane[:, :, :6].reshape(192, -1)
     out_rows = plane[:, :, 6:].reshape(96, out_width)
@@ -427,12 +357,21 @@
     three = x_later(total, 3)
     two = x_later(one, 1)
     rest = core_swap(other)
-    velocity, advanced = base(where_am_i, step_index, step_sizes, own, other, rest, anchor)
-    two, velocity, advanced = lax.optimization_barrier((two, velocity, advanced))
-    sums = one.astype(F32) + two.astype(F32) + three.astype(F32) + size_even * own.astype(F32)
-    earlier = core_swap(sums.astype(BF16))
-    advanced = add_half(where_am_i, True, advanced, [one, two, three], "add_near")
-    advanced = add_half(where_am_i, False, advanced, [earlier], "add_far")
+    parts = (2, rows // 2, width)
+    near_half = (jnp.arange(2, dtype=jnp.int32) == core)[:, None, None]
+    own32 = own.astype(F32)
+    velocity = jnp.where(near_half, own[None], rest[None]).reshape(rows, width)
+    two, velocity = lax.optimization_barrier((two, velocity))
+    even = jnp.where(core == 0, size_own, 0.0)
+    odd = jnp.where(core == 1, size_other, 0.0)
+    sums = one.astype(F32) + two.astype(F32) + three.astype(F32)
+    earlier = core_swap((sums + even * own32).astype(BF16))
+    one, two, three, own = lax.optimization_barrier((one, two, three, own))
+    sums = one.astype(F32) + two.astype(F32) + three.astype(F32)
+    own_part = sums + odd * other.astype(F32) + size_own * own.astype(F32)
+    rest_part = earlier.astype(F32) + size_own * rest.astype(F32)
+    advanced = anchor.reshape(parts) + jnp.where(near_half, own_part[None], rest_part[None])
+    advanced = advanced.reshape(rows, width)
     return (velocity[None], advanced[None])
 
 

time: 184 us -> 181 us (0.984)
  Pallas kernels: 45.3 us -> 35.3 us
  other arithmetic: 3.09 us -> 7.27 us
  starting transfers between devices: 42.5 us -> 45.2 us
  between operations: 3.56 us -> 5.97 us
  local copies, waits for them, and re-layouts: 10 us -> 8.04 us
    ppermute x7, waiting for transfers between devices: 36.3 us -> 23.9 us  [y_shift(): return lax.ppermute(block, 'frame', pairs)]
    pallas_call x3 -> x0, Pallas kernels: 10.1 us -> none  [the longest x2 5.74 us: add_half(): pl.pallas_call(add_kernel, grid_spec=pltpu.PrefetchScalarGridSpec(num_sca...]
    ppermute x6, waiting for transfers between devices: 21.9 us -> 29.7 us  [z_shift(): return lax.ppermute(block, 'frame', pairs)]
    add x0 -> x3, other arithmetic: none -> 2.94 us  [the longest x1 1.42 us: on_device(): anchor.reshape(parts)]
    all_to_all x1, waiting for transfers between devices: 0.01 us -> 2.76 us  [on_device(): lax.all_to_all(jnp.broadcast_to(packed[None], (NZ,) + packed.shape), 'fra...]
    select_n x0 -> x1, other arithmetic: none -> 2.03 us  [on_device(): velocity = jnp.where(near_half, own[None], rest[None]).reshape(rows, width)]
    ppermute x8, starting transfers between devices: 9.83 us -> 11.7 us  [core_swap(): return lax.ppermute(block, 'step', [(i, i ^ 1) for i in range(2 * NX)])]
  transfers between devices with their start and end apart: 31 -> 31, of which waited for: 14 -> 20; matrix products, arithmetic and copies ran while one was open for 3% -> 5% of each run, Pallas kernels for 21% -> 15%
where the time goes in v3:
time: 181 us; the launch traced here: 180 us
  waiting for transfers between devices  78.3 us (43%)
  starting transfers between devices  45.2 us (25%)
  Pallas kernels  35.3 us (20%)
  local copies, waits for them, and re-layouts  8.04 us (4%)
  other arithmetic  7.27 us (4%)
  between operations  5.97 us (3%)
    ppermute x6, waiting for transfers between devices, z_shift(): return lax.ppermute(block, 'frame', pairs)  29.7 us
    pallas_call x1, Pallas kernels, attend(): pl.pallas_call(attend_kernel, in_specs=[smem, smem, pl.BlockSpec(memory_s...  27.8 us
    ppermute x7, waiting for transfers between devices, y_shift(): return lax.ppermute(block, 'frame', pairs)  23.9 us
    ppermute x3, waiting for transfers between devices, x_later(): return lax.ppermute(block, 'step', pairs)  18.7 us
    ppermute x8, starting transfers between devices, core_swap(): return lax.ppermute(block, 'step', [(i, i ^ 1) for i in range(2 * NX)])  11.7 us
    ppermute x7, starting transfers between devices, y_shift(): return lax.ppermute(block, 'frame', pairs)  10.1 us
    all_to_all x1, starting transfers between devices, on_device(): lax.all_to_all(jnp.broadcast_to(packed[None], (NZ,) + packed.shape), 'fra...  7.56 us
    ppermute x6, starting transfers between devices, z_shift(): return lax.ppermute(block, 'frame', pairs)  6.52 us
  transfers between devices with their start and end apart: 31, of which 20 were waited for; matrix products, arithmetic and copies ran while one was open for 5% of the time, Pallas kernels for 15%

profile of v3, /device:TPU:79, one launch (start us, length us, event | category | flops | bytes accessed | tf_op | source)
XLA Modules:
  0.0 180.0 jit_solution(6288725993293222664)
XLA Ops:
  0.6 0.6 pad_add_fusion.where_ref
  1.3 2.9 %modulate.1.refs_0_ = bf16[256,1536]{1,0:T(8,128)(2,1)} custom-call(s32[4]{0:T(128)} %pad_add_fusion.where_ref, s32[8]{0:T(128)} %index_ref.3, bf16[256,1536]{1,0:T(8,128)(2,1)} %bitcast.46, f32[3,50,1536]{2,1,0:T(8,128)} %bitcast.37), custom_call_target="tpu_custom_call" | custom-call | tf_op jit(solution)/shard_map/modulate/pallas_call | solution.py:63
  4.2 2.1 %collective-permute-start = (bf16[256,1536]{1,0:T(8,128)(2,1)}, bf16[256,1536]{1,0:T(8,128)(2,1)S(1)}, u32[]{:S(2)}, u32[]{:S(2)}) collective-permute-start(bf16[256,1536]{1,0:T(8,128)(2,1)} %modulate.1.refs_0_), channel_id=1, source_target_pairs={{0,2},{1,3},{2,0},{3,1},{4,6},{5,7},{6,4},{7,5},{8,10},{9,11},{10,... | collective-permute-start | bytes 2359304 | tf_op jit(solution)/shard_map/ppermute | solution.py:22
  6.4 0.7 broadcast_in_dim.75
  7.2 7.6 %all-to-all-start = ((bf16[8,8,2304]{2,1,0:T(8,128)(2,1)}), bf16[8,8,2304]{2,1,0:T(8,128)(2,1)S(1)}, u32[]{:S(2)}, u32[]{:S(2)}) async-start(bf16[8,8,2304]{2,1,0:T(8,128)(2,1)} %broadcast_in_dim.75), calls=%async_computation | async-start | bytes 589824 | tf_op jit(solution)/shard_map/all_to_all | solution.py:312
  14.7 0.6 fusion.2
  19.1 0.7 fusion.1
  19.7 2.8 %all-to-all-done = bf16[8,8,2304]{2,1,0:T(8,128)(2,1)S(1)} async-done(((bf16[8,8,2304]{2,1,0:T(8,128)(2,1)}), bf16[8,8,2304]{2,1,0:T(8,128)(2,1)S(1)}, u32[]{:S(2)}, u32[]{:S(2)}) %all-to-all-start) | async-done | bytes 294944 | tf_op jit(solution)/shard_map/all_to_all | solution.py:312
  22.5 2.0 %collective-permute-done.refs_3_ = bf16[256,1536]{1,0:T(8,128)(2,1)S(1)} collective-permute-done((bf16[256,1536]{1,0:T(8,128)(2,1)}, bf16[256,1536]{1,0:T(8,128)(2,1)S(1)}, u32[]{:S(2)}, u32[]{:S(2)}) %collective-permute-start) | collective-permute-done | bytes 786464 | tf_op jit(solution)/shard_map/ppermute | solution.py:22
  24.6 2.3 %collective-permute-start.2 = (bf16[64,2304]{1,0:T(8,128)(2,1)S(1)}, bf16[64,2304]{1,0:T(8,128)(2,1)S(1)}, u32[]{:S(2)}, u32[]{:S(2)}) collective-permute-start(bf16[64,2304]{1,0:T(8,128)(2,1)S(1)} %bitcast.41), channel_id=1, source_target_pairs={{0,2},{1,3},{2,0},{3,1},{4,6},{5,7},{6,4},{7,5},{8,10},{9,11},{10,... | collective-permute-start | bytes 884744 | tf_op jit(solution)/shard_map/ppermute | solution.py:22
  26.9 1.6 collective-permute-start.3
  28.5 1.6 collective-permute-start.4
  30.3 1.1 collective-permute-done.1
  31.4 7.3 %collective-permute-done.2 = bf16[64,2304]{1,0:T(8,128)(2,1)S(1)} collective-permute-done((bf16[64,2304]{1,0:T(8,128)(2,1)S(1)}, bf16[64,2304]{1,0:T(8,128)(2,1)S(1)}, u32[]{:S(2)}, u32[]{:S(2)}) %collective-permute-start.2) | collective-permute-done | bytes 294944 | tf_op jit(solution)/shard_map/ppermute | solution.py:22
  38.8 1.7 collective-permute-done.3
  40.5 4.9 %collective-permute-done.4.refs_1_ = bf16[256,1536]{1,0:T(8,128)(2,1)S(1)} collective-permute-done((bf16[256,1536]{1,0:T(8,128)(2,1)}, bf16[256,1536]{1,0:T(8,128)(2,1)S(1)}, u32[]{:S(2)}, u32[]{:S(2)}) %collective-permute-start.4) | collective-permute-done | bytes 786464 | tf_op jit(solution)/shard_map/ppermute | solution.py:27
  45.4 3.1 %collective-permute-done.5.refs_2_ = bf16[256,1536]{1,0:T(8,128)(2,1)S(1)} collective-permute-done((bf16[256,1536]{1,0:T(8,128)(2,1)}, bf16[256,1536]{1,0:T(8,128)(2,1)S(1)}, u32[]{:S(2)}, u32[]{:S(2)}) %collective-permute-start.5) | collective-permute-done | bytes 786464 | tf_op jit(solution)/shard_map/ppermute | solution.py:27
  48.5 1.2 reshape.60.refs_11_
  49.7 0.2 collective-permute-start.6
  49.9 1.3 broadcast_select_fusion.1
  51.2 1.5 collective-permute-start.9
  52.6 2.4 %collective-permute-start.7 = (bf16[256,1536]{1,0:T(8,128)(2,1)S(1)}, bf16[256,1536]{1,0:T(8,128)(2,1)}, u32[]{:S(2)}, u32[]{:S(2)}) collective-permute-start(bf16[256,1536]{1,0:T(8,128)(2,1)S(1)} %collective-permute-done.4.refs_1_), channel_id=1, source_target_pairs={{0,4},{1,5},{2,6},{3,7},{4,8},{5,9},{6,10},{7,11},{8,12},{9,13},{1... | collective-permute-start | bytes 2359304 | tf_op jit(solution)/shard_map/ppermute | solution.py:27
  55.0 0.3 slice.13
  55.5 11.4 %collective-permute-done.10.refs_7_ = bf16[256,1536]{1,0:T(8,128)(2,1)} collective-permute-done((bf16[256,1536]{1,0:T(8,128)(2,1)}, bf16[256,1536]{1,0:T(8,128)(2,1)}, u32[]{:S(2)}, u32[]{:S(2)}) %collective-permute-start.10) | collective-permute-done | bytes 786464 | tf_op jit(solution)/shard_map/ppermute | solution.py:22
  66.9 0.4 collective-permute-done.9.refs_6_
  67.3 0.3 collective-permute-done.7.refs_4_
  67.6 1.8 %collective-permute-done.8.refs_5_ = bf16[256,1536]{1,0:T(8,128)(2,1)} collective-permute-done((bf16[256,1536]{1,0:T(8,128)(2,1)S(1)}, bf16[256,1536]{1,0:T(8,128)(2,1)}, u32[]{:S(2)}, u32[]{:S(2)}) %collective-permute-start.8) | collective-permute-done | bytes 786464 | tf_op jit(solution)/shard_map/ppermute | solution.py:27
  69.4 1.3 collective-permute-start.11
  70.7 1.4 collective-permute-start.12
  72.2 2.4 %collective-permute-start.15 = (bf16[256,1536]{1,0:T(8,128)(2,1)S(1)}, bf16[256,1536]{1,0:T(8,128)(2,1)S(1)}, u32[]{:S(2)}, u32[]{:S(2)}) collective-permute-start(bf16[256,1536]{1,0:T(8,128)(2,1)S(1)} %broadcast_select_fusion), channel_id=1, source_target_pairs={{0,2},{1,3},{2,0},{3,1},{4,6},{5,7},{6,4},{7,5},{8,10},{9,11},{10,... | collective-permute-start | bytes 2359304 | tf_op jit(solution)/shard_map/ppermute | solution.py:22
  74.6 6.5 %collective-permute-start.16 = (bf16[96,1536]{1,0:T(8,128)(2,1)S(1)}, bf16[96,1536]{1,0:T(8,128)(2,1)S(1)}, u32[]{:S(2)}, u32[]{:S(2)}) collective-permute-start(bf16[96,1536]{1,0:T(8,128)(2,1)S(1)} %reshape.61), channel_id=1, source_target_pairs={{0,32},{32,0},{64,96},{96,64},{128,160},{160,128},{192,224},{224,1... | collective-permute-start | bytes 884744 | tf_op jit(solution)/shard_map/ppermute | solution.py:41
  81.1 1.0 slice.14
  82.2 1.5 collective-permute-start.13
  83.6 1.0 slice.15
  84.7 1.0 collective-permute-start.14
  85.8 10.5 %collective-permute-done.13.refs_9_ = bf16[128,1536]{1,0:T(8,128)(2,1)} collective-permute-done((bf16[128,1536]{1,0:T(8,128)(2,1)S(1)}, bf16[128,1536]{1,0:T(8,128)(2,1)}, u32[]{:S(2)}, u32[]{:S(2)}) %collective-permute-start.13) | collective-permute-done | bytes 393248 | tf_op jit(solution)/shard_map/ppermute | solution.py:27
  96.3 0.8 collective-permute-start.17
  97.1 9.1 %collective-permute-done.14.refs_10_ = bf16[128,1536]{1,0:T(8,128)(2,1)} collective-permute-done((bf16[128,1536]{1,0:T(8,128)(2,1)S(1)}, bf16[128,1536]{1,0:T(8,128)(2,1)}, u32[]{:S(2)}, u32[]{:S(2)}) %collective-permute-start.14) | collective-permute-done | bytes 393248 | tf_op jit(solution)/shard_map/ppermute | solution.py:27
  106.2 0.7 collective-permute-start.18
  107.1 0.5 collective-permute-start.20
  107.6 1.5 collective-permute-start.23
  109.2 0.9 collective-permute-start.24
  110.1 1.4 collective-permute-done.19.refs_17_
  111.5 1.0 copy-done.20
  112.5 27.8 %attend.1 = (bf16[128,768]{1,0:T(8,128)(2,1)}, bf16[128,768]{1,0:T(8,128)(2,1)}) custom-call(s32[4]{0:T(128)} %pad_add_fusion.where_ref, s32[2,64]{1,0:T(2,128)} %mask_ref.1, f32[2,768]{1,0:T(2,128)} %gain_ref.1, bf16[256,1536]{1,0:T(8,128)(2,1)} %modulate.1.refs_0_, bf16[256,1536]{1,0:T(8,128)(2,1)} %copy-done.1, bf16[256,1536]{1,0:T(8,128)(2,1)} %copy-done.2, ...), custom_call_target="tpu_custom_call" | custom-call | flops 16000000000 | bytes 16000000 | tf_op jit(solution)/shard_map/attend/pallas_call | solution.py:188
  140.4 0.5 collective-permute-start.21
  140.9 1.2 collective-permute-done.21.got_ref
  142.2 0.7 copy-done.11
  142.8 4.5 %output.1 = (bf16[128,1536]{1,0:T(8,128)(2,1)}, bf16[128,1536]{1,0:T(8,128)(2,1)}, bf16[128,1536]{1,0:T(8,128)(2,1)}) custom-call(s32[4]{0:T(128)} %pad_add_fusion.where_ref, s32[8]{0:T(128)} %index_ref.3, f32[50]{0:T(128)} %size_ref.1, bf16[128,768]{1,0:T(8,128)(2,1)} %get-tuple-element.62.keep_ref, bf16[128,768]{1,0:T(8,128)(2,1)} %copy-done.11, ...), custom_call_target="tpu_custom_call" | custom-call | tf_op jit(solution)/shard_map/output/pallas_call | solution.py:256
  147.3 1.4 collective-permute-start.25
  148.8 0.5 collective-permute-start.27
  149.2 10.7 %collective-permute-done.25 = bf16[128,1536]{1,0:T(8,128)(2,1)S(1)} collective-permute-done((bf16[128,1536]{1,0:T(8,128)(2,1)}, bf16[128,1536]{1,0:T(8,128)(2,1)S(1)}, u32[]{:S(2)}, u32[]{:S(2)}) %collective-permute-start.25) | collective-permute-done | bytes 393248 | tf_op jit(solution)/shard_map/ppermute | solution.py:37
  159.9 1.3 collective-permute-start.26
  161.2 1.3 collective-permute-start.28
  163.8 2.0 %bitcast_select_fusion.1 = bf16[256,1536]{1,0:T(8,128)(2,1)} fusion(pred[256]{0:T(512)(128)(4,1)S(1)} %broadcast_bitcast_fusion, bf16[128,1536]{1,0:T(8,128)(2,1)S(1)} %collective-permute-done.27, bf16[128,1536]{1,0:T(8,128)(2,1)} %get-tuple-element.75), kind=kLoop, calls=%fused_computation.2 | loop fusion | flops 393216 | bytes 1573120 | tf_op jit(solution)/shard_map/jit(_where)/select_n | solution.py:363
  165.9 5.3 %collective-permute-done.26 = bf16[128,1536]{1,0:T(8,128)(2,1)S(1)} collective-permute-done((bf16[128,1536]{1,0:T(8,128)(2,1)S(1)}, bf16[128,1536]{1,0:T(8,128)(2,1)S(1)}, u32[]{:S(2)}, u32[]{:S(2)}) %collective-permute-start.26) | collective-permute-done | bytes 393248 | tf_op jit(solution)/shard_map/ppermute | solution.py:37
  171.2 2.7 %collective-permute-done.28 = bf16[128,1536]{1,0:T(8,128)(2,1)S(1)} collective-permute-done((bf16[128,1536]{1,0:T(8,128)(2,1)}, bf16[128,1536]{1,0:T(8,128)(2,1)S(1)}, u32[]{:S(2)}, u32[]{:S(2)}) %collective-permute-start.28) | collective-permute-done | bytes 393248 | tf_op jit(solution)/shard_map/ppermute | solution.py:37
  173.9 0.2 add_convert_fusion
  174.1 2.2 %collective-permute-start.29 = (bf16[128,1536]{1,0:T(8,128)(2,1)S(1)}, bf16[128,1536]{1,0:T(8,128)(2,1)S(1)}, u32[]{:S(2)}, u32[]{:S(2)}) collective-permute-start(bf16[128,1536]{1,0:T(8,128)(2,1)S(1)} %add_convert_fusion), channel_id=1, source_target_pairs={{0,32},{32,0},{64,96},{96,64},{128,160},{160,128},{192,224},{224,1... | collective-permute-start | bytes 1179656 | tf_op jit(solution)/shard_map/ppermute | solution.py:41
  176.4 0.9 multiply_add_fusion.1
  177.2 0.5 collective-permute-done.29
  177.7 0.7 multiply_add_fusion
  178.4 0.2 copy-done.5
  178.6 1.4 fusion
  (73 shorter events, 1.2 us)
Async XLA Ops:
  1.3 5.1 %copy-start.13 = (bf16[3,1536]{1,0:T(4,128)(2,1)S(1)}, bf16[3,1536]{1,0:T(4,128)(2,1)}, u32[]{:S(2)}) copy-start(bf16[3,1536]{1,0:T(4,128)(2,1)} %param.15) | copy-start | bytes 27652
  1.3 5.1 %copy-start.12 = (bf16[6,2304]{1,0:T(8,128)(2,1)S(1)}, bf16[6,2304]{1,0:T(8,128)(2,1)}, u32[]{:S(2)}) copy-start(bf16[6,2304]{1,0:T(8,128)(2,1)} %param.14) | copy-start | bytes 82948
  1.3 13.4 %copy-start.14 = (s32[8]{0:T(128)S(1)}, s32[8]{0:T(128)}, u32[]{:S(2)}) copy-start(s32[8]{0:T(128)} %index_ref.3) | copy-start | bytes 100
  1.3 17.8 %copy-start.15 = (f32[50]{0:T(128)S(1)}, f32[50]{0:T(128)}, u32[]{:S(2)}) copy-start(f32[50]{0:T(128)} %size_ref.1) | copy-start | bytes 604
  4.2 20.2 %collective-permute-start = (bf16[256,1536]{1,0:T(8,128)(2,1)}, bf16[256,1536]{1,0:T(8,128)(2,1)S(1)}, u32[]{:S(2)}, u32[]{:S(2)}) collective-permute-start(bf16[256,1536]{1,0:T(8,128)(2,1)} %modulate.1.refs_0_), channel_id=1, source_target_pairs={{0,2},{1,3},{2,0},{3,1},{4,6},{5,7},{6,4},{7,5},{8,10},{9,11},{10,... | collective-permute-start | bytes 2359304 | tf_op jit(solution)/shard_map/ppermute | solution.py:22
  7.2 15.3 %all-to-all-start = ((bf16[8,8,2304]{2,1,0:T(8,128)(2,1)}), bf16[8,8,2304]{2,1,0:T(8,128)(2,1)S(1)}, u32[]{:S(2)}, u32[]{:S(2)}) async-start(bf16[8,8,2304]{2,1,0:T(8,128)(2,1)} %broadcast_in_dim.75), calls=%async_computation | async-start | bytes 589824 | tf_op jit(solution)/shard_map/all_to_all | solution.py:312
  24.5 2.5 %copy-start.21 = (bf16[256,1536]{1,0:T(8,128)(2,1)}, bf16[256,1536]{1,0:T(8,128)(2,1)S(1)}, u32[]{:S(2)}) copy-start(bf16[256,1536]{1,0:T(8,128)(2,1)S(1)} %collective-permute-done.refs_3_) | copy-start | bytes 2359300
  24.5 7.0 %collective-permute-start.1 = (bf16[64,2304]{1,0:T(8,128)(2,1)S(1)}, bf16[64,2304]{1,0:T(8,128)(2,1)S(1)}, u32[]{:S(2)}, u32[]{:S(2)}) collective-permute-start(bf16[64,2304]{1,0:T(8,128)(2,1)S(1)} %bitcast.40), channel_id=1, source_target_pairs={{0,3},{1,0},{2,1},{3,2},{4,7},{5,4},{6,5},{7,6},{8,11},{9,8},{10,9... | collective-permute-start | bytes 884744 | tf_op jit(solution)/shard_map/ppermute | solution.py:22
  24.6 14.1 %collective-permute-start.2 = (bf16[64,2304]{1,0:T(8,128)(2,1)S(1)}, bf16[64,2304]{1,0:T(8,128)(2,1)S(1)}, u32[]{:S(2)}, u32[]{:S(2)}) collective-permute-start(bf16[64,2304]{1,0:T(8,128)(2,1)S(1)} %bitcast.41), channel_id=1, source_target_pairs={{0,2},{1,3},{2,0},{3,1},{4,6},{5,7},{6,4},{7,5},{8,10},{9,11},{10,... | collective-permute-start | bytes 884744 | tf_op jit(solution)/shard_map/ppermute | solution.py:22
  26.9 13.5 %collective-permute-start.3 = (bf16[64,2304]{1,0:T(8,128)(2,1)S(1)}, bf16[64,2304]{1,0:T(8,128)(2,1)S(1)}, u32[]{:S(2)}, u32[]{:S(2)}) collective-permute-start(bf16[64,2304]{1,0:T(8,128)(2,1)S(1)} %bitcast.42), channel_id=1, source_target_pairs={{0,1},{1,2},{2,3},{3,0},{4,5},{5,6},{6,7},{7,4},{8,9},{9,10},{10,1... | collective-permute-start | bytes 884744 | tf_op jit(solution)/shard_map/ppermute | solution.py:22
  28.5 16.9 %collective-permute-start.4 = (bf16[256,1536]{1,0:T(8,128)(2,1)}, bf16[256,1536]{1,0:T(8,128)(2,1)S(1)}, u32[]{:S(2)}, u32[]{:S(2)}) collective-permute-start(bf16[256,1536]{1,0:T(8,128)(2,1)} %modulate.1.refs_0_), channel_id=1, source_target_pairs={{0,4},{1,5},{2,6},{3,7},{4,8},{5,9},{6,10},{7,11},{8,12},{9,13},{1... | collective-permute-start | bytes 2359304 | tf_op jit(solution)/shard_map/ppermute | solution.py:27
  30.2 18.3 %collective-permute-start.5 = (bf16[256,1536]{1,0:T(8,128)(2,1)}, bf16[256,1536]{1,0:T(8,128)(2,1)S(1)}, u32[]{:S(2)}, u32[]{:S(2)}) collective-permute-start(bf16[256,1536]{1,0:T(8,128)(2,1)} %modulate.1.refs_0_), channel_id=1, source_target_pairs={{0,28},{1,29},{2,30},{3,31},{4,0},{5,1},{6,2},{7,3},{8,4},{9,5},{1... | collective-permute-start | bytes 2359304 | tf_op jit(solution)/shard_map/ppermute | solution.py:27
  40.5 9.4 %copy-start.3 = (bf16[256,1536]{1,0:T(8,128)(2,1)S(1)}, bf16[256,1536]{1,0:T(8,128)(2,1)}, u32[]{:S(2)}) copy-start(bf16[256,1536]{1,0:T(8,128)(2,1)} %modulate.1.refs_0_) | copy-start | bytes 2359300
  45.4 26.7 %copy-start.1 = (bf16[256,1536]{1,0:T(8,128)(2,1)}, bf16[256,1536]{1,0:T(8,128)(2,1)S(1)}, u32[]{:S(2)}) copy-start(bf16[256,1536]{1,0:T(8,128)(2,1)S(1)} %collective-permute-done.4.refs_1_) | copy-start | bytes 2359300
  48.5 23.7 %copy-start.2 = (bf16[256,1536]{1,0:T(8,128)(2,1)}, bf16[256,1536]{1,0:T(8,128)(2,1)S(1)}, u32[]{:S(2)}) copy-start(bf16[256,1536]{1,0:T(8,128)(2,1)S(1)} %collective-permute-done.5.refs_2_) | copy-start | bytes 2359300
  49.7 19.7 %collective-permute-start.6 = (bf16[192,2304]{1,0:T(8,128)(2,1)}, bf16[192,2304]{1,0:T(8,128)(2,1)}, u32[]{:S(2)}, u32[]{:S(2)}) collective-permute-start(bf16[192,2304]{1,0:T(8,128)(2,1)} %reshape.60.refs_11_), channel_id=1, source_target_pairs={{0,64},{32,96},{64,128},{96,160},{128,192},{160,224},{192,0},{224,... | collective-permute-start | bytes 2654216 | tf_op jit(solution)/shard_map/ppermute | solution.py:32
  51.2 15.8 %collective-permute-start.10 = (bf16[256,1536]{1,0:T(8,128)(2,1)}, bf16[256,1536]{1,0:T(8,128)(2,1)}, u32[]{:S(2)}, u32[]{:S(2)}) collective-permute-start(bf16[256,1536]{1,0:T(8,128)(2,1)} %get-tuple-element.76), channel_id=1, source_target_pairs={{0,3},{1,0},{2,1},{3,2},{4,7},{5,4},{6,5},{7,6},{8,11},{9,8},{10,9... | collective-permute-start | bytes 2359304 | tf_op jit(solution)/shard_map/ppermute | solution.py:22
  51.2 16.1 %collective-permute-start.9 = (bf16[256,1536]{1,0:T(8,128)(2,1)}, bf16[256,1536]{1,0:T(8,128)(2,1)}, u32[]{:S(2)}, u32[]{:S(2)}) collective-permute-start(bf16[256,1536]{1,0:T(8,128)(2,1)} %get-tuple-element.77), channel_id=1, source_target_pairs={{0,1},{1,2},{2,3},{3,0},{4,5},{5,6},{6,7},{7,4},{8,9},{9,10},{10,1... | collective-permute-start | bytes 2359304 | tf_op jit(solution)/shard_map/ppermute | solution.py:22
  52.6 15.0 %collective-permute-start.7 = (bf16[256,1536]{1,0:T(8,128)(2,1)S(1)}, bf16[256,1536]{1,0:T(8,128)(2,1)}, u32[]{:S(2)}, u32[]{:S(2)}) collective-permute-start(bf16[256,1536]{1,0:T(8,128)(2,1)S(1)} %collective-permute-done.4.refs_1_), channel_id=1, source_target_pairs={{0,4},{1,5},{2,6},{3,7},{4,8},{5,9},{6,10},{7,11},{8,12},{9,13},{1... | collective-permute-start | bytes 2359304 | tf_op jit(solution)/shard_map/ppermute | solution.py:27
  55.0 14.4 %collective-permute-start.8 = (bf16[256,1536]{1,0:T(8,128)(2,1)S(1)}, bf16[256,1536]{1,0:T(8,128)(2,1)}, u32[]{:S(2)}, u32[]{:S(2)}) collective-permute-start(bf16[256,1536]{1,0:T(8,128)(2,1)S(1)} %collective-permute-done.5.refs_2_), channel_id=1, source_target_pairs={{0,28},{1,29},{2,30},{3,31},{4,0},{5,1},{6,2},{7,3},{8,4},{9,5},{1... | collective-permute-start | bytes 2359304 | tf_op jit(solution)/shard_map/ppermute | solution.py:27
  69.4 37.5 %collective-permute-start.11 = (bf16[192,2304]{1,0:T(8,128)(2,1)}, bf16[192,2304]{1,0:T(8,128)(2,1)S(1)}, u32[]{:S(2)}, u32[]{:S(2)}) collective-permute-start(bf16[192,2304]{1,0:T(8,128)(2,1)} %reshape.60.refs_11_), channel_id=1, source_target_pairs={{0,192},{32,224},{64,0},{96,32},{128,64},{160,96},{192,128},{224,1... | collective-permute-start | bytes 2654216 | tf_op jit(solution)/shard_map/ppermute | solution.py:32
  70.7 36.3 %collective-permute-start.12 = (bf16[192,2304]{1,0:T(8,128)(2,1)}, bf16[192,2304]{1,0:T(8,128)(2,1)S(1)}, u32[]{:S(2)}, u32[]{:S(2)}) collective-permute-start(bf16[192,2304]{1,0:T(8,128)(2,1)} %collective-permute-done.6.refs_12_), channel_id=1, source_target_pairs={{0,64},{32,96},{64,128},{96,160},{128,192},{160,224},{192,0},{224,... | collective-permute-start | bytes 2654216 | tf_op jit(solution)/shard_map/ppermute | solution.py:32
  72.2 34.7 %collective-permute-start.15 = (bf16[256,1536]{1,0:T(8,128)(2,1)S(1)}, bf16[256,1536]{1,0:T(8,128)(2,1)S(1)}, u32[]{:S(2)}, u32[]{:S(2)}) collective-permute-start(bf16[256,1536]{1,0:T(8,128)(2,1)S(1)} %broadcast_select_fusion), channel_id=1, source_target_pairs={{0,2},{1,3},{2,0},{3,1},{4,6},{5,7},{6,4},{7,5},{8,10},{9,11},{10,... | collective-permute-start | bytes 2359304 | tf_op jit(solution)/shard_map/ppermute | solution.py:22
  74.6 10.0 %collective-permute-start.16 = (bf16[96,1536]{1,0:T(8,128)(2,1)S(1)}, bf16[96,1536]{1,0:T(8,128)(2,1)S(1)}, u32[]{:S(2)}, u32[]{:S(2)}) collective-permute-start(bf16[96,1536]{1,0:T(8,128)(2,1)S(1)} %reshape.61), channel_id=1, source_target_pairs={{0,32},{32,0},{64,96},{96,64},{128,160},{160,128},{192,224},{224,1... | collective-permute-start | bytes 884744 | tf_op jit(solution)/shard_map/ppermute | solution.py:41
  82.1 14.2 %copy-start.6 = (bf16[192,2304]{1,0:T(8,128)(2,1)S(1)}, bf16[192,2304]{1,0:T(8,128)(2,1)}, u32[]{:S(2)}) copy-start(bf16[192,2304]{1,0:T(8,128)(2,1)} %reshape.60.refs_11_) | copy-start | bytes 2654212
  82.2 14.1 %collective-permute-start.13 = (bf16[128,1536]{1,0:T(8,128)(2,1)S(1)}, bf16[128,1536]{1,0:T(8,128)(2,1)}, u32[]{:S(2)}, u32[]{:S(2)}) collective-permute-start(bf16[128,1536]{1,0:T(8,128)(2,1)S(1)} %slice.14), channel_id=1, source_target_pairs={{0,8},{1,9},{2,10},{3,11},{4,12},{5,13},{6,14},{7,15},{8,16},{9,17... | collective-permute-start | bytes 1179656 | tf_op jit(solution)/shard_map/ppermute | solution.py:27
  84.7 21.6 %collective-permute-start.14 = (bf16[128,1536]{1,0:T(8,128)(2,1)S(1)}, bf16[128,1536]{1,0:T(8,128)(2,1)}, u32[]{:S(2)}, u32[]{:S(2)}) collective-permute-start(bf16[128,1536]{1,0:T(8,128)(2,1)S(1)} %slice.15), channel_id=1, source_target_pairs={{0,24},{1,25},{2,26},{3,27},{4,28},{5,29},{6,30},{7,31},{8,0},{9,1... | collective-permute-start | bytes 1179656 | tf_op jit(solution)/shard_map/ppermute | solution.py:27
  85.8 54.6 %copy-start.4 = (bf16[2,96,1536]{2,1,0:T(8,128)(2,1)}, bf16[2,96,1536]{2,1,0:T(8,128)(2,1)S(1)}, u32[]{:S(2)}) copy-start(bf16[2,96,1536]{2,1,0:T(8,128)(2,1)S(1)} %pad_maximum_fusion.refs_0_) | copy-start | bytes 1769476
  96.3 11.3 %collective-permute-start.17 = (bf16[192,2304]{1,0:T(8,128)(2,1)S(1)}, bf16[192,2304]{1,0:T(8,128)(2,1)S(1)}, u32[]{:S(2)}, u32[]{:S(2)}) collective-permute-start(bf16[192,2304]{1,0:T(8,128)(2,1)S(1)} %copy-done.6), channel_id=1, source_target_pairs={{0,32},{32,0},{64,96},{96,64},{128,160},{160,128},{192,224},{224,1... | collective-permute-start | bytes 2654216 | tf_op jit(solution)/shard_map/ppermute | solution.py:41
  106.2 3.0 %collective-permute-start.18 = (bf16[192,2304]{1,0:T(8,128)(2,1)}, bf16[192,2304]{1,0:T(8,128)(2,1)S(1)}, u32[]{:S(2)}, u32[]{:S(2)}) collective-permute-start(bf16[192,2304]{1,0:T(8,128)(2,1)} %collective-permute-done.6.refs_12_), channel_id=1, source_target_pairs={{0,32},{32,0},{64,96},{96,64},{128,160},{160,128},{192,224},{224,1... | collective-permute-start | bytes 2654216 | tf_op jit(solution)/shard_map/ppermute | solution.py:41
  107.0 5.6 %copy-start.22 = (bf16[256,1536]{1,0:T(8,128)(2,1)}, bf16[256,1536]{1,0:T(8,128)(2,1)S(1)}, u32[]{:S(2)}) copy-start(bf16[256,1536]{1,0:T(8,128)(2,1)S(1)} %collective-permute-done.15.refs_8_) | copy-start | bytes 2359300
  107.0 5.5 %copy-start.16 = (bf16[192,2304]{1,0:T(8,128)(2,1)}, bf16[192,2304]{1,0:T(8,128)(2,1)S(1)}, u32[]{:S(2)}) copy-start(bf16[192,2304]{1,0:T(8,128)(2,1)S(1)} %collective-permute-done.11.refs_13_) | copy-start | bytes 2654212
  107.0 5.5 %copy-start.17 = (bf16[192,2304]{1,0:T(8,128)(2,1)}, bf16[192,2304]{1,0:T(8,128)(2,1)S(1)}, u32[]{:S(2)}) copy-start(bf16[192,2304]{1,0:T(8,128)(2,1)S(1)} %collective-permute-done.12.refs_14_) | copy-start | bytes 2654212
  107.0 4.5 %collective-permute-start.19 = (bf16[192,2304]{1,0:T(8,128)(2,1)S(1)}, bf16[192,2304]{1,0:T(8,128)(2,1)S(1)}, u32[]{:S(2)}, u32[]{:S(2)}) collective-permute-start(bf16[192,2304]{1,0:T(8,128)(2,1)S(1)} %collective-permute-done.11.refs_13_), channel_id=1, source_target_pairs={{0,32},{32,0},{64,96},{96,64},{128,160},{160,128},{192,224},{224,1... | collective-permute-start | bytes 2654216 | tf_op jit(solution)/shard_map/ppermute | solution.py:41
  107.1 5.4 %collective-permute-start.20 = (bf16[192,2304]{1,0:T(8,128)(2,1)S(1)}, bf16[192,2304]{1,0:T(8,128)(2,1)}, u32[]{:S(2)}, u32[]{:S(2)}) collective-permute-start(bf16[192,2304]{1,0:T(8,128)(2,1)S(1)} %collective-permute-done.12.refs_14_), channel_id=1, source_target_pairs={{0,32},{32,0},{64,96},{96,64},{128,160},{160,128},{192,224},{224,1... | collective-permute-start | bytes 2654216 | tf_op jit(solution)/shard_map/ppermute | solution.py:41
  107.6 33.3 %collective-permute-start.22 = (bf16[2,96,1536]{2,1,0:T(8,128)(2,1)S(1)}, bf16[2,96,1536]{2,1,0:T(8,128)(2,1)S(1)}, u32[]{:S(2)}, u32[]{:S(2)}) collective-permute-start(bf16[2,96,1536]{2,1,0:T(8,128)(2,1)S(1)} %pad_maximum_fusion.refs_0_), channel_id=1, source_target_pairs={{0,64},{32,96},{64,128},{96,160},{128,192},{160,224},{192,0},{224,... | collective-permute-start | bytes 1769480 | tf_op jit(solution)/shard_map/ppermute | solution.py:32
  107.6 4.9 %copy-start.18 = (bf16[192,2304]{1,0:T(8,128)(2,1)}, bf16[192,2304]{1,0:T(8,128)(2,1)S(1)}, u32[]{:S(2)}) copy-start(bf16[192,2304]{1,0:T(8,128)(2,1)S(1)} %collective-permute-done.17.refs_15_) | copy-start | bytes 2654212
  107.6 33.3 %collective-permute-start.23 = (bf16[2,96,1536]{2,1,0:T(8,128)(2,1)S(1)}, bf16[2,96,1536]{2,1,0:T(8,128)(2,1)S(1)}, u32[]{:S(2)}, u32[]{:S(2)}) collective-permute-start(bf16[2,96,1536]{2,1,0:T(8,128)(2,1)S(1)} %pad_maximum_fusion.refs_0_), channel_id=1, source_target_pairs={{0,192},{32,224},{64,0},{96,32},{128,64},{160,96},{192,128},{224,1... | collective-permute-start | bytes 1769480 | tf_op jit(solution)/shard_map/ppermute | solution.py:32
  109.2 3.3 %copy-start.19 = (bf16[192,2304]{1,0:T(8,128)(2,1)}, bf16[192,2304]{1,0:T(8,128)(2,1)S(1)}, u32[]{:S(2)}) copy-start(bf16[192,2304]{1,0:T(8,128)(2,1)S(1)} %collective-permute-done.18.refs_16_) | copy-start | bytes 2654212
  109.2 31.7 %collective-permute-start.24 = (bf16[2,96,1536]{2,1,0:T(8,128)(2,1)S(1)}, bf16[2,96,1536]{2,1,0:T(8,128)(2,1)S(1)}, u32[]{:S(2)}, u32[]{:S(2)}) collective-permute-start(bf16[2,96,1536]{2,1,0:T(8,128)(2,1)S(1)} %pad_maximum_fusion.refs_0_), channel_id=1, source_target_pairs={{0,128},{32,160},{64,192},{96,224},{128,0},{160,32},{192,64},{224,... | collective-permute-start | bytes 1769480 | tf_op jit(solution)/shard_map/ppermute | solution.py:32
  111.5 1.0 copy-start.20
  140.4 1.7 collective-permute-start.21
  140.9 1.3 copy-start.7
  140.9 1.3 copy-start.8
  140.9 1.3 copy-start.9
  142.1 0.7 copy-start.11
  147.3 26.6 %copy-start = (bf16[128,1536]{1,0:T(8,128)(2,1)S(1)}, bf16[128,1536]{1,0:T(8,128)(2,1)}, u32[]{:S(2)}) copy-start(bf16[128,1536]{1,0:T(8,128)(2,1)} %get-tuple-element.75) | copy-start | bytes 1179652
  147.3 12.6 %collective-permute-start.25 = (bf16[128,1536]{1,0:T(8,128)(2,1)}, bf16[128,1536]{1,0:T(8,128)(2,1)S(1)}, u32[]{:S(2)}, u32[]{:S(2)}) collective-permute-start(bf16[128,1536]{1,0:T(8,128)(2,1)} %get-tuple-element.65), channel_id=1, source_target_pairs={{0,64},{32,96},{64,128},{96,160},{128,192},{160,224},{1,65},{33,97... | collective-permute-start | bytes 1179656 | tf_op jit(solution)/shard_map/ppermute | solution.py:37
  148.8 15.1 %collective-permute-start.27 = (bf16[128,1536]{1,0:T(8,128)(2,1)}, bf16[128,1536]{1,0:T(8,128)(2,1)S(1)}, u32[]{:S(2)}, u32[]{:S(2)}) collective-permute-start(bf16[128,1536]{1,0:T(8,128)(2,1)} %get-tuple-element.67), channel_id=1, source_target_pairs={{0,32},{32,0},{64,96},{96,64},{128,160},{160,128},{192,224},{224,1... | collective-permute-start | bytes 1179656 | tf_op jit(solution)/shard_map/ppermute | solution.py:41
  159.9 11.3 %collective-permute-start.26 = (bf16[128,1536]{1,0:T(8,128)(2,1)S(1)}, bf16[128,1536]{1,0:T(8,128)(2,1)S(1)}, u32[]{:S(2)}, u32[]{:S(2)}) collective-permute-start(bf16[128,1536]{1,0:T(8,128)(2,1)S(1)} %collective-permute-done.25), channel_id=1, source_target_pairs={{0,64},{32,96},{64,128},{96,160},{128,192},{160,224},{1,65},{33,97... | collective-permute-start | bytes 1179656 | tf_op jit(solution)/shard_map/ppermute | solution.py:37
  161.2 12.7 %collective-permute-start.28 = (bf16[128,1536]{1,0:T(8,128)(2,1)}, bf16[128,1536]{1,0:T(8,128)(2,1)S(1)}, u32[]{:S(2)}, u32[]{:S(2)}) collective-permute-start(bf16[128,1536]{1,0:T(8,128)(2,1)} %get-tuple-element.65), channel_id=1, source_target_pairs={{0,192},{32,224},{1,193},{33,225},{2,194},{34,226},{3,195},{35,227... | collective-permute-start | bytes 1179656 | tf_op jit(solution)/shard_map/ppermute | solution.py:37
  165.9 10.5 %copy-start.10 = (bf16[128,1536]{1,0:T(8,128)(2,1)S(1)}, bf16[128,1536]{1,0:T(8,128)(2,1)}, u32[]{:S(2)}) copy-start(bf16[128,1536]{1,0:T(8,128)(2,1)} %get-tuple-element.67) | copy-start | bytes 1179652
  174.1 3.6 %collective-permute-start.29 = (bf16[128,1536]{1,0:T(8,128)(2,1)S(1)}, bf16[128,1536]{1,0:T(8,128)(2,1)S(1)}, u32[]{:S(2)}, u32[]{:S(2)}) collective-permute-start(bf16[128,1536]{1,0:T(8,128)(2,1)S(1)} %add_convert_fusion), channel_id=1, source_target_pairs={{0,32},{32,0},{64,96},{96,64},{128,160},{160,128},{192,224},{224,1... | collective-permute-start | bytes 1179656 | tf_op jit(solution)/shard_map/ppermute | solution.py:41
  177.2 1.4 copy-start.5

commit v4 on v3

--- a/solution.py
+++ b/solution.py
@@ -14,7 +14,8 @@
 NORM_EPS = 1e-06
 F32 = jnp.float32
 BF16 = jnp.bfloat16
-VMEM_LIMIT = 56 * 1024 * 1024
+ATTEND_VMEM = 40 * 1024 * 1024
+OUTPUT_VMEM = 16 * 1024 * 1024
 
 
 def y_shift(block, distance):
@@ -71,6 +72,7 @@
         out_specs=pl.BlockSpec(memory_space=pltpu.VMEM),
         out_shape=jax.ShapeDtypeStruct((rows, width), BF16),
         scratch_shapes=[pltpu.VMEM((2, 1, width), F32), pltpu.SemaphoreType.DMA((2,))],
+        compiler_params=pltpu.CompilerParams(vmem_limit_bytes=OUTPUT_VMEM),
         name="modulate",
     )(where, step_index, latent, table)
 
@@ -201,7 +203,7 @@
             pltpu.SemaphoreType.DMA((11,)),
             pltpu.SemaphoreType.DMA((8,)),
         ],
-        compiler_params=pltpu.CompilerParams(vmem_limit_bytes=VMEM_LIMIT),
+        compiler_params=pltpu.CompilerParams(vmem_limit_bytes=ATTEND_VMEM),
         cost_estimate=pl.CostEstimate(
             flops=16_000_000_000, bytes_accessed=16_000_000, transcendentals=4_000_000
         ),
@@ -264,7 +266,7 @@
             pltpu.SemaphoreType.DMA((2,)),
         ],
         out_shape=[jax.ShapeDtypeStruct((half, width), BF16)] * 3,
-        compiler_params=pltpu.CompilerParams(vmem_limit_bytes=VMEM_LIMIT),
+        compiler_params=pltpu.CompilerParams(vmem_limit_bytes=OUTPUT_VMEM),
         name="output",
     )(where, step_index, step_sizes, keep, got, table, *pieces)
 
@@ -355,7 +357,7 @@
     )
     one = x_later(total, 1)
     three = x_later(total, 3)
-    two = x_later(one, 1)
+    two = x_later(total, 2)
     rest = core_swap(other)
     parts = (2, rows // 2, width)
     near_half = (jnp.arange(2, dtype=jnp.int32) == core)[:, None, None]

time: 181 us -> 169 us (0.934)
  waiting for transfers between devices: 78.3 us -> 69.5 us
  local copies, waits for them, and re-layouts: 8.04 us -> 16.3 us
  Pallas kernels: 35.3 us -> 27.5 us
  starting transfers between devices: 45.2 us -> 43.3 us
    ppermute x7, waiting for transfers between devices: 23.9 us -> 18.5 us  [y_shift(): return lax.ppermute(block, 'frame', pairs)]
    pallas_call x1, Pallas kernels: 27.8 us -> 24.3 us  [attend(): pl.pallas_call(attend_kernel, in_specs=[smem, smem, pl.BlockSpec(memory_s...]
    dynamic_update_slice x4, local copies, waits for them, and re-layouts: 0.1 us -> 2.93 us  [placed_y(): lax.dynamic_update_slice_in_dim(result, part, lax.rem(own + i, NY), 1)]
    pallas_call x1, Pallas kernels: 4.51 us -> 2 us  [output(): pl.pallas_call(output_kernel, in_specs=[smem, smem, smem, vmem, vmem] + [...]
    unnamed x46 -> x30, local copies, waits for them, and re-layouts: 1.96 us -> 4.16 us
    ppermute x3, waiting for transfers between devices: 18.7 us -> 16.6 us  [x_later(): return lax.ppermute(block, 'step', pairs)]
  transfers between devices with their start and end apart: 31 -> 31, of which waited for: 20 -> 18; matrix products, arithmetic and copies ran while one was open for 5% -> 8% of each run, Pallas kernels for 15% -> 14%
where the time goes in v4:
time: 169 us
  waiting for transfers between devices  69.5 us (41%)
  starting transfers between devices  43.3 us (26%)
  Pallas kernels  27.5 us (16%)
  local copies, waits for them, and re-layouts  16.3 us (10%)
  between operations  6.01 us (4%)
  other arithmetic  5.92 us (4%)
    ppermute x6, waiting for transfers between devices, z_shift(): return lax.ppermute(block, 'frame', pairs)  28.7 us
    pallas_call x1, Pallas kernels, attend(): pl.pallas_call(attend_kernel, in_specs=[smem, smem, pl.BlockSpec(memory_s...  24.3 us
    ppermute x7, waiting for transfers between devices, y_shift(): return lax.ppermute(block, 'frame', pairs)  18.5 us
    ppermute x3, waiting for transfers between devices, x_later(): return lax.ppermute(block, 'step', pairs)  16.6 us
    ppermute x7, starting transfers between devices, y_shift(): return lax.ppermute(block, 'frame', pairs)  10.1 us
    ppermute x8, starting transfers between devices, core_swap(): return lax.ppermute(block, 'step', [(i, i ^ 1) for i in range(2 * NX)])  9.92 us
    all_to_all x1, starting transfers between devices, on_device(): lax.all_to_all(jnp.broadcast_to(packed[None], (NZ,) + packed.shape), 'fra...  7.56 us
    ppermute x6, starting transfers between devices, z_shift(): return lax.ppermute(block, 'frame', pairs)  6.56 us
  transfers between devices with their start and end apart: 31, of which 18 were waited for; matrix products, arithmetic and copies ran while one was open for 8% of the time, Pallas kernels for 14%

profile of v4, /device:TPU:79, one launch (start us, length us, event | category | flops | bytes accessed | tf_op | source)
XLA Modules:
  0.0 168.5 jit_solution(10344036749162843598)
XLA Ops:
  0.7 1.2 copy-done
  1.9 1.1 copy-done.2
  3.1 0.7 copy-done.3
  3.7 1.2 modulate.1.refs_0_
  5.0 2.1 %collective-permute-start = (bf16[256,1536]{1,0:T(8,128)(2,1)S(1)}, bf16[256,1536]{1,0:T(8,128)(2,1)S(1)}, u32[]{:S(2)}, u32[]{:S(2)}) collective-permute-start(bf16[256,1536]{1,0:T(8,128)(2,1)S(1)} %modulate.1.refs_0_), channel_id=1, source_target_pairs={{0,2},{1,3},{2,0},{3,1},{4,6},{5,7},{6,4},{7,5},{8,10},{9,11},{10,... | collective-permute-start | bytes 2359304 | tf_op jit(solution)/shard_map/ppermute | solution.py:23
  7.1 0.7 broadcast_in_dim.75
  7.9 7.6 %all-to-all-start = ((bf16[8,8,2304]{2,1,0:T(8,128)(2,1)}), bf16[8,8,2304]{2,1,0:T(8,128)(2,1)S(1)}, u32[]{:S(2)}, u32[]{:S(2)}) async-start(bf16[8,8,2304]{2,1,0:T(8,128)(2,1)} %broadcast_in_dim.75), calls=%async_computation | async-start | bytes 589824 | tf_op jit(solution)/shard_map/all_to_all | solution.py:314
  15.4 0.6 fusion.2
  19.9 0.7 fusion.1
  20.6 2.6 %all-to-all-done = bf16[8,8,2304]{2,1,0:T(8,128)(2,1)S(1)} async-done(((bf16[8,8,2304]{2,1,0:T(8,128)(2,1)}), bf16[8,8,2304]{2,1,0:T(8,128)(2,1)S(1)}, u32[]{:S(2)}, u32[]{:S(2)}) %all-to-all-start) | async-done | bytes 294944 | tf_op jit(solution)/shard_map/all_to_all | solution.py:314
  23.2 1.7 %collective-permute-done.refs_3_ = bf16[256,1536]{1,0:T(8,128)(2,1)S(1)} collective-permute-done((bf16[256,1536]{1,0:T(8,128)(2,1)S(1)}, bf16[256,1536]{1,0:T(8,128)(2,1)S(1)}, u32[]{:S(2)}, u32[]{:S(2)}) %collective-permute-start) | collective-permute-done | bytes 786464 | tf_op jit(solution)/shard_map/ppermute | solution.py:23
  25.1 2.3 %collective-permute-start.2 = (bf16[64,2304]{1,0:T(8,128)(2,1)S(1)}, bf16[64,2304]{1,0:T(8,128)(2,1)S(1)}, u32[]{:S(2)}, u32[]{:S(2)}) collective-permute-start(bf16[64,2304]{1,0:T(8,128)(2,1)S(1)} %bitcast.41), channel_id=1, source_target_pairs={{0,2},{1,3},{2,0},{3,1},{4,6},{5,7},{6,4},{7,5},{8,10},{9,11},{10,... | collective-permute-start | bytes 884744 | tf_op jit(solution)/shard_map/ppermute | solution.py:23
  27.4 1.6 collective-permute-start.3
  29.0 1.6 collective-permute-start.4
  30.7 1.1 broadcast_in_dim.76
  31.8 0.7 bitcast_dynamic-update-slice_fusion.3
  32.5 0.7 bitcast_dynamic-update-slice_fusion.2
  33.2 6.0 %collective-permute-done.2 = bf16[64,2304]{1,0:T(8,128)(2,1)S(1)} collective-permute-done((bf16[64,2304]{1,0:T(8,128)(2,1)S(1)}, bf16[64,2304]{1,0:T(8,128)(2,1)S(1)}, u32[]{:S(2)}, u32[]{:S(2)}) %collective-permute-start.2) | collective-permute-done | bytes 294944 | tf_op jit(solution)/shard_map/ppermute | solution.py:23
  39.2 0.7 bitcast_dynamic-update-slice_fusion.1
  40.0 1.0 collective-permute-done.3
  41.0 0.7 bitcast_dynamic-update-slice_fusion
  41.7 4.0 %collective-permute-done.4.refs_1_ = bf16[256,1536]{1,0:T(8,128)(2,1)S(1)} collective-permute-done((bf16[256,1536]{1,0:T(8,128)(2,1)S(1)}, bf16[256,1536]{1,0:T(8,128)(2,1)S(1)}, u32[]{:S(2)}, u32[]{:S(2)}) %collective-permute-start.4) | collective-permute-done | bytes 786464 | tf_op jit(solution)/shard_map/ppermute | solution.py:28
  45.7 3.0 %collective-permute-done.5.refs_2_ = bf16[256,1536]{1,0:T(8,128)(2,1)S(1)} collective-permute-done((bf16[256,1536]{1,0:T(8,128)(2,1)S(1)}, bf16[256,1536]{1,0:T(8,128)(2,1)S(1)}, u32[]{:S(2)}, u32[]{:S(2)}) %collective-permute-start.5) | collective-permute-done | bytes 786464 | tf_op jit(solution)/shard_map/ppermute | solution.py:28
  48.7 1.5 reshape.60.refs_11_
  50.5 1.3 broadcast_select_fusion.1
  51.7 1.5 collective-permute-start.9
  53.2 2.4 %collective-permute-start.7 = (bf16[256,1536]{1,0:T(8,128)(2,1)S(1)}, bf16[256,1536]{1,0:T(8,128)(2,1)}, u32[]{:S(2)}, u32[]{:S(2)}) collective-permute-start(bf16[256,1536]{1,0:T(8,128)(2,1)S(1)} %collective-permute-done.4.refs_1_), channel_id=1, source_target_pairs={{0,4},{1,5},{2,6},{3,7},{4,8},{5,9},{6,10},{7,11},{8,12},{9,13},{1... | collective-permute-start | bytes 2359304 | tf_op jit(solution)/shard_map/ppermute | solution.py:28
  55.6 1.6 slice.13
  57.2 0.9 reshape.61
  58.1 9.4 %collective-permute-done.10.refs_7_ = bf16[256,1536]{1,0:T(8,128)(2,1)} collective-permute-done((bf16[256,1536]{1,0:T(8,128)(2,1)}, bf16[256,1536]{1,0:T(8,128)(2,1)}, u32[]{:S(2)}, u32[]{:S(2)}) %collective-permute-start.10) | collective-permute-done | bytes 786464 | tf_op jit(solution)/shard_map/ppermute | solution.py:23
  68.2 1.8 %collective-permute-done.8.refs_5_ = bf16[256,1536]{1,0:T(8,128)(2,1)} collective-permute-done((bf16[256,1536]{1,0:T(8,128)(2,1)S(1)}, bf16[256,1536]{1,0:T(8,128)(2,1)}, u32[]{:S(2)}, u32[]{:S(2)}) %collective-permute-start.8) | collective-permute-done | bytes 786464 | tf_op jit(solution)/shard_map/ppermute | solution.py:28
  70.0 1.3 collective-permute-start.11
  71.3 1.4 collective-permute-start.12
  72.8 2.4 %collective-permute-start.15 = (bf16[256,1536]{1,0:T(8,128)(2,1)S(1)}, bf16[256,1536]{1,0:T(8,128)(2,1)S(1)}, u32[]{:S(2)}, u32[]{:S(2)}) collective-permute-start(bf16[256,1536]{1,0:T(8,128)(2,1)S(1)} %broadcast_select_fusion), channel_id=1, source_target_pairs={{0,2},{1,3},{2,0},{3,1},{4,6},{5,7},{6,4},{7,5},{8,10},{9,11},{10,... | collective-permute-start | bytes 2359304 | tf_op jit(solution)/shard_map/ppermute | solution.py:23
  75.2 6.5 %collective-permute-start.16 = (bf16[96,1536]{1,0:T(8,128)(2,1)S(1)}, bf16[96,1536]{1,0:T(8,128)(2,1)S(1)}, u32[]{:S(2)}, u32[]{:S(2)}) collective-permute-start(bf16[96,1536]{1,0:T(8,128)(2,1)S(1)} %copy-done.11), channel_id=1, source_target_pairs={{0,32},{32,0},{64,96},{96,64},{128,160},{160,128},{192,224},{224,1... | collective-permute-start | bytes 884744 | tf_op jit(solution)/shard_map/ppermute | solution.py:42
  81.7 1.0 slice.14
  82.8 1.3 collective-permute-start.13
  84.1 1.0 slice.15
  85.1 1.2 collective-permute-start.14
  86.4 10.5 %collective-permute-done.13.refs_9_ = bf16[128,1536]{1,0:T(8,128)(2,1)S(1)} collective-permute-done((bf16[128,1536]{1,0:T(8,128)(2,1)S(1)}, bf16[128,1536]{1,0:T(8,128)(2,1)S(1)}, u32[]{:S(2)}, u32[]{:S(2)}) %collective-permute-start.13) | collective-permute-done | bytes 393248 | tf_op jit(solution)/shard_map/ppermute | solution.py:28
  96.9 0.8 collective-permute-start.17
  97.6 9.1 %collective-permute-done.14.refs_10_ = bf16[128,1536]{1,0:T(8,128)(2,1)S(1)} collective-permute-done((bf16[128,1536]{1,0:T(8,128)(2,1)S(1)}, bf16[128,1536]{1,0:T(8,128)(2,1)S(1)}, u32[]{:S(2)}, u32[]{:S(2)}) %collective-permute-start.14) | collective-permute-done | bytes 393248 | tf_op jit(solution)/shard_map/ppermute | solution.py:28
  106.8 0.6 collective-permute-start.18
  107.4 0.5 collective-permute-start.20
  108.0 1.5 collective-permute-start.23
  109.8 0.9 collective-permute-start.24
  110.7 1.2 collective-permute-done.20.refs_18_
  111.9 0.9 copy-done.14
  112.8 24.3 %attend.1 = (bf16[128,768]{1,0:T(8,128)(2,1)S(1)}, bf16[128,768]{1,0:T(8,128)(2,1)S(1)}) custom-call(s32[4]{0:T(128)S(1)} %pad_add_fusion.where_ref, s32[2,64]{1,0:T(2,128)S(1)} %copy-done.9, f32[2,768]{1,0:T(2,128)S(1)} %copy-done.8, bf16[256,1536]{1,0:T(8,128)(2,1)S(1)} %modulate.1.refs_0_, bf16[256,1536]{1,0:T(8,128)(2,1)S(1)} %collective-permute-done.4.refs_1_, ...), custom_call_target="tpu_custom_call" | custom-call | flops 16000000000 | bytes 16000000 | tf_op jit(solution)/shard_map/attend/pallas_call | solution.py:190
  137.1 0.5 collective-permute-start.21
  137.6 1.1 collective-permute-done.21.got_ref
  138.6 2.0 %output.1 = (bf16[128,1536]{1,0:T(8,128)(2,1)S(1)}, bf16[128,1536]{1,0:T(8,128)(2,1)S(1)}, bf16[128,1536]{1,0:T(8,128)(2,1)S(1)}) custom-call(s32[4]{0:T(128)S(1)} %pad_add_fusion.where_ref, s32[8]{0:T(128)S(1)} %copy-done.4, f32[50]{0:T(128)S(1)} %copy-done.5, bf16[128,768]{1,0:T(8,128)(2,1)S(1)} %get-tuple-element.62.keep_ref, ...), custom_call_target="tpu_custom_call" | custom-call | tf_op jit(solution)/shard_map/output/pallas_call | solution.py:258
  140.6 0.5 collective-permute-start.26
  141.1 1.3 collective-permute-start.25
  142.4 1.3 collective-permute-start.27
  143.7 1.3 collective-permute-start.28
  146.4 1.0 bitcast_select_fusion.1
  147.4 7.7 %collective-permute-done.25 = bf16[128,1536]{1,0:T(8,128)(2,1)S(1)} collective-permute-done((bf16[128,1536]{1,0:T(8,128)(2,1)S(1)}, bf16[128,1536]{1,0:T(8,128)(2,1)S(1)}, u32[]{:S(2)}, u32[]{:S(2)}) %collective-permute-start.25) | collective-permute-done | bytes 393248 | tf_op jit(solution)/shard_map/ppermute | solution.py:38
  155.1 8.9 %collective-permute-done.28 = bf16[128,1536]{1,0:T(8,128)(2,1)S(1)} collective-permute-done((bf16[128,1536]{1,0:T(8,128)(2,1)S(1)}, bf16[128,1536]{1,0:T(8,128)(2,1)S(1)}, u32[]{:S(2)}, u32[]{:S(2)}) %collective-permute-start.28) | collective-permute-done | bytes 393248 | tf_op jit(solution)/shard_map/ppermute | solution.py:38
  164.2 0.6 collective-permute-start.29
  164.8 0.9 multiply_add_fusion.1
  165.7 0.4 collective-permute-done.29
  166.1 0.8 multiply_add_fusion
  167.1 1.4 fusion
  (57 shorter events, 2.4 us)
Async XLA Ops:
  0.7 1.2 copy-start
  1.9 1.1 copy-start.2
  3.1 0.7 copy-start.3
  3.7 3.3 %copy-start.13 = (bf16[3,1536]{1,0:T(4,128)(2,1)S(1)}, bf16[3,1536]{1,0:T(4,128)(2,1)}, u32[]{:S(2)}) copy-start(bf16[3,1536]{1,0:T(4,128)(2,1)} %param.15) | copy-start | bytes 27652
  3.7 3.4 %copy-start.12 = (bf16[6,2304]{1,0:T(8,128)(2,1)S(1)}, bf16[6,2304]{1,0:T(8,128)(2,1)}, u32[]{:S(2)}) copy-start(bf16[6,2304]{1,0:T(8,128)(2,1)} %param.14) | copy-start | bytes 82948
  3.7 11.7 %copy-start.4 = (s32[8]{0:T(128)S(1)}, s32[8]{0:T(128)}, u32[]{:S(2)}) copy-start(s32[8]{0:T(128)} %index_ref.3) | copy-start | bytes 100
  3.7 16.2 %copy-start.5 = (f32[50]{0:T(128)S(1)}, f32[50]{0:T(128)}, u32[]{:S(2)}) copy-start(f32[50]{0:T(128)} %size_ref.1) | copy-start | bytes 604
  5.0 20.0 %collective-permute-start = (bf16[256,1536]{1,0:T(8,128)(2,1)S(1)}, bf16[256,1536]{1,0:T(8,128)(2,1)S(1)}, u32[]{:S(2)}, u32[]{:S(2)}) collective-permute-start(bf16[256,1536]{1,0:T(8,128)(2,1)S(1)} %modulate.1.refs_0_), channel_id=1, source_target_pairs={{0,2},{1,3},{2,0},{3,1},{4,6},{5,7},{6,4},{7,5},{8,10},{9,11},{10,... | collective-permute-start | bytes 2359304 | tf_op jit(solution)/shard_map/ppermute | solution.py:23
  7.9 15.3 %all-to-all-start = ((bf16[8,8,2304]{2,1,0:T(8,128)(2,1)}), bf16[8,8,2304]{2,1,0:T(8,128)(2,1)S(1)}, u32[]{:S(2)}, u32[]{:S(2)}) async-start(bf16[8,8,2304]{2,1,0:T(8,128)(2,1)} %broadcast_in_dim.75), calls=%async_computation | async-start | bytes 589824 | tf_op jit(solution)/shard_map/all_to_all | solution.py:314
  25.0 8.3 %copy-start.6 = (bf16[256,1536]{1,0:T(8,128)(2,1)}, bf16[256,1536]{1,0:T(8,128)(2,1)S(1)}, u32[]{:S(2)}) copy-start(bf16[256,1536]{1,0:T(8,128)(2,1)S(1)} %collective-permute-done.refs_3_) | copy-start | bytes 2359300
  25.0 7.6 %collective-permute-start.1 = (bf16[64,2304]{1,0:T(8,128)(2,1)S(1)}, bf16[64,2304]{1,0:T(8,128)(2,1)S(1)}, u32[]{:S(2)}, u32[]{:S(2)}) collective-permute-start(bf16[64,2304]{1,0:T(8,128)(2,1)S(1)} %bitcast.40), channel_id=1, source_target_pairs={{0,3},{1,0},{2,1},{3,2},{4,7},{5,4},{6,5},{7,6},{8,11},{9,8},{10,9... | collective-permute-start | bytes 884744 | tf_op jit(solution)/shard_map/ppermute | solution.py:23
  25.1 14.1 %collective-permute-start.2 = (bf16[64,2304]{1,0:T(8,128)(2,1)S(1)}, bf16[64,2304]{1,0:T(8,128)(2,1)S(1)}, u32[]{:S(2)}, u32[]{:S(2)}) collective-permute-start(bf16[64,2304]{1,0:T(8,128)(2,1)S(1)} %bitcast.41), channel_id=1, source_target_pairs={{0,2},{1,3},{2,0},{3,1},{4,6},{5,7},{6,4},{7,5},{8,10},{9,11},{10,... | collective-permute-start | bytes 884744 | tf_op jit(solution)/shard_map/ppermute | solution.py:23
  27.4 13.5 %collective-permute-start.3 = (bf16[64,2304]{1,0:T(8,128)(2,1)S(1)}, bf16[64,2304]{1,0:T(8,128)(2,1)S(1)}, u32[]{:S(2)}, u32[]{:S(2)}) collective-permute-start(bf16[64,2304]{1,0:T(8,128)(2,1)S(1)} %bitcast.42), channel_id=1, source_target_pairs={{0,1},{1,2},{2,3},{3,0},{4,5},{5,6},{6,7},{7,4},{8,9},{9,10},{10,1... | collective-permute-start | bytes 884744 | tf_op jit(solution)/shard_map/ppermute | solution.py:23
  29.0 16.6 %collective-permute-start.4 = (bf16[256,1536]{1,0:T(8,128)(2,1)S(1)}, bf16[256,1536]{1,0:T(8,128)(2,1)S(1)}, u32[]{:S(2)}, u32[]{:S(2)}) collective-permute-start(bf16[256,1536]{1,0:T(8,128)(2,1)S(1)} %modulate.1.refs_0_), channel_id=1, source_target_pairs={{0,4},{1,5},{2,6},{3,7},{4,8},{5,9},{6,10},{7,11},{8,12},{9,13},{1... | collective-permute-start | bytes 2359304 | tf_op jit(solution)/shard_map/ppermute | solution.py:28
  30.7 18.0 %collective-permute-start.5 = (bf16[256,1536]{1,0:T(8,128)(2,1)S(1)}, bf16[256,1536]{1,0:T(8,128)(2,1)S(1)}, u32[]{:S(2)}, u32[]{:S(2)}) collective-permute-start(bf16[256,1536]{1,0:T(8,128)(2,1)S(1)} %modulate.1.refs_0_), channel_id=1, source_target_pairs={{0,28},{1,29},{2,30},{3,31},{4,0},{5,1},{6,2},{7,3},{8,4},{9,5},{1... | collective-permute-start | bytes 2359304 | tf_op jit(solution)/shard_map/ppermute | solution.py:28
  50.2 19.9 %collective-permute-start.6 = (bf16[192,2304]{1,0:T(8,128)(2,1)S(1)}, bf16[192,2304]{1,0:T(8,128)(2,1)}, u32[]{:S(2)}, u32[]{:S(2)}) collective-permute-start(bf16[192,2304]{1,0:T(8,128)(2,1)S(1)} %reshape.60.refs_11_), channel_id=1, source_target_pairs={{0,64},{32,96},{64,128},{96,160},{128,192},{160,224},{192,0},{224,... | collective-permute-start | bytes 2654216 | tf_op jit(solution)/shard_map/ppermute | solution.py:33
  51.7 15.8 %collective-permute-start.10 = (bf16[256,1536]{1,0:T(8,128)(2,1)}, bf16[256,1536]{1,0:T(8,128)(2,1)}, u32[]{:S(2)}, u32[]{:S(2)}) collective-permute-start(bf16[256,1536]{1,0:T(8,128)(2,1)} %get-tuple-element.76), channel_id=1, source_target_pairs={{0,3},{1,0},{2,1},{3,2},{4,7},{5,4},{6,5},{7,6},{8,11},{9,8},{10,9... | collective-permute-start | bytes 2359304 | tf_op jit(solution)/shard_map/ppermute | solution.py:23
  51.7 16.1 %collective-permute-start.9 = (bf16[256,1536]{1,0:T(8,128)(2,1)}, bf16[256,1536]{1,0:T(8,128)(2,1)}, u32[]{:S(2)}, u32[]{:S(2)}) collective-permute-start(bf16[256,1536]{1,0:T(8,128)(2,1)} %get-tuple-element.77), channel_id=1, source_target_pairs={{0,1},{1,2},{2,3},{3,0},{4,5},{5,6},{6,7},{7,4},{8,9},{9,10},{10,1... | collective-permute-start | bytes 2359304 | tf_op jit(solution)/shard_map/ppermute | solution.py:23
  53.2 15.0 %collective-permute-start.7 = (bf16[256,1536]{1,0:T(8,128)(2,1)S(1)}, bf16[256,1536]{1,0:T(8,128)(2,1)}, u32[]{:S(2)}, u32[]{:S(2)}) collective-permute-start(bf16[256,1536]{1,0:T(8,128)(2,1)S(1)} %collective-permute-done.4.refs_1_), channel_id=1, source_target_pairs={{0,4},{1,5},{2,6},{3,7},{4,8},{5,9},{6,10},{7,11},{8,12},{9,13},{1... | collective-permute-start | bytes 2359304 | tf_op jit(solution)/shard_map/ppermute | solution.py:28
  55.6 14.4 %collective-permute-start.8 = (bf16[256,1536]{1,0:T(8,128)(2,1)S(1)}, bf16[256,1536]{1,0:T(8,128)(2,1)}, u32[]{:S(2)}, u32[]{:S(2)}) collective-permute-start(bf16[256,1536]{1,0:T(8,128)(2,1)S(1)} %collective-permute-done.5.refs_2_), channel_id=1, source_target_pairs={{0,28},{1,29},{2,30},{3,31},{4,0},{5,1},{6,2},{7,3},{8,4},{9,5},{1... | collective-permute-start | bytes 2359304 | tf_op jit(solution)/shard_map/ppermute | solution.py:28
  58.1 17.2 %copy-start.11 = (bf16[96,1536]{1,0:T(8,128)(2,1)S(1)}, bf16[96,1536]{1,0:T(8,128)(2,1)}, u32[]{:S(2)}) copy-start(bf16[96,1536]{1,0:T(8,128)(2,1)} %reshape.61) | copy-start | bytes 884740
  70.0 37.3 %collective-permute-start.11 = (bf16[192,2304]{1,0:T(8,128)(2,1)S(1)}, bf16[192,2304]{1,0:T(8,128)(2,1)S(1)}, u32[]{:S(2)}, u32[]{:S(2)}) collective-permute-start(bf16[192,2304]{1,0:T(8,128)(2,1)S(1)} %reshape.60.refs_11_), channel_id=1, source_target_pairs={{0,192},{32,224},{64,0},{96,32},{128,64},{160,96},{192,128},{224,1... | collective-permute-start | bytes 2654216 | tf_op jit(solution)/shard_map/ppermute | solution.py:33
  71.3 36.0 %collective-permute-start.12 = (bf16[192,2304]{1,0:T(8,128)(2,1)}, bf16[192,2304]{1,0:T(8,128)(2,1)S(1)}, u32[]{:S(2)}, u32[]{:S(2)}) collective-permute-start(bf16[192,2304]{1,0:T(8,128)(2,1)} %collective-permute-done.6.refs_12_), channel_id=1, source_target_pairs={{0,64},{32,96},{64,128},{96,160},{128,192},{160,224},{192,0},{224,... | collective-permute-start | bytes 2654216 | tf_op jit(solution)/shard_map/ppermute | solution.py:33
  72.8 34.5 %collective-permute-start.15 = (bf16[256,1536]{1,0:T(8,128)(2,1)S(1)}, bf16[256,1536]{1,0:T(8,128)(2,1)S(1)}, u32[]{:S(2)}, u32[]{:S(2)}) collective-permute-start(bf16[256,1536]{1,0:T(8,128)(2,1)S(1)} %broadcast_select_fusion), channel_id=1, source_target_pairs={{0,2},{1,3},{2,0},{3,1},{4,6},{5,7},{6,4},{7,5},{8,10},{9,11},{10,... | collective-permute-start | bytes 2359304 | tf_op jit(solution)/shard_map/ppermute | solution.py:23
  75.2 9.8 %collective-permute-start.16 = (bf16[96,1536]{1,0:T(8,128)(2,1)S(1)}, bf16[96,1536]{1,0:T(8,128)(2,1)S(1)}, u32[]{:S(2)}, u32[]{:S(2)}) collective-permute-start(bf16[96,1536]{1,0:T(8,128)(2,1)S(1)} %copy-done.11), channel_id=1, source_target_pairs={{0,32},{32,0},{64,96},{96,64},{128,160},{160,128},{192,224},{224,1... | collective-permute-start | bytes 884744 | tf_op jit(solution)/shard_map/ppermute | solution.py:42
  82.7 30.1 %copy-start.7 = (bf16[256,1536]{1,0:T(8,128)(2,1)S(1)}, bf16[256,1536]{1,0:T(8,128)(2,1)}, u32[]{:S(2)}) copy-start(bf16[256,1536]{1,0:T(8,128)(2,1)} %copy-done.6) | copy-start | bytes 2359300
  82.7 30.1 %copy-start.8 = (f32[2,768]{1,0:T(2,128)S(1)}, f32[2,768]{1,0:T(2,128)}, u32[]{:S(2)}) copy-start(f32[2,768]{1,0:T(2,128)} %gain_ref.1) | copy-start | bytes 18436
  82.8 30.1 %copy-start.9 = (s32[2,64]{1,0:T(2,128)S(1)}, s32[2,64]{1,0:T(2,128)}, u32[]{:S(2)}) copy-start(s32[2,64]{1,0:T(2,128)} %mask_ref.1) | copy-start | bytes 1540
  82.8 14.1 %collective-permute-start.13 = (bf16[128,1536]{1,0:T(8,128)(2,1)S(1)}, bf16[128,1536]{1,0:T(8,128)(2,1)S(1)}, u32[]{:S(2)}, u32[]{:S(2)}) collective-permute-start(bf16[128,1536]{1,0:T(8,128)(2,1)S(1)} %slice.14), channel_id=1, source_target_pairs={{0,8},{1,9},{2,10},{3,11},{4,12},{5,13},{6,14},{7,15},{8,16},{9,17... | collective-permute-start | bytes 1179656 | tf_op jit(solution)/shard_map/ppermute | solution.py:28
  85.1 21.7 %collective-permute-start.14 = (bf16[128,1536]{1,0:T(8,128)(2,1)S(1)}, bf16[128,1536]{1,0:T(8,128)(2,1)S(1)}, u32[]{:S(2)}, u32[]{:S(2)}) collective-permute-start(bf16[128,1536]{1,0:T(8,128)(2,1)S(1)} %slice.15), channel_id=1, source_target_pairs={{0,24},{1,25},{2,26},{3,27},{4,28},{5,29},{6,30},{7,31},{8,0},{9,1... | collective-permute-start | bytes 1179656 | tf_op jit(solution)/shard_map/ppermute | solution.py:28
  86.4 52.3 %copy-start.1 = (f32[50,3,1536]{2,0,1:T(8,128)S(1)}, f32[50,3,1536]{2,0,1:T(8,128)}, u32[]{:S(2)}) copy-start(f32[50,3,1536]{2,0,1:T(8,128)} %param.12) | copy-start | bytes 2764804
  96.9 11.1 %collective-permute-start.17 = (bf16[192,2304]{1,0:T(8,128)(2,1)S(1)}, bf16[192,2304]{1,0:T(8,128)(2,1)S(1)}, u32[]{:S(2)}, u32[]{:S(2)}) collective-permute-start(bf16[192,2304]{1,0:T(8,128)(2,1)S(1)} %reshape.60.refs_11_), channel_id=1, source_target_pairs={{0,32},{32,0},{64,96},{96,64},{128,160},{160,128},{192,224},{224,1... | collective-permute-start | bytes 2654216 | tf_op jit(solution)/shard_map/ppermute | solution.py:42
  106.8 3.0 %collective-permute-start.18 = (bf16[192,2304]{1,0:T(8,128)(2,1)}, bf16[192,2304]{1,0:T(8,128)(2,1)S(1)}, u32[]{:S(2)}, u32[]{:S(2)}) collective-permute-start(bf16[192,2304]{1,0:T(8,128)(2,1)} %collective-permute-done.6.refs_12_), channel_id=1, source_target_pairs={{0,32},{32,0},{64,96},{96,64},{128,160},{160,128},{192,224},{224,1... | collective-permute-start | bytes 2654216 | tf_op jit(solution)/shard_map/ppermute | solution.py:42
  107.3 3.3 %collective-permute-start.19 = (bf16[192,2304]{1,0:T(8,128)(2,1)S(1)}, bf16[192,2304]{1,0:T(8,128)(2,1)S(1)}, u32[]{:S(2)}, u32[]{:S(2)}) collective-permute-start(bf16[192,2304]{1,0:T(8,128)(2,1)S(1)} %collective-permute-done.11.refs_13_), channel_id=1, source_target_pairs={{0,32},{32,0},{64,96},{96,64},{128,160},{160,128},{192,224},{224,1... | collective-permute-start | bytes 2654216 | tf_op jit(solution)/shard_map/ppermute | solution.py:42
  107.4 4.5 %collective-permute-start.20 = (bf16[192,2304]{1,0:T(8,128)(2,1)S(1)}, bf16[192,2304]{1,0:T(8,128)(2,1)S(1)}, u32[]{:S(2)}, u32[]{:S(2)}) collective-permute-start(bf16[192,2304]{1,0:T(8,128)(2,1)S(1)} %collective-permute-done.12.refs_14_), channel_id=1, source_target_pairs={{0,32},{32,0},{64,96},{96,64},{128,160},{160,128},{192,224},{224,1... | collective-permute-start | bytes 2654216 | tf_op jit(solution)/shard_map/ppermute | solution.py:42
  107.9 29.6 %collective-permute-start.22 = (bf16[2,96,1536]{2,1,0:T(8,128)(2,1)S(1)}, bf16[2,96,1536]{2,1,0:T(8,128)(2,1)S(1)}, u32[]{:S(2)}, u32[]{:S(2)}) collective-permute-start(bf16[2,96,1536]{2,1,0:T(8,128)(2,1)S(1)} %pad_maximum_fusion.refs_0_), channel_id=1, source_target_pairs={{0,64},{32,96},{64,128},{96,160},{128,192},{160,224},{192,0},{224,... | collective-permute-start | bytes 1769480 | tf_op jit(solution)/shard_map/ppermute | solution.py:33
  108.0 29.6 %collective-permute-start.23 = (bf16[2,96,1536]{2,1,0:T(8,128)(2,1)S(1)}, bf16[2,96,1536]{2,1,0:T(8,128)(2,1)S(1)}, u32[]{:S(2)}, u32[]{:S(2)}) collective-permute-start(bf16[2,96,1536]{2,1,0:T(8,128)(2,1)S(1)} %pad_maximum_fusion.refs_0_), channel_id=1, source_target_pairs={{0,192},{32,224},{64,0},{96,32},{128,64},{160,96},{192,128},{224,1... | collective-permute-start | bytes 1769480 | tf_op jit(solution)/shard_map/ppermute | solution.py:33
  109.8 27.8 %collective-permute-start.24 = (bf16[2,96,1536]{2,1,0:T(8,128)(2,1)S(1)}, bf16[2,96,1536]{2,1,0:T(8,128)(2,1)S(1)}, u32[]{:S(2)}, u32[]{:S(2)}) collective-permute-start(bf16[2,96,1536]{2,1,0:T(8,128)(2,1)S(1)} %pad_maximum_fusion.refs_0_), channel_id=1, source_target_pairs={{0,128},{32,160},{64,192},{96,224},{128,0},{160,32},{192,64},{224,... | collective-permute-start | bytes 1769480 | tf_op jit(solution)/shard_map/ppermute | solution.py:33
  111.9 0.9 copy-start.14
  137.1 1.5 collective-permute-start.21
  140.6 5.7 %collective-permute-start.26 = (bf16[128,1536]{1,0:T(8,128)(2,1)S(1)}, bf16[128,1536]{1,0:T(8,128)(2,1)S(1)}, u32[]{:S(2)}, u32[]{:S(2)}) collective-permute-start(bf16[128,1536]{1,0:T(8,128)(2,1)S(1)} %get-tuple-element.67), channel_id=1, source_target_pairs={{0,32},{32,0},{64,96},{96,64},{128,160},{160,128},{192,224},{224,1... | collective-permute-start | bytes 1179656 | tf_op jit(solution)/shard_map/ppermute | solution.py:42
  141.1 14.0 %collective-permute-start.25 = (bf16[128,1536]{1,0:T(8,128)(2,1)S(1)}, bf16[128,1536]{1,0:T(8,128)(2,1)S(1)}, u32[]{:S(2)}, u32[]{:S(2)}) collective-permute-start(bf16[128,1536]{1,0:T(8,128)(2,1)S(1)} %get-tuple-element.65), channel_id=1, source_target_pairs={{0,128},{32,160},{64,192},{96,224},{1,129},{33,161},{65,193},{97,2... | collective-permute-start | bytes 1179656 | tf_op jit(solution)/shard_map/ppermute | solution.py:38
  142.4 12.7 %collective-permute-start.27 = (bf16[128,1536]{1,0:T(8,128)(2,1)S(1)}, bf16[128,1536]{1,0:T(8,128)(2,1)S(1)}, u32[]{:S(2)}, u32[]{:S(2)}) collective-permute-start(bf16[128,1536]{1,0:T(8,128)(2,1)S(1)} %get-tuple-element.65), channel_id=1, source_target_pairs={{0,64},{32,96},{64,128},{96,160},{128,192},{160,224},{1,65},{33,97... | collective-permute-start | bytes 1179656 | tf_op jit(solution)/shard_map/ppermute | solution.py:38
  143.7 20.3 %collective-permute-start.28 = (bf16[128,1536]{1,0:T(8,128)(2,1)S(1)}, bf16[128,1536]{1,0:T(8,128)(2,1)S(1)}, u32[]{:S(2)}, u32[]{:S(2)}) collective-permute-start(bf16[128,1536]{1,0:T(8,128)(2,1)S(1)} %get-tuple-element.65), channel_id=1, source_target_pairs={{0,192},{32,224},{1,193},{33,225},{2,194},{34,226},{3,195},{35,227... | collective-permute-start | bytes 1179656 | tf_op jit(solution)/shard_map/ppermute | solution.py:38
  164.2 1.9 %collective-permute-start.29 = (bf16[128,1536]{1,0:T(8,128)(2,1)S(1)}, bf16[128,1536]{1,0:T(8,128)(2,1)S(1)}, u32[]{:S(2)}, u32[]{:S(2)}) collective-permute-start(bf16[128,1536]{1,0:T(8,128)(2,1)S(1)} %add_convert_fusion), channel_id=1, source_target_pairs={{0,32},{32,0},{64,96},{96,64},{128,160},{160,128},{192,224},{224,1... | collective-permute-start | bytes 1179656 | tf_op jit(solution)/shard_map/ppermute | solution.py:42
  165.7 1.4 copy-start.10

commit v5 on v4

--- a/solution.py
+++ b/solution.py
@@ -304,22 +304,16 @@
     size_other = step_sizes[step_index[step + 1 - 2 * core]]
 
     out_width = output_weight.shape[1]
+    two_raw = y_shift(latent, 2)
+    packed = jnp.concatenate([input_weight, output_weight.reshape(2, -1)], axis=0)
+    packed = jnp.broadcast_to(packed[None], (NZ,) + packed.shape)
+    packed, latent = lax.optimization_barrier((packed, latent))
+    columns_z = [[NY * i + j for i in range(NZ)] for j in range(NY)]
+    column = lax.all_to_all(packed, "frame", 0, 0, axis_index_groups=columns_z)
+    column = column.reshape(8 * NZ, -1)
     modulated = modulate(where_am_i, step_index, latent, table)
-    input_weight, output_weight, modulated = lax.optimization_barrier(
-        (input_weight, output_weight, modulated)
-    )
-    two_a = y_shift(modulated, 2)
-    packed = jnp.concatenate([input_weight, output_weight.reshape(2, -1)], axis=0)
-    columns_z = [[NY * i + j for i in range(NZ)] for j in range(NY)]
-    column = lax.all_to_all(
-        jnp.broadcast_to(packed[None], (NZ,) + packed.shape),
-        "frame",
-        0,
-        0,
-        axis_index_groups=columns_z,
-    ).reshape(8 * NZ, -1)
-    column, modulated, two_a, size_own, size_other = lax.optimization_barrier(
-        (column, modulated, two_a, size_own, size_other)
+    column, modulated, two_raw, size_own, size_other = lax.optimization_barrier(
+        (column, modulated, two_raw, size_own, size_other)
     )
 
     zp, zm = z_shift(modulated, 1), z_shift(modulated, -1)
@@ -332,8 +326,9 @@
     zp2, zm2 = z_shift(zp, 1), z_shift(zm, -1)
     before = y_shift(jnp.where(y == NY - 1, zp, modulated), 1)
     after = y_shift(jnp.where(y == 0, zm, modulated), -1)
-    in_rows, out_rows, left, zp2, zm2, zp, zm, before, after = lax.optimization_barrier(
-        (in_rows, out_rows, left, zp2, zm2, zp, zm, before, after)
+    two_a = modulate(where_am_i, step_index, two_raw, table)
+    in_rows, out_rows, left, zp2, zm2, zp, zm, before, after, two_a = lax.optimization_barrier(
+        (in_rows, out_rows, left, zp2, zm2, zp, zm, before, after, two_a)
     )
 
     right, far = x_shift(in_rows, -1), x_shift(left, 1)
@@ -361,18 +356,17 @@
     rest = core_swap(other)
     parts = (2, rows // 2, width)
     near_half = (jnp.arange(2, dtype=jnp.int32) == core)[:, None, None]
-    own32 = own.astype(F32)
-    velocity = jnp.where(near_half, own[None], rest[None]).reshape(rows, width)
-    two, velocity = lax.optimization_barrier((two, velocity))
+    odd = jnp.where(core == 1, size_other, 0.0)
     even = jnp.where(core == 0, size_own, 0.0)
-    odd = jnp.where(core == 1, size_other, 0.0)
+    velocity = jnp.where(near_half, own[None], rest[None])
+    inner = jnp.where(near_half, odd * other.astype(F32)[None], 0.0)
+    base = anchor.reshape(parts) + inner + size_own * velocity.astype(F32)
+    two, velocity, base = lax.optimization_barrier((two, velocity.reshape(rows, width), base))
     sums = one.astype(F32) + two.astype(F32) + three.astype(F32)
-    earlier = core_swap((sums + even * own32).astype(BF16))
-    one, two, three, own = lax.optimization_barrier((one, two, three, own))
+    earlier = core_swap((sums + even * own.astype(F32)).astype(BF16))
+    one, two, three = lax.optimization_barrier((one, two, three))
     sums = one.astype(F32) + two.astype(F32) + three.astype(F32)
-    own_part = sums + odd * other.astype(F32) + size_own * own.astype(F32)
-    rest_part = earlier.astype(F32) + size_own * rest.astype(F32)
-    advanced = anchor.reshape(parts) + jnp.where(near_half, own_part[None], rest_part[None])
+    advanced = base + jnp.where(near_half, sums[None], earlier.astype(F32)[None])
     advanced = advanced.reshape(rows, width)
     return (velocity[None], advanced[None])
 

time: 169 us -> 175 us (1.036)
  local copies, waits for them, and re-layouts: 16.3 us -> 27.1 us
  waiting for transfers between devices: 69.5 us -> 60.7 us
  Pallas kernels: 27.5 us -> 30.9 us
    unnamed x30 -> x46, local copies, waits for them, and re-layouts: 4.16 us -> 14 us
    ppermute x7, waiting for transfers between devices: 18.5 us -> 15 us  [y_shift(): return lax.ppermute(block, 'frame', pairs)]
    all_to_all x1, waiting for transfers between devices: 2.62 us -> 0.01 us  [on_device(): column = lax.all_to_all(packed, 'frame', 0, 0, axis_index_groups=columns_z)]
    dynamic_update_slice x4, local copies, waits for them, and re-layouts: 2.93 us -> 1.06 us  [placed_y(): lax.dynamic_update_slice_in_dim(result, part, lax.rem(own + i, NY), 1)]
    ppermute x6, waiting for transfers between devices: 28.7 us -> 26.9 us  [z_shift(): return lax.ppermute(block, 'frame', pairs)]
  transfers between devices with their start and end apart: 31 -> 31, of which waited for: 18 -> 16; matrix products, arithmetic and copies ran while one was open for 8% -> 9% of each run, Pallas kernels for 14% -> 16%
where the time goes in v5:
time: 175 us; the launch traced here: 174 us
  waiting for transfers between devices  60.7 us (35%)
  starting transfers between devices  42.4 us (24%)
  Pallas kernels  30.9 us (18%)
  local copies, waits for them, and re-layouts  27.1 us (15%)
  other arithmetic  7.11 us (4%)
  between operations  5.96 us (3%)
    ppermute x6, waiting for transfers between devices, z_shift(): return lax.ppermute(block, 'frame', pairs)  26.9 us
    pallas_call x1, Pallas kernels, attend(): pl.pallas_call(attend_kernel, in_specs=[smem, smem, pl.BlockSpec(memory_s...  25.5 us
    ppermute x3, waiting for transfers between devices, x_later(): return lax.ppermute(block, 'step', pairs)  15.1 us
    ppermute x7, waiting for transfers between devices, y_shift(): return lax.ppermute(block, 'frame', pairs)  15 us
    unnamed x46, local copies, waits for them, and re-layouts  14 us
    ppermute x8, starting transfers between devices, core_swap(): return lax.ppermute(block, 'step', [(i, i ^ 1) for i in range(2 * NX)])  9.64 us
    ppermute x7, starting transfers between devices, y_shift(): return lax.ppermute(block, 'frame', pairs)  9.27 us
    all_to_all x1, starting transfers between devices, on_device(): column = lax.all_to_all(packed, 'frame', 0, 0, axis_index_groups=columns_z)  7.69 us
  transfers between devices with their start and end apart: 31, of which 16 were waited for; matrix products, arithmetic and copies ran while one was open for 9% of the time, Pallas kernels for 16%

profile of v5, /device:TPU:79, one launch (start us, length us, event | category | flops | bytes accessed | tf_op | source)
XLA Modules:
  0.0 174.2 jit_solution(9876004614528272437)
XLA Ops:
  0.6 2.1 %collective-permute-start = (bf16[256,1536]{1,0:T(8,128)(2,1)}, bf16[256,1536]{1,0:T(8,128)(2,1)S(1)}, u32[]{:S(2)}, u32[]{:S(2)}) collective-permute-start(bf16[256,1536]{1,0:T(8,128)(2,1)} %bitcast.34), channel_id=1, source_target_pairs={{0,2},{1,3},{2,0},{3,1},{4,6},{5,7},{6,4},{7,5},{8,10},{9,11},{10,... | collective-permute-start | bytes 2359304 | tf_op jit(solution)/shard_map/ppermute | solution.py:23
  3.5 0.8 pad_maximum_fusion.1
  4.3 0.7 broadcast_in_dim.92
  5.0 7.7 %all-to-all-start = ((bf16[8,8,2304]{2,1,0:T(8,128)(2,1)}), bf16[8,8,2304]{2,1,0:T(8,128)(2,1)}, u32[]{:S(2)}, u32[]{:S(2)}) async-start(bf16[8,8,2304]{2,1,0:T(8,128)(2,1)} %broadcast_in_dim.92), calls=%async_computation | async-start | bytes 589824 | tf_op jit(solution)/shard_map/all_to_all | solution.py:312
  12.7 1.3 fusion.1
  18.0 1.1 copy-done.2
  19.8 1.2 modulate.2.refs_0_
  21.6 0.9 copy-done.3
  22.5 1.1 collective-permute-start.1
  23.5 0.8 collective-permute-start.2
  24.3 1.6 collective-permute-start.3
  25.9 1.6 collective-permute-start.4
  27.6 1.0 bitcast_dynamic-update-slice_fusion.3
  29.0 7.5 %collective-permute-done.2 = bf16[64,2304]{1,0:T(8,128)(2,1)S(1)} collective-permute-done((bf16[64,2304]{1,0:T(8,128)(2,1)}, bf16[64,2304]{1,0:T(8,128)(2,1)S(1)}, u32[]{:S(2)}, u32[]{:S(2)}) %collective-permute-start.2) | collective-permute-done | bytes 294944 | tf_op jit(solution)/shard_map/ppermute | solution.py:23
  36.5 2.3 %collective-permute-done.3 = bf16[64,2304]{1,0:T(8,128)(2,1)S(1)} collective-permute-done((bf16[64,2304]{1,0:T(8,128)(2,1)}, bf16[64,2304]{1,0:T(8,128)(2,1)S(1)}, u32[]{:S(2)}, u32[]{:S(2)}) %collective-permute-start.3) | collective-permute-done | bytes 294944 | tf_op jit(solution)/shard_map/ppermute | solution.py:23
  38.8 3.4 %collective-permute-done.4.refs_1_ = bf16[256,1536]{1,0:T(8,128)(2,1)S(1)} collective-permute-done((bf16[256,1536]{1,0:T(8,128)(2,1)S(1)}, bf16[256,1536]{1,0:T(8,128)(2,1)S(1)}, u32[]{:S(2)}, u32[]{:S(2)}) %collective-permute-start.4) | collective-permute-done | bytes 786464 | tf_op jit(solution)/shard_map/ppermute | solution.py:28
  42.3 3.2 %collective-permute-done.5.refs_2_ = bf16[256,1536]{1,0:T(8,128)(2,1)S(1)} collective-permute-done((bf16[256,1536]{1,0:T(8,128)(2,1)S(1)}, bf16[256,1536]{1,0:T(8,128)(2,1)S(1)}, u32[]{:S(2)}, u32[]{:S(2)}) %collective-permute-start.5) | collective-permute-done | bytes 786464 | tf_op jit(solution)/shard_map/ppermute | solution.py:28
  45.5 2.3 %reshape.52.refs_11_ = bf16[192,2304]{1,0:T(8,128)(2,1)} reshape(bf16[8,4,6,2304]{3,2,1,0:T(8,128)(2,1)} %bitcast.36) | data formatting | bytes 1769472 | tf_op jit(solution)/shard_map/reshape | solution.py:322
  48.0 1.3 broadcast_select_fusion.1
  49.2 1.5 collective-permute-start.9
  50.7 2.4 %collective-permute-start.7 = (bf16[256,1536]{1,0:T(8,128)(2,1)S(1)}, bf16[256,1536]{1,0:T(8,128)(2,1)}, u32[]{:S(2)}, u32[]{:S(2)}) collective-permute-start(bf16[256,1536]{1,0:T(8,128)(2,1)S(1)} %collective-permute-done.4.refs_1_), channel_id=1, source_target_pairs={{0,4},{1,5},{2,6},{3,7},{4,8},{5,9},{6,10},{7,11},{8,12},{9,13},{1... | collective-permute-start | bytes 2359304 | tf_op jit(solution)/shard_map/ppermute | solution.py:28
  53.1 1.1 copy-done.4
  54.2 1.2 modulate.3.refs_3_
  55.4 0.9 copy-done.5
  56.3 2.3 %slice.13 = bf16[8,4,2,2304]{3,2,1,0:T(2,128)(2,1)} slice(bf16[8,4,8,2304]{3,2,1,0:T(8,128)(2,1)} %copy-done.20), slice={[0:8], [0:4], [6:8], [0:2304]} | slice | bytes 589824 | tf_op jit(solution)/shard_map/slice | solution.py:323
  58.6 1.9 %reshape.53 = bf16[96,1536]{1,0:T(8,128)(2,1)} reshape(bf16[8,4,2,2304]{3,2,1,0:T(2,128)(2,1)} %slice.13) | data formatting | bytes 589824 | tf_op jit(solution)/shard_map/reshape | solution.py:323
  60.5 4.5 %collective-permute-done.10.refs_7_ = bf16[256,1536]{1,0:T(8,128)(2,1)} collective-permute-done((bf16[256,1536]{1,0:T(8,128)(2,1)}, bf16[256,1536]{1,0:T(8,128)(2,1)}, u32[]{:S(2)}, u32[]{:S(2)}) %collective-permute-start.10) | collective-permute-done | bytes 786464 | tf_op jit(solution)/shard_map/ppermute | solution.py:23
  65.7 1.8 %collective-permute-done.8.refs_5_ = bf16[256,1536]{1,0:T(8,128)(2,1)} collective-permute-done((bf16[256,1536]{1,0:T(8,128)(2,1)S(1)}, bf16[256,1536]{1,0:T(8,128)(2,1)}, u32[]{:S(2)}, u32[]{:S(2)}) %collective-permute-start.8) | collective-permute-done | bytes 786464 | tf_op jit(solution)/shard_map/ppermute | solution.py:28
  67.5 1.3 collective-permute-start.11
  68.8 1.4 collective-permute-start.12
  70.3 2.3 %collective-permute-start.15 = (bf16[256,1536]{1,0:T(8,128)(2,1)S(1)}, bf16[256,1536]{1,0:T(8,128)(2,1)S(1)}, u32[]{:S(2)}, u32[]{:S(2)}) collective-permute-start(bf16[256,1536]{1,0:T(8,128)(2,1)S(1)} %broadcast_select_fusion), channel_id=1, source_target_pairs={{0,2},{1,3},{2,0},{3,1},{4,6},{5,7},{6,4},{7,5},{8,10},{9,11},{10,... | collective-permute-start | bytes 2359304 | tf_op jit(solution)/shard_map/ppermute | solution.py:23
  72.6 6.5 %collective-permute-start.16 = (bf16[96,1536]{1,0:T(8,128)(2,1)S(1)}, bf16[96,1536]{1,0:T(8,128)(2,1)S(1)}, u32[]{:S(2)}, u32[]{:S(2)}) collective-permute-start(bf16[96,1536]{1,0:T(8,128)(2,1)S(1)} %copy-done.22), channel_id=1, source_target_pairs={{0,32},{32,0},{64,96},{96,64},{128,160},{160,128},{192,224},{224,1... | collective-permute-start | bytes 884744 | tf_op jit(solution)/shard_map/ppermute | solution.py:42
  79.1 1.0 slice.14
  80.1 1.3 collective-permute-start.13
  81.4 1.0 slice.15
  82.4 1.2 collective-permute-start.14
  83.6 0.9 pad_maximum_fusion.refs_0_
  84.5 9.6 %collective-permute-done.13.refs_9_ = bf16[128,1536]{1,0:T(8,128)(2,1)S(1)} collective-permute-done((bf16[128,1536]{1,0:T(8,128)(2,1)S(1)}, bf16[128,1536]{1,0:T(8,128)(2,1)S(1)}, u32[]{:S(2)}, u32[]{:S(2)}) %collective-permute-start.13) | collective-permute-done | bytes 393248 | tf_op jit(solution)/shard_map/ppermute | solution.py:28
  94.1 0.7 copy-done.14
  94.8 0.8 collective-permute-start.17
  95.6 8.5 %collective-permute-done.14.refs_10_ = bf16[128,1536]{1,0:T(8,128)(2,1)S(1)} collective-permute-done((bf16[128,1536]{1,0:T(8,128)(2,1)S(1)}, bf16[128,1536]{1,0:T(8,128)(2,1)S(1)}, u32[]{:S(2)}, u32[]{:S(2)}) %collective-permute-start.14) | collective-permute-done | bytes 393248 | tf_op jit(solution)/shard_map/ppermute | solution.py:28
  104.1 0.8 copy-done.16
  105.4 0.9 copy-done.12
  106.8 1.5 collective-permute-start.23
  108.3 0.9 collective-permute-start.24
  109.2 1.1 collective-permute-done.20.refs_18_
  110.3 1.1 copy-done.6
  111.5 1.1 copy-done.13
  112.6 1.0 copy-done.15
  113.6 1.0 copy-done.17
  114.6 25.5 %attend.1 = (bf16[128,768]{1,0:T(8,128)(2,1)S(1)}, bf16[128,768]{1,0:T(8,128)(2,1)}) custom-call(s32[4]{0:T(128)S(1)} %pad_add_fusion.where_ref, s32[2,64]{1,0:T(2,128)S(1)} %copy-done.19, f32[2,768]{1,0:T(2,128)S(1)} %copy-done.18, bf16[256,1536]{1,0:T(8,128)(2,1)S(1)} %modulate.2.refs_0_, bf16[256,1536]{1,0:T(8,128)(2,1)S(1)} %collective-permute-done.4.refs_1_, ...), custom_call_target="tpu_custom_call" | custom-call | flops 16000000000 | bytes 16000000 | tf_op jit(solution)/shard_map/attend/pallas_call | solution.py:190
  142.5 1.1 copy-done.1
  143.6 0.9 copy-done.8
  144.5 3.0 %output.1 = (bf16[128,1536]{1,0:T(8,128)(2,1)S(1)}, bf16[128,1536]{1,0:T(8,128)(2,1)S(1)}, bf16[128,1536]{1,0:T(8,128)(2,1)S(1)}) custom-call(s32[4]{0:T(128)S(1)} %pad_add_fusion.where_ref, s32[8]{0:T(128)S(1)} %copy-done.10, f32[50]{0:T(128)S(1)} %copy-done.11, bf16[128,768]{1,0:T(8,128)(2,1)S(1)} %copy-done.8, ...), custom_call_target="tpu_custom_call" | custom-call | tf_op jit(solution)/shard_map/output/pallas_call | solution.py:258
  147.5 1.4 collective-permute-start.25
  148.9 1.3 collective-permute-start.27
  150.2 1.3 collective-permute-start.28
  152.0 1.3 collective-permute-done.26
  153.3 1.1 bitcast_select_fusion
  154.4 1.0 multiply_add_fusion
  155.4 6.1 %collective-permute-done.25 = bf16[128,1536]{1,0:T(8,128)(2,1)S(1)} collective-permute-done((bf16[128,1536]{1,0:T(8,128)(2,1)S(1)}, bf16[128,1536]{1,0:T(8,128)(2,1)S(1)}, u32[]{:S(2)}, u32[]{:S(2)}) %collective-permute-start.25) | collective-permute-done | bytes 393248 | tf_op jit(solution)/shard_map/ppermute | solution.py:38
  161.5 9.0 %collective-permute-done.28 = bf16[128,1536]{1,0:T(8,128)(2,1)S(1)} collective-permute-done((bf16[128,1536]{1,0:T(8,128)(2,1)S(1)}, bf16[128,1536]{1,0:T(8,128)(2,1)S(1)}, u32[]{:S(2)}, u32[]{:S(2)}) %collective-permute-start.28) | collective-permute-done | bytes 393248 | tf_op jit(solution)/shard_map/ppermute | solution.py:38
  171.4 1.2 collective-permute-done.29
  172.7 1.4 select_add_fusion
  (76 shorter events, 7.3 us)
Async XLA Ops:
  0.6 17.3 %copy-start = (f32[50,3,1536]{2,0,1:T(8,128)S(1)}, f32[50,3,1536]{2,0,1:T(8,128)}, u32[]{:S(2)}) copy-start(f32[50,3,1536]{2,0,1:T(8,128)} %param.12) | copy-start | bytes 2764804
  0.6 20.9 %collective-permute-start = (bf16[256,1536]{1,0:T(8,128)(2,1)}, bf16[256,1536]{1,0:T(8,128)(2,1)S(1)}, u32[]{:S(2)}, u32[]{:S(2)}) collective-permute-start(bf16[256,1536]{1,0:T(8,128)(2,1)} %bitcast.34), channel_id=1, source_target_pairs={{0,2},{1,3},{2,0},{3,1},{4,6},{5,7},{6,4},{7,5},{8,10},{9,11},{10,... | collective-permute-start | bytes 2359304 | tf_op jit(solution)/shard_map/ppermute | solution.py:23
  5.0 16.0 %copy-start.11 = (f32[50]{0:T(128)S(1)}, f32[50]{0:T(128)}, u32[]{:S(2)}) copy-start(f32[50]{0:T(128)} %size_ref.1) | copy-start | bytes 604
  5.0 16.6 %all-to-all-start = ((bf16[8,8,2304]{2,1,0:T(8,128)(2,1)}), bf16[8,8,2304]{2,1,0:T(8,128)(2,1)}, u32[]{:S(2)}, u32[]{:S(2)}) async-start(bf16[8,8,2304]{2,1,0:T(8,128)(2,1)} %broadcast_in_dim.92), calls=%async_computation | async-start | bytes 589824 | tf_op jit(solution)/shard_map/all_to_all | solution.py:312
  18.0 1.1 copy-start.2
  19.1 0.7 copy-start.9
  21.6 0.9 copy-start.3
  22.5 6.5 %collective-permute-start.1 = (bf16[64,2304]{1,0:T(8,128)(2,1)}, bf16[64,2304]{1,0:T(8,128)(2,1)S(1)}, u32[]{:S(2)}, u32[]{:S(2)}) collective-permute-start(bf16[64,2304]{1,0:T(8,128)(2,1)} %bitcast.5), channel_id=1, source_target_pairs={{0,3},{1,0},{2,1},{3,2},{4,7},{5,4},{6,5},{7,6},{8,11},{9,8},{10,9... | collective-permute-start | bytes 884744 | tf_op jit(solution)/shard_map/ppermute | solution.py:23
  23.5 12.9 %collective-permute-start.2 = (bf16[64,2304]{1,0:T(8,128)(2,1)}, bf16[64,2304]{1,0:T(8,128)(2,1)S(1)}, u32[]{:S(2)}, u32[]{:S(2)}) collective-permute-start(bf16[64,2304]{1,0:T(8,128)(2,1)} %bitcast.5), channel_id=1, source_target_pairs={{0,2},{1,3},{2,0},{3,1},{4,6},{5,7},{6,4},{7,5},{8,10},{9,11},{10,... | collective-permute-start | bytes 884744 | tf_op jit(solution)/shard_map/ppermute | solution.py:23
  24.3 14.5 %collective-permute-start.3 = (bf16[64,2304]{1,0:T(8,128)(2,1)}, bf16[64,2304]{1,0:T(8,128)(2,1)S(1)}, u32[]{:S(2)}, u32[]{:S(2)}) collective-permute-start(bf16[64,2304]{1,0:T(8,128)(2,1)} %bitcast.5), channel_id=1, source_target_pairs={{0,1},{1,2},{2,3},{3,0},{4,5},{5,6},{6,7},{7,4},{8,9},{9,10},{10,1... | collective-permute-start | bytes 884744 | tf_op jit(solution)/shard_map/ppermute | solution.py:23
  25.9 16.4 %collective-permute-start.4 = (bf16[256,1536]{1,0:T(8,128)(2,1)S(1)}, bf16[256,1536]{1,0:T(8,128)(2,1)S(1)}, u32[]{:S(2)}, u32[]{:S(2)}) collective-permute-start(bf16[256,1536]{1,0:T(8,128)(2,1)S(1)} %modulate.2.refs_0_), channel_id=1, source_target_pairs={{0,4},{1,5},{2,6},{3,7},{4,8},{5,9},{6,10},{7,11},{8,12},{9,13},{1... | collective-permute-start | bytes 2359304 | tf_op jit(solution)/shard_map/ppermute | solution.py:28
  27.6 17.9 %collective-permute-start.5 = (bf16[256,1536]{1,0:T(8,128)(2,1)S(1)}, bf16[256,1536]{1,0:T(8,128)(2,1)S(1)}, u32[]{:S(2)}, u32[]{:S(2)}) collective-permute-start(bf16[256,1536]{1,0:T(8,128)(2,1)S(1)} %modulate.2.refs_0_), channel_id=1, source_target_pairs={{0,28},{1,29},{2,30},{3,31},{4,0},{5,1},{6,2},{7,3},{8,4},{9,5},{1... | collective-permute-start | bytes 2359304 | tf_op jit(solution)/shard_map/ppermute | solution.py:28
  38.8 6.7 %copy-start.20 = (bf16[8,4,8,2304]{3,2,1,0:T(8,128)(2,1)}, bf16[8,4,8,2304]{3,2,1,0:T(8,128)(2,1)S(1)}, u32[]{:S(2)}) copy-start(bf16[8,4,8,2304]{3,2,1,0:T(8,128)(2,1)S(1)} %bitcast_dynamic-update-slice_fusion) | copy-start | bytes 3538948
  47.8 5.3 %copy-start.10 = (s32[8]{0:T(128)S(1)}, s32[8]{0:T(128)}, u32[]{:S(2)}) copy-start(s32[8]{0:T(128)} %index_ref.5) | copy-start | bytes 100
  47.8 19.8 %collective-permute-start.6 = (bf16[192,2304]{1,0:T(8,128)(2,1)}, bf16[192,2304]{1,0:T(8,128)(2,1)}, u32[]{:S(2)}, u32[]{:S(2)}) collective-permute-start(bf16[192,2304]{1,0:T(8,128)(2,1)} %reshape.52.refs_11_), channel_id=1, source_target_pairs={{0,64},{32,96},{64,128},{96,160},{128,192},{160,224},{192,0},{224,... | collective-permute-start | bytes 2654216 | tf_op jit(solution)/shard_map/ppermute | solution.py:33
  49.2 15.8 %collective-permute-start.10 = (bf16[256,1536]{1,0:T(8,128)(2,1)}, bf16[256,1536]{1,0:T(8,128)(2,1)}, u32[]{:S(2)}, u32[]{:S(2)}) collective-permute-start(bf16[256,1536]{1,0:T(8,128)(2,1)} %get-tuple-element.76), channel_id=1, source_target_pairs={{0,3},{1,0},{2,1},{3,2},{4,7},{5,4},{6,5},{7,6},{8,11},{9,8},{10,9... | collective-permute-start | bytes 2359304 | tf_op jit(solution)/shard_map/ppermute | solution.py:23
  49.2 16.1 %collective-permute-start.9 = (bf16[256,1536]{1,0:T(8,128)(2,1)}, bf16[256,1536]{1,0:T(8,128)(2,1)}, u32[]{:S(2)}, u32[]{:S(2)}) collective-permute-start(bf16[256,1536]{1,0:T(8,128)(2,1)} %get-tuple-element.77), channel_id=1, source_target_pairs={{0,1},{1,2},{2,3},{3,0},{4,5},{5,6},{6,7},{7,4},{8,9},{9,10},{10,1... | collective-permute-start | bytes 2359304 | tf_op jit(solution)/shard_map/ppermute | solution.py:23
  50.7 15.0 %collective-permute-start.7 = (bf16[256,1536]{1,0:T(8,128)(2,1)S(1)}, bf16[256,1536]{1,0:T(8,128)(2,1)}, u32[]{:S(2)}, u32[]{:S(2)}) collective-permute-start(bf16[256,1536]{1,0:T(8,128)(2,1)S(1)} %collective-permute-done.4.refs_1_), channel_id=1, source_target_pairs={{0,4},{1,5},{2,6},{3,7},{4,8},{5,9},{6,10},{7,11},{8,12},{9,13},{1... | collective-permute-start | bytes 2359304 | tf_op jit(solution)/shard_map/ppermute | solution.py:28
  53.1 14.4 %collective-permute-start.8 = (bf16[256,1536]{1,0:T(8,128)(2,1)S(1)}, bf16[256,1536]{1,0:T(8,128)(2,1)}, u32[]{:S(2)}, u32[]{:S(2)}) collective-permute-start(bf16[256,1536]{1,0:T(8,128)(2,1)S(1)} %collective-permute-done.5.refs_2_), channel_id=1, source_target_pairs={{0,28},{1,29},{2,30},{3,31},{4,0},{5,1},{6,2},{7,3},{8,4},{9,5},{1... | collective-permute-start | bytes 2359304 | tf_op jit(solution)/shard_map/ppermute | solution.py:28
  53.1 1.1 copy-start.4
  55.4 0.9 copy-start.5
  60.5 12.1 %copy-start.22 = (bf16[96,1536]{1,0:T(8,128)(2,1)S(1)}, bf16[96,1536]{1,0:T(8,128)(2,1)}, u32[]{:S(2)}) copy-start(bf16[96,1536]{1,0:T(8,128)(2,1)} %reshape.53) | copy-start | bytes 884740
  67.5 38.8 %collective-permute-start.11 = (bf16[192,2304]{1,0:T(8,128)(2,1)}, bf16[192,2304]{1,0:T(8,128)(2,1)}, u32[]{:S(2)}, u32[]{:S(2)}) collective-permute-start(bf16[192,2304]{1,0:T(8,128)(2,1)} %reshape.52.refs_11_), channel_id=1, source_target_pairs={{0,192},{32,224},{64,0},{96,32},{128,64},{160,96},{192,128},{224,1... | collective-permute-start | bytes 2654216 | tf_op jit(solution)/shard_map/ppermute | solution.py:33
  68.8 37.5 %collective-permute-start.12 = (bf16[192,2304]{1,0:T(8,128)(2,1)}, bf16[192,2304]{1,0:T(8,128)(2,1)}, u32[]{:S(2)}, u32[]{:S(2)}) collective-permute-start(bf16[192,2304]{1,0:T(8,128)(2,1)} %collective-permute-done.6.refs_12_), channel_id=1, source_target_pairs={{0,64},{32,96},{64,128},{96,160},{128,192},{160,224},{192,0},{224,... | collective-permute-start | bytes 2654216 | tf_op jit(solution)/shard_map/ppermute | solution.py:33
  70.3 40.0 %copy-start.18 = (f32[2,768]{1,0:T(2,128)S(1)}, f32[2,768]{1,0:T(2,128)}, u32[]{:S(2)}) copy-start(f32[2,768]{1,0:T(2,128)} %gain_ref.1) | copy-start | bytes 18436
  70.3 40.0 %copy-start.19 = (s32[2,64]{1,0:T(2,128)S(1)}, s32[2,64]{1,0:T(2,128)}, u32[]{:S(2)}) copy-start(s32[2,64]{1,0:T(2,128)} %mask_ref.1) | copy-start | bytes 1540
  70.3 35.1 %collective-permute-start.15 = (bf16[256,1536]{1,0:T(8,128)(2,1)S(1)}, bf16[256,1536]{1,0:T(8,128)(2,1)S(1)}, u32[]{:S(2)}, u32[]{:S(2)}) collective-permute-start(bf16[256,1536]{1,0:T(8,128)(2,1)S(1)} %broadcast_select_fusion), channel_id=1, source_target_pairs={{0,2},{1,3},{2,0},{3,1},{4,6},{5,7},{6,4},{7,5},{8,10},{9,11},{10,... | collective-permute-start | bytes 2359304 | tf_op jit(solution)/shard_map/ppermute | solution.py:23
  72.6 9.8 %collective-permute-start.16 = (bf16[96,1536]{1,0:T(8,128)(2,1)S(1)}, bf16[96,1536]{1,0:T(8,128)(2,1)S(1)}, u32[]{:S(2)}, u32[]{:S(2)}) collective-permute-start(bf16[96,1536]{1,0:T(8,128)(2,1)S(1)} %copy-done.22), channel_id=1, source_target_pairs={{0,32},{32,0},{64,96},{96,64},{128,160},{160,128},{192,224},{224,1... | collective-permute-start | bytes 884744 | tf_op jit(solution)/shard_map/ppermute | solution.py:42
  80.1 14.0 %collective-permute-start.13 = (bf16[128,1536]{1,0:T(8,128)(2,1)S(1)}, bf16[128,1536]{1,0:T(8,128)(2,1)S(1)}, u32[]{:S(2)}, u32[]{:S(2)}) collective-permute-start(bf16[128,1536]{1,0:T(8,128)(2,1)S(1)} %slice.14), channel_id=1, source_target_pairs={{0,8},{1,9},{2,10},{3,11},{4,12},{5,13},{6,14},{7,15},{8,16},{9,17... | collective-permute-start | bytes 1179656 | tf_op jit(solution)/shard_map/ppermute | solution.py:28
  82.4 21.7 %collective-permute-start.14 = (bf16[128,1536]{1,0:T(8,128)(2,1)S(1)}, bf16[128,1536]{1,0:T(8,128)(2,1)S(1)}, u32[]{:S(2)}, u32[]{:S(2)}) collective-permute-start(bf16[128,1536]{1,0:T(8,128)(2,1)S(1)} %slice.15), channel_id=1, source_target_pairs={{0,24},{1,25},{2,26},{3,27},{4,28},{5,29},{6,30},{7,31},{8,0},{9,1... | collective-permute-start | bytes 1179656 | tf_op jit(solution)/shard_map/ppermute | solution.py:28
  94.1 0.7 copy-start.14
  94.8 12.0 %collective-permute-start.17 = (bf16[192,2304]{1,0:T(8,128)(2,1)}, bf16[192,2304]{1,0:T(8,128)(2,1)}, u32[]{:S(2)}, u32[]{:S(2)}) collective-permute-start(bf16[192,2304]{1,0:T(8,128)(2,1)} %reshape.52.refs_11_), channel_id=1, source_target_pairs={{0,32},{32,0},{64,96},{96,64},{128,160},{160,128},{192,224},{224,1... | collective-permute-start | bytes 2654216 | tf_op jit(solution)/shard_map/ppermute | solution.py:42
  104.1 0.8 copy-start.16
  104.9 3.4 %collective-permute-start.18 = (bf16[192,2304]{1,0:T(8,128)(2,1)}, bf16[192,2304]{1,0:T(8,128)(2,1)}, u32[]{:S(2)}, u32[]{:S(2)}) collective-permute-start(bf16[192,2304]{1,0:T(8,128)(2,1)} %collective-permute-done.6.refs_12_), channel_id=1, source_target_pairs={{0,32},{32,0},{64,96},{96,64},{128,160},{160,128},{192,224},{224,1... | collective-permute-start | bytes 2654216 | tf_op jit(solution)/shard_map/ppermute | solution.py:42
  105.4 0.9 copy-start.12
  106.3 2.9 %collective-permute-start.19 = (bf16[192,2304]{1,0:T(8,128)(2,1)}, bf16[192,2304]{1,0:T(8,128)(2,1)}, u32[]{:S(2)}, u32[]{:S(2)}) collective-permute-start(bf16[192,2304]{1,0:T(8,128)(2,1)} %collective-permute-done.11.refs_13_), channel_id=1, source_target_pairs={{0,32},{32,0},{64,96},{96,64},{128,160},{160,128},{192,224},{224,1... | collective-permute-start | bytes 2654216 | tf_op jit(solution)/shard_map/ppermute | solution.py:42
  106.3 4.0 %collective-permute-start.20 = (bf16[192,2304]{1,0:T(8,128)(2,1)}, bf16[192,2304]{1,0:T(8,128)(2,1)}, u32[]{:S(2)}, u32[]{:S(2)}) collective-permute-start(bf16[192,2304]{1,0:T(8,128)(2,1)} %collective-permute-done.12.refs_14_), channel_id=1, source_target_pairs={{0,32},{32,0},{64,96},{96,64},{128,160},{160,128},{192,224},{224,1... | collective-permute-start | bytes 2654216 | tf_op jit(solution)/shard_map/ppermute | solution.py:42
  106.8 35.7 %collective-permute-start.22 = (bf16[2,96,1536]{2,1,0:T(8,128)(2,1)}, bf16[2,96,1536]{2,1,0:T(8,128)(2,1)}, u32[]{:S(2)}, u32[]{:S(2)}) collective-permute-start(bf16[2,96,1536]{2,1,0:T(8,128)(2,1)} %pad_maximum_fusion.refs_0_), channel_id=1, source_target_pairs={{0,64},{32,96},{64,128},{96,160},{128,192},{160,224},{192,0},{224,... | collective-permute-start | bytes 1769480 | tf_op jit(solution)/shard_map/ppermute | solution.py:33
  106.8 35.7 %collective-permute-start.23 = (bf16[2,96,1536]{2,1,0:T(8,128)(2,1)}, bf16[2,96,1536]{2,1,0:T(8,128)(2,1)}, u32[]{:S(2)}, u32[]{:S(2)}) collective-permute-start(bf16[2,96,1536]{2,1,0:T(8,128)(2,1)} %pad_maximum_fusion.refs_0_), channel_id=1, source_target_pairs={{0,192},{32,224},{64,0},{96,32},{128,64},{160,96},{192,128},{224,1... | collective-permute-start | bytes 1769480 | tf_op jit(solution)/shard_map/ppermute | solution.py:33
  108.3 34.2 %collective-permute-start.24 = (bf16[2,96,1536]{2,1,0:T(8,128)(2,1)}, bf16[2,96,1536]{2,1,0:T(8,128)(2,1)}, u32[]{:S(2)}, u32[]{:S(2)}) collective-permute-start(bf16[2,96,1536]{2,1,0:T(8,128)(2,1)} %pad_maximum_fusion.refs_0_), channel_id=1, source_target_pairs={{0,128},{32,160},{64,192},{96,224},{128,0},{160,32},{192,64},{224,... | collective-permute-start | bytes 1769480 | tf_op jit(solution)/shard_map/ppermute | solution.py:33
  110.3 1.1 copy-start.6
  111.5 1.1 copy-start.13
  112.6 1.0 copy-start.15
  113.6 1.0 copy-start.17
  140.2 0.7 copy-start.7
  140.8 1.7 collective-permute-start.21
  142.5 1.1 copy-start.1
  143.6 0.9 copy-start.8
  147.5 6.9 %copy-start.21 = (f32[256,1536]{1,0:T(8,128)S(1)}, f32[256,1536]{1,0:T(8,128)}, u32[]{:S(2)}) copy-start(f32[256,1536]{1,0:T(8,128)} %param.10) | copy-start | bytes 4718596
  147.5 14.0 %collective-permute-start.25 = (bf16[128,1536]{1,0:T(8,128)(2,1)S(1)}, bf16[128,1536]{1,0:T(8,128)(2,1)S(1)}, u32[]{:S(2)}, u32[]{:S(2)}) collective-permute-start(bf16[128,1536]{1,0:T(8,128)(2,1)S(1)} %get-tuple-element.65), channel_id=1, source_target_pairs={{0,128},{32,160},{64,192},{96,224},{1,129},{33,161},{65,193},{97,2... | collective-permute-start | bytes 1179656 | tf_op jit(solution)/shard_map/ppermute | solution.py:38
  148.9 12.5 %collective-permute-start.27 = (bf16[128,1536]{1,0:T(8,128)(2,1)S(1)}, bf16[128,1536]{1,0:T(8,128)(2,1)S(1)}, u32[]{:S(2)}, u32[]{:S(2)}) collective-permute-start(bf16[128,1536]{1,0:T(8,128)(2,1)S(1)} %get-tuple-element.65), channel_id=1, source_target_pairs={{0,64},{32,96},{64,128},{96,160},{128,192},{160,224},{1,65},{33,97... | collective-permute-start | bytes 1179656 | tf_op jit(solution)/shard_map/ppermute | solution.py:38
  150.2 20.3 %collective-permute-start.28 = (bf16[128,1536]{1,0:T(8,128)(2,1)S(1)}, bf16[128,1536]{1,0:T(8,128)(2,1)S(1)}, u32[]{:S(2)}, u32[]{:S(2)}) collective-permute-start(bf16[128,1536]{1,0:T(8,128)(2,1)S(1)} %get-tuple-element.65), channel_id=1, source_target_pairs={{0,192},{32,224},{1,193},{33,225},{2,194},{34,226},{3,195},{35,227... | collective-permute-start | bytes 1179656 | tf_op jit(solution)/shard_map/ppermute | solution.py:38
  151.5 1.8 %collective-permute-start.26 = (bf16[128,1536]{1,0:T(8,128)(2,1)S(1)}, bf16[128,1536]{1,0:T(8,128)(2,1)S(1)}, u32[]{:S(2)}, u32[]{:S(2)}) collective-permute-start(bf16[128,1536]{1,0:T(8,128)(2,1)S(1)} %get-tuple-element.67), channel_id=1, source_target_pairs={{0,32},{32,0},{64,96},{96,64},{128,160},{160,128},{192,224},{224,1... | collective-permute-start | bytes 1179656 | tf_op jit(solution)/shard_map/ppermute | solution.py:42
  170.7 1.9 %collective-permute-start.29 = (bf16[128,1536]{1,0:T(8,128)(2,1)S(1)}, bf16[128,1536]{1,0:T(8,128)(2,1)S(1)}, u32[]{:S(2)}, u32[]{:S(2)}) collective-permute-start(bf16[128,1536]{1,0:T(8,128)(2,1)S(1)} %add_convert_fusion), channel_id=1, source_target_pairs={{0,32},{32,0},{64,96},{96,64},{128,160},{160,128},{192,224},{224,1... | collective-permute-start | bytes 1179656 | tf_op jit(solution)/shard_map/ppermute | solution.py:42

commit v6 on v5

--- a/solution.py
+++ b/solution.py
@@ -14,7 +14,7 @@
 NORM_EPS = 1e-06
 F32 = jnp.float32
 BF16 = jnp.bfloat16
-ATTEND_VMEM = 40 * 1024 * 1024
+ATTEND_VMEM = 32 * 1024 * 1024
 OUTPUT_VMEM = 16 * 1024 * 1024
 
 
@@ -356,17 +356,18 @@
     rest = core_swap(other)
     parts = (2, rows // 2, width)
     near_half = (jnp.arange(2, dtype=jnp.int32) == core)[:, None, None]
+    own32 = own.astype(F32)
+    velocity = jnp.where(near_half, own[None], rest[None]).reshape(rows, width)
+    two, velocity = lax.optimization_barrier((two, velocity))
+    even = jnp.where(core == 0, size_own, 0.0)
     odd = jnp.where(core == 1, size_other, 0.0)
-    even = jnp.where(core == 0, size_own, 0.0)
-    velocity = jnp.where(near_half, own[None], rest[None])
-    inner = jnp.where(near_half, odd * other.astype(F32)[None], 0.0)
-    base = anchor.reshape(parts) + inner + size_own * velocity.astype(F32)
-    two, velocity, base = lax.optimization_barrier((two, velocity.reshape(rows, width), base))
     sums = one.astype(F32) + two.astype(F32) + three.astype(F32)
-    earlier = core_swap((sums + even * own.astype(F32)).astype(BF16))
-    one, two, three = lax.optimization_barrier((one, two, three))
+    earlier = core_swap((sums + even * own32).astype(BF16))
+    one, two, three, own = lax.optimization_barrier((one, two, three, own))
     sums = one.astype(F32) + two.astype(F32) + three.astype(F32)
-    advanced = base + jnp.where(near_half, sums[None], earlier.astype(F32)[None])
+    own_part = sums + odd * other.astype(F32) + size_own * own.astype(F32)
+    rest_part = earlier.astype(F32) + size_own * rest.astype(F32)
+    advanced = anchor.reshape(parts) + jnp.where(near_half, own_part[None], rest_part[None])
     advanced = advanced.reshape(rows, width)
     return (velocity[None], advanced[None])
 

time: 175 us -> 166 us (0.949)
  local copies, waits for them, and re-layouts: 27.1 us -> 17.4 us
  waiting for transfers between devices: 60.7 us -> 63.1 us
  Pallas kernels: 30.9 us -> 28.8 us
    unnamed x46 -> x28, local copies, waits for them, and re-layouts: 14 us -> 4.28 us
    ppermute x6, waiting for transfers between devices: 26.9 us -> 29.5 us  [z_shift(): return lax.ppermute(block, 'frame', pairs)]
  transfers between devices with their start and end apart: 31 -> 31, of which waited for: 16 -> 17; matrix products, arithmetic and copies ran while one was open for 9% -> 9% of each run, Pallas kernels for 16% -> 16%
where the time goes in v6:
time: 166 us; the launch traced here: 165 us
  waiting for transfers between devices  63.1 us (38%)
  starting transfers between devices  43.1 us (26%)
  Pallas kernels  28.8 us (17%)
  local copies, waits for them, and re-layouts  17.4 us (10%)
  other arithmetic  6.75 us (4%)
  between operations  6 us (4%)
    ppermute x6, waiting for transfers between devices, z_shift(): return lax.ppermute(block, 'frame', pairs)  29.5 us
    pallas_call x1, Pallas kernels, attend(): pl.pallas_call(attend_kernel, in_specs=[smem, smem, pl.BlockSpec(memory_s...  24.4 us
    ppermute x3, waiting for transfers between devices, x_later(): return lax.ppermute(block, 'step', pairs)  16.6 us
    ppermute x7, waiting for transfers between devices, y_shift(): return lax.ppermute(block, 'frame', pairs)  14 us
    ppermute x8, starting transfers between devices, core_swap(): return lax.ppermute(block, 'step', [(i, i ^ 1) for i in range(2 * NX)])  9.96 us
    ppermute x7, starting transfers between devices, y_shift(): return lax.ppermute(block, 'frame', pairs)  9.91 us
    all_to_all x1, starting transfers between devices, on_device(): column = lax.all_to_all(packed, 'frame', 0, 0, axis_index_groups=columns_z)  7.56 us
    ppermute x6, starting transfers between devices, z_shift(): return lax.ppermute(block, 'frame', pairs)  6.52 us
  transfers between devices with their start and end apart: 31, of which 17 were waited for; matrix products, arithmetic and copies ran while one was open for 9% of the time, Pallas kernels for 16%

profile of v6, /device:TPU:79, one launch (start us, length us, event | category | flops | bytes accessed | tf_op | source)
XLA Modules:
  0.0 165.2 jit_solution(9547367127837989564)
XLA Ops:
  0.7 2.1 %collective-permute-start = (bf16[256,1536]{1,0:T(8,128)(2,1)}, bf16[256,1536]{1,0:T(8,128)(2,1)S(1)}, u32[]{:S(2)}, u32[]{:S(2)}) collective-permute-start(bf16[256,1536]{1,0:T(8,128)(2,1)} %bitcast.39), channel_id=1, source_target_pairs={{0,2},{1,3},{2,0},{3,1},{4,6},{5,7},{6,4},{7,5},{8,10},{9,11},{10,... | collective-permute-start | bytes 2359304 | tf_op jit(solution)/shard_map/ppermute | solution.py:23
  2.8 0.7 reshape.54
  3.5 0.8 pad_maximum_fusion.1
  4.3 0.7 broadcast_in_dim.75
  5.0 7.6 %all-to-all-start = ((bf16[8,8,2304]{2,1,0:T(8,128)(2,1)}), bf16[8,8,2304]{2,1,0:T(8,128)(2,1)}, u32[]{:S(2)}, u32[]{:S(2)}) async-start(bf16[8,8,2304]{2,1,0:T(8,128)(2,1)} %broadcast_in_dim.75), calls=%async_computation | async-start | bytes 589824 | tf_op jit(solution)/shard_map/all_to_all | solution.py:312
  12.6 1.4 fusion.2
  17.9 1.1 copy-done.2
  19.0 1.2 modulate.2.refs_0_
  20.2 0.6 fusion.1
  21.0 0.9 copy-done.3
  21.8 1.0 collective-permute-start.1
  22.8 1.5 collective-permute-start.2
  24.3 1.6 collective-permute-start.3
  25.9 1.6 collective-permute-start.4
  27.6 1.0 bitcast_dynamic-update-slice_fusion.3
  28.7 7.8 %collective-permute-done.2 = bf16[64,2304]{1,0:T(8,128)(2,1)S(1)} collective-permute-done((bf16[64,2304]{1,0:T(8,128)(2,1)}, bf16[64,2304]{1,0:T(8,128)(2,1)S(1)}, u32[]{:S(2)}, u32[]{:S(2)}) %collective-permute-start.2) | collective-permute-done | bytes 294944 | tf_op jit(solution)/shard_map/ppermute | solution.py:23
  36.5 1.2 collective-permute-done.3
  37.7 4.7 %collective-permute-done.4.refs_1_ = bf16[256,1536]{1,0:T(8,128)(2,1)S(1)} collective-permute-done((bf16[256,1536]{1,0:T(8,128)(2,1)S(1)}, bf16[256,1536]{1,0:T(8,128)(2,1)S(1)}, u32[]{:S(2)}, u32[]{:S(2)}) %collective-permute-start.4) | collective-permute-done | bytes 786464 | tf_op jit(solution)/shard_map/ppermute | solution.py:28
  42.4 3.1 %collective-permute-done.5.refs_2_ = bf16[256,1536]{1,0:T(8,128)(2,1)S(1)} collective-permute-done((bf16[256,1536]{1,0:T(8,128)(2,1)S(1)}, bf16[256,1536]{1,0:T(8,128)(2,1)S(1)}, u32[]{:S(2)}, u32[]{:S(2)}) %collective-permute-start.5) | collective-permute-done | bytes 786464 | tf_op jit(solution)/shard_map/ppermute | solution.py:28
  45.5 2.2 %reshape.60.refs_11_ = bf16[192,2304]{1,0:T(8,128)(2,1)} reshape(bf16[8,4,6,2304]{3,2,1,0:T(8,128)(2,1)} %bitcast.41) | data formatting | bytes 1769472 | tf_op jit(solution)/shard_map/reshape | solution.py:322
  47.9 1.4 broadcast_select_fusion.1
  49.3 1.5 collective-permute-start.9
  50.8 2.4 %collective-permute-start.7 = (bf16[256,1536]{1,0:T(8,128)(2,1)S(1)}, bf16[256,1536]{1,0:T(8,128)(2,1)}, u32[]{:S(2)}, u32[]{:S(2)}) collective-permute-start(bf16[256,1536]{1,0:T(8,128)(2,1)S(1)} %collective-permute-done.4.refs_1_), channel_id=1, source_target_pairs={{0,4},{1,5},{2,6},{3,7},{4,8},{5,9},{6,10},{7,11},{8,12},{9,13},{1... | collective-permute-start | bytes 2359304 | tf_op jit(solution)/shard_map/ppermute | solution.py:28
  53.2 1.1 copy-done.4
  54.3 1.2 modulate.3.refs_3_
  55.5 0.9 copy-done.5
  56.4 2.3 %slice.13 = bf16[8,4,2,2304]{3,2,1,0:T(2,128)(2,1)} slice(bf16[8,4,8,2304]{3,2,1,0:T(8,128)(2,1)} %copy-done.11), slice={[0:8], [0:4], [6:8], [0:2304]} | slice | bytes 589824 | tf_op jit(solution)/shard_map/slice | solution.py:323
  58.7 1.9 %reshape.61 = bf16[96,1536]{1,0:T(8,128)(2,1)} reshape(bf16[8,4,2,2304]{3,2,1,0:T(2,128)(2,1)} %slice.13) | data formatting | bytes 589824 | tf_op jit(solution)/shard_map/reshape | solution.py:323
  60.5 4.5 %collective-permute-done.10.refs_7_ = bf16[256,1536]{1,0:T(8,128)(2,1)} collective-permute-done((bf16[256,1536]{1,0:T(8,128)(2,1)}, bf16[256,1536]{1,0:T(8,128)(2,1)}, u32[]{:S(2)}, u32[]{:S(2)}) %collective-permute-start.10) | collective-permute-done | bytes 786464 | tf_op jit(solution)/shard_map/ppermute | solution.py:23
  65.1 0.4 collective-permute-done.9.refs_6_
  65.8 1.8 %collective-permute-done.8.refs_5_ = bf16[256,1536]{1,0:T(8,128)(2,1)} collective-permute-done((bf16[256,1536]{1,0:T(8,128)(2,1)S(1)}, bf16[256,1536]{1,0:T(8,128)(2,1)}, u32[]{:S(2)}, u32[]{:S(2)}) %collective-permute-start.8) | collective-permute-done | bytes 786464 | tf_op jit(solution)/shard_map/ppermute | solution.py:28
  67.6 1.3 collective-permute-start.11
  68.9 1.4 collective-permute-start.12
  70.4 2.3 %collective-permute-start.15 = (bf16[256,1536]{1,0:T(8,128)(2,1)S(1)}, bf16[256,1536]{1,0:T(8,128)(2,1)S(1)}, u32[]{:S(2)}, u32[]{:S(2)}) collective-permute-start(bf16[256,1536]{1,0:T(8,128)(2,1)S(1)} %broadcast_select_fusion), channel_id=1, source_target_pairs={{0,2},{1,3},{2,0},{3,1},{4,6},{5,7},{6,4},{7,5},{8,10},{9,11},{10,... | collective-permute-start | bytes 2359304 | tf_op jit(solution)/shard_map/ppermute | solution.py:23
  72.6 6.5 %collective-permute-start.16 = (bf16[96,1536]{1,0:T(8,128)(2,1)S(1)}, bf16[96,1536]{1,0:T(8,128)(2,1)S(1)}, u32[]{:S(2)}, u32[]{:S(2)}) collective-permute-start(bf16[96,1536]{1,0:T(8,128)(2,1)S(1)} %copy-done.13), channel_id=1, source_target_pairs={{0,32},{32,0},{64,96},{96,64},{128,160},{160,128},{192,224},{224,1... | collective-permute-start | bytes 884744 | tf_op jit(solution)/shard_map/ppermute | solution.py:42
  79.1 1.0 slice.14
  80.2 1.3 collective-permute-start.13
  81.5 1.0 slice.15
  82.5 1.2 collective-permute-start.14
  83.8 10.4 %collective-permute-done.13.refs_9_ = bf16[128,1536]{1,0:T(8,128)(2,1)S(1)} collective-permute-done((bf16[128,1536]{1,0:T(8,128)(2,1)S(1)}, bf16[128,1536]{1,0:T(8,128)(2,1)S(1)}, u32[]{:S(2)}, u32[]{:S(2)}) %collective-permute-start.13) | collective-permute-done | bytes 393248 | tf_op jit(solution)/shard_map/ppermute | solution.py:28
  94.2 0.8 collective-permute-start.17
  95.0 9.2 %collective-permute-done.14.refs_10_ = bf16[128,1536]{1,0:T(8,128)(2,1)S(1)} collective-permute-done((bf16[128,1536]{1,0:T(8,128)(2,1)S(1)}, bf16[128,1536]{1,0:T(8,128)(2,1)S(1)}, u32[]{:S(2)}, u32[]{:S(2)}) %collective-permute-start.14) | collective-permute-done | bytes 393248 | tf_op jit(solution)/shard_map/ppermute | solution.py:28
  104.1 0.6 collective-permute-start.18
  104.8 0.5 collective-permute-start.20
  105.4 1.5 collective-permute-start.23
  106.8 0.3 collective-permute-done.18.refs_16_
  107.2 0.9 collective-permute-start.24
  108.1 1.2 collective-permute-done.20.refs_18_
  109.3 24.4 %attend.1 = (bf16[128,768]{1,0:T(8,128)(2,1)S(1)}, bf16[128,768]{1,0:T(8,128)(2,1)S(1)}) custom-call(s32[4]{0:T(128)S(1)} %pad_add_fusion.where_ref, s32[2,64]{1,0:T(2,128)S(1)} %copy-done.10, f32[2,768]{1,0:T(2,128)S(1)} %copy-done.9, bf16[256,1536]{1,0:T(8,128)(2,1)S(1)} %modulate.2.refs_0_, bf16[256,1536]{1,0:T(8,128)(2,1)S(1)} %collective-permute-done.4.refs_1_, ...), custom_call_target="tpu_custom_call" | custom-call | flops 16000000000 | bytes 16000000 | tf_op jit(solution)/shard_map/attend/pallas_call | solution.py:190
  133.7 0.5 collective-permute-start.21
  134.2 1.1 collective-permute-done.21.got_ref
  135.3 2.0 %output.1 = (bf16[128,1536]{1,0:T(8,128)(2,1)S(1)}, bf16[128,1536]{1,0:T(8,128)(2,1)S(1)}, bf16[128,1536]{1,0:T(8,128)(2,1)S(1)}) custom-call(s32[4]{0:T(128)S(1)} %pad_add_fusion.where_ref, s32[8]{0:T(128)S(1)} %copy-done.7, f32[50]{0:T(128)S(1)} %copy-done.8, bf16[128,768]{1,0:T(8,128)(2,1)S(1)} %get-tuple-element.62.keep_ref, ...), custom_call_target="tpu_custom_call" | custom-call | tf_op jit(solution)/shard_map/output/pallas_call | solution.py:258
  137.3 0.5 collective-permute-start.26
  137.7 1.3 collective-permute-start.25
  139.0 1.3 collective-permute-start.27
  140.3 1.3 collective-permute-start.28
  143.0 1.0 bitcast_select_fusion.1
  144.0 7.7 %collective-permute-done.25 = bf16[128,1536]{1,0:T(8,128)(2,1)S(1)} collective-permute-done((bf16[128,1536]{1,0:T(8,128)(2,1)S(1)}, bf16[128,1536]{1,0:T(8,128)(2,1)S(1)}, u32[]{:S(2)}, u32[]{:S(2)}) %collective-permute-start.25) | collective-permute-done | bytes 393248 | tf_op jit(solution)/shard_map/ppermute | solution.py:38
  151.8 8.9 %collective-permute-done.28 = bf16[128,1536]{1,0:T(8,128)(2,1)S(1)} collective-permute-done((bf16[128,1536]{1,0:T(8,128)(2,1)S(1)}, bf16[128,1536]{1,0:T(8,128)(2,1)S(1)}, u32[]{:S(2)}, u32[]{:S(2)}) %collective-permute-start.28) | collective-permute-done | bytes 393248 | tf_op jit(solution)/shard_map/ppermute | solution.py:38
  160.9 0.6 collective-permute-start.29
  161.4 0.9 multiply_add_fusion.1
  162.3 0.4 collective-permute-done.29
  162.8 0.8 multiply_add_fusion
  163.7 1.4 fusion
  (56 shorter events, 1.8 us)
Async XLA Ops:
  0.6 17.2 %copy-start.7 = (s32[8]{0:T(128)S(1)}, s32[8]{0:T(128)}, u32[]{:S(2)}) copy-start(s32[8]{0:T(128)} %index_ref.5) | copy-start | bytes 100
  0.6 17.2 %copy-start = (f32[50,3,1536]{2,0,1:T(8,128)S(1)}, f32[50,3,1536]{2,0,1:T(8,128)}, u32[]{:S(2)}) copy-start(f32[50,3,1536]{2,0,1:T(8,128)} %param.12) | copy-start | bytes 2764804
  0.7 20.3 %collective-permute-start = (bf16[256,1536]{1,0:T(8,128)(2,1)}, bf16[256,1536]{1,0:T(8,128)(2,1)S(1)}, u32[]{:S(2)}, u32[]{:S(2)}) collective-permute-start(bf16[256,1536]{1,0:T(8,128)(2,1)} %bitcast.39), channel_id=1, source_target_pairs={{0,2},{1,3},{2,0},{3,1},{4,6},{5,7},{6,4},{7,5},{8,10},{9,11},{10,... | collective-permute-start | bytes 2359304 | tf_op jit(solution)/shard_map/ppermute | solution.py:23
  5.0 15.8 %all-to-all-start = ((bf16[8,8,2304]{2,1,0:T(8,128)(2,1)}), bf16[8,8,2304]{2,1,0:T(8,128)(2,1)}, u32[]{:S(2)}, u32[]{:S(2)}) async-start(bf16[8,8,2304]{2,1,0:T(8,128)(2,1)} %broadcast_in_dim.75), calls=%async_computation | async-start | bytes 589824 | tf_op jit(solution)/shard_map/all_to_all | solution.py:312
  17.9 1.1 copy-start.2
  19.0 1.2 copy-start.8
  21.0 0.9 copy-start.3
  21.8 6.8 %collective-permute-start.1 = (bf16[64,2304]{1,0:T(8,128)(2,1)}, bf16[64,2304]{1,0:T(8,128)(2,1)S(1)}, u32[]{:S(2)}, u32[]{:S(2)}) collective-permute-start(bf16[64,2304]{1,0:T(8,128)(2,1)} %bitcast.5), channel_id=1, source_target_pairs={{0,3},{1,0},{2,1},{3,2},{4,7},{5,4},{6,5},{7,6},{8,11},{9,8},{10,9... | collective-permute-start | bytes 884744 | tf_op jit(solution)/shard_map/ppermute | solution.py:23
  22.8 13.6 %collective-permute-start.2 = (bf16[64,2304]{1,0:T(8,128)(2,1)}, bf16[64,2304]{1,0:T(8,128)(2,1)S(1)}, u32[]{:S(2)}, u32[]{:S(2)}) collective-permute-start(bf16[64,2304]{1,0:T(8,128)(2,1)} %bitcast.5), channel_id=1, source_target_pairs={{0,2},{1,3},{2,0},{3,1},{4,6},{5,7},{6,4},{7,5},{8,10},{9,11},{10,... | collective-permute-start | bytes 884744 | tf_op jit(solution)/shard_map/ppermute | solution.py:23
  24.3 13.4 %collective-permute-start.3 = (bf16[64,2304]{1,0:T(8,128)(2,1)}, bf16[64,2304]{1,0:T(8,128)(2,1)S(1)}, u32[]{:S(2)}, u32[]{:S(2)}) collective-permute-start(bf16[64,2304]{1,0:T(8,128)(2,1)} %bitcast.5), channel_id=1, source_target_pairs={{0,1},{1,2},{2,3},{3,0},{4,5},{5,6},{6,7},{7,4},{8,9},{9,10},{10,1... | collective-permute-start | bytes 884744 | tf_op jit(solution)/shard_map/ppermute | solution.py:23
  25.9 16.5 %collective-permute-start.4 = (bf16[256,1536]{1,0:T(8,128)(2,1)S(1)}, bf16[256,1536]{1,0:T(8,128)(2,1)S(1)}, u32[]{:S(2)}, u32[]{:S(2)}) collective-permute-start(bf16[256,1536]{1,0:T(8,128)(2,1)S(1)} %modulate.2.refs_0_), channel_id=1, source_target_pairs={{0,4},{1,5},{2,6},{3,7},{4,8},{5,9},{6,10},{7,11},{8,12},{9,13},{1... | collective-permute-start | bytes 2359304 | tf_op jit(solution)/shard_map/ppermute | solution.py:28
  27.5 18.0 %collective-permute-start.5 = (bf16[256,1536]{1,0:T(8,128)(2,1)S(1)}, bf16[256,1536]{1,0:T(8,128)(2,1)S(1)}, u32[]{:S(2)}, u32[]{:S(2)}) collective-permute-start(bf16[256,1536]{1,0:T(8,128)(2,1)S(1)} %modulate.2.refs_0_), channel_id=1, source_target_pairs={{0,28},{1,29},{2,30},{3,31},{4,0},{5,1},{6,2},{7,3},{8,4},{9,5},{1... | collective-permute-start | bytes 2359304 | tf_op jit(solution)/shard_map/ppermute | solution.py:28
  37.7 7.8 %copy-start.11 = (bf16[8,4,8,2304]{3,2,1,0:T(8,128)(2,1)}, bf16[8,4,8,2304]{3,2,1,0:T(8,128)(2,1)S(1)}, u32[]{:S(2)}) copy-start(bf16[8,4,8,2304]{3,2,1,0:T(8,128)(2,1)S(1)} %bitcast_dynamic-update-slice_fusion) | copy-start | bytes 3538948
  47.7 19.9 %collective-permute-start.6 = (bf16[192,2304]{1,0:T(8,128)(2,1)}, bf16[192,2304]{1,0:T(8,128)(2,1)}, u32[]{:S(2)}, u32[]{:S(2)}) collective-permute-start(bf16[192,2304]{1,0:T(8,128)(2,1)} %reshape.60.refs_11_), channel_id=1, source_target_pairs={{0,64},{32,96},{64,128},{96,160},{128,192},{160,224},{192,0},{224,... | collective-permute-start | bytes 2654216 | tf_op jit(solution)/shard_map/ppermute | solution.py:33
  49.3 15.8 %collective-permute-start.10 = (bf16[256,1536]{1,0:T(8,128)(2,1)}, bf16[256,1536]{1,0:T(8,128)(2,1)}, u32[]{:S(2)}, u32[]{:S(2)}) collective-permute-start(bf16[256,1536]{1,0:T(8,128)(2,1)} %get-tuple-element.76), channel_id=1, source_target_pairs={{0,3},{1,0},{2,1},{3,2},{4,7},{5,4},{6,5},{7,6},{8,11},{9,8},{10,9... | collective-permute-start | bytes 2359304 | tf_op jit(solution)/shard_map/ppermute | solution.py:23
  49.3 16.1 %collective-permute-start.9 = (bf16[256,1536]{1,0:T(8,128)(2,1)}, bf16[256,1536]{1,0:T(8,128)(2,1)}, u32[]{:S(2)}, u32[]{:S(2)}) collective-permute-start(bf16[256,1536]{1,0:T(8,128)(2,1)} %get-tuple-element.77), channel_id=1, source_target_pairs={{0,1},{1,2},{2,3},{3,0},{4,5},{5,6},{6,7},{7,4},{8,9},{9,10},{10,1... | collective-permute-start | bytes 2359304 | tf_op jit(solution)/shard_map/ppermute | solution.py:23
  50.8 15.0 %collective-permute-start.7 = (bf16[256,1536]{1,0:T(8,128)(2,1)S(1)}, bf16[256,1536]{1,0:T(8,128)(2,1)}, u32[]{:S(2)}, u32[]{:S(2)}) collective-permute-start(bf16[256,1536]{1,0:T(8,128)(2,1)S(1)} %collective-permute-done.4.refs_1_), channel_id=1, source_target_pairs={{0,4},{1,5},{2,6},{3,7},{4,8},{5,9},{6,10},{7,11},{8,12},{9,13},{1... | collective-permute-start | bytes 2359304 | tf_op jit(solution)/shard_map/ppermute | solution.py:28
  53.2 14.4 %collective-permute-start.8 = (bf16[256,1536]{1,0:T(8,128)(2,1)S(1)}, bf16[256,1536]{1,0:T(8,128)(2,1)}, u32[]{:S(2)}, u32[]{:S(2)}) collective-permute-start(bf16[256,1536]{1,0:T(8,128)(2,1)S(1)} %collective-permute-done.5.refs_2_), channel_id=1, source_target_pairs={{0,28},{1,29},{2,30},{3,31},{4,0},{5,1},{6,2},{7,3},{8,4},{9,5},{1... | collective-permute-start | bytes 2359304 | tf_op jit(solution)/shard_map/ppermute | solution.py:28
  53.2 1.1 copy-start.4
  55.5 0.9 copy-start.5
  60.5 12.1 %copy-start.13 = (bf16[96,1536]{1,0:T(8,128)(2,1)S(1)}, bf16[96,1536]{1,0:T(8,128)(2,1)}, u32[]{:S(2)}) copy-start(bf16[96,1536]{1,0:T(8,128)(2,1)} %reshape.61) | copy-start | bytes 884740
  67.6 37.1 %collective-permute-start.11 = (bf16[192,2304]{1,0:T(8,128)(2,1)}, bf16[192,2304]{1,0:T(8,128)(2,1)S(1)}, u32[]{:S(2)}, u32[]{:S(2)}) collective-permute-start(bf16[192,2304]{1,0:T(8,128)(2,1)} %reshape.60.refs_11_), channel_id=1, source_target_pairs={{0,192},{32,224},{64,0},{96,32},{128,64},{160,96},{192,128},{224,1... | collective-permute-start | bytes 2654216 | tf_op jit(solution)/shard_map/ppermute | solution.py:33
  68.9 35.9 %collective-permute-start.12 = (bf16[192,2304]{1,0:T(8,128)(2,1)}, bf16[192,2304]{1,0:T(8,128)(2,1)S(1)}, u32[]{:S(2)}, u32[]{:S(2)}) collective-permute-start(bf16[192,2304]{1,0:T(8,128)(2,1)} %collective-permute-done.6.refs_12_), channel_id=1, source_target_pairs={{0,64},{32,96},{64,128},{96,160},{128,192},{160,224},{192,0},{224,... | collective-permute-start | bytes 2654216 | tf_op jit(solution)/shard_map/ppermute | solution.py:33
  70.4 34.4 %collective-permute-start.15 = (bf16[256,1536]{1,0:T(8,128)(2,1)S(1)}, bf16[256,1536]{1,0:T(8,128)(2,1)S(1)}, u32[]{:S(2)}, u32[]{:S(2)}) collective-permute-start(bf16[256,1536]{1,0:T(8,128)(2,1)S(1)} %broadcast_select_fusion), channel_id=1, source_target_pairs={{0,2},{1,3},{2,0},{3,1},{4,6},{5,7},{6,4},{7,5},{8,10},{9,11},{10,... | collective-permute-start | bytes 2359304 | tf_op jit(solution)/shard_map/ppermute | solution.py:23
  72.6 9.9 %collective-permute-start.16 = (bf16[96,1536]{1,0:T(8,128)(2,1)S(1)}, bf16[96,1536]{1,0:T(8,128)(2,1)S(1)}, u32[]{:S(2)}, u32[]{:S(2)}) collective-permute-start(bf16[96,1536]{1,0:T(8,128)(2,1)S(1)} %copy-done.13), channel_id=1, source_target_pairs={{0,32},{32,0},{64,96},{96,64},{128,160},{160,128},{192,224},{224,1... | collective-permute-start | bytes 884744 | tf_op jit(solution)/shard_map/ppermute | solution.py:42
  80.1 14.1 %copy-start.1 = (bf16[192,2304]{1,0:T(8,128)(2,1)S(1)}, bf16[192,2304]{1,0:T(8,128)(2,1)}, u32[]{:S(2)}) copy-start(bf16[192,2304]{1,0:T(8,128)(2,1)} %reshape.60.refs_11_) | copy-start | bytes 2654212
  80.1 29.2 %copy-start.6 = (bf16[256,1536]{1,0:T(8,128)(2,1)S(1)}, bf16[256,1536]{1,0:T(8,128)(2,1)}, u32[]{:S(2)}) copy-start(bf16[256,1536]{1,0:T(8,128)(2,1)} %copy-done.5) | copy-start | bytes 2359300
  80.1 29.2 %copy-start.9 = (f32[2,768]{1,0:T(2,128)S(1)}, f32[2,768]{1,0:T(2,128)}, u32[]{:S(2)}) copy-start(f32[2,768]{1,0:T(2,128)} %gain_ref.1) | copy-start | bytes 18436
  80.2 29.2 %copy-start.10 = (s32[2,64]{1,0:T(2,128)S(1)}, s32[2,64]{1,0:T(2,128)}, u32[]{:S(2)}) copy-start(s32[2,64]{1,0:T(2,128)} %mask_ref.1) | copy-start | bytes 1540
  80.2 14.0 %collective-permute-start.13 = (bf16[128,1536]{1,0:T(8,128)(2,1)S(1)}, bf16[128,1536]{1,0:T(8,128)(2,1)S(1)}, u32[]{:S(2)}, u32[]{:S(2)}) collective-permute-start(bf16[128,1536]{1,0:T(8,128)(2,1)S(1)} %slice.14), channel_id=1, source_target_pairs={{0,8},{1,9},{2,10},{3,11},{4,12},{5,13},{6,14},{7,15},{8,16},{9,17... | collective-permute-start | bytes 1179656 | tf_op jit(solution)/shard_map/ppermute | solution.py:28
  82.5 21.6 %collective-permute-start.14 = (bf16[128,1536]{1,0:T(8,128)(2,1)S(1)}, bf16[128,1536]{1,0:T(8,128)(2,1)S(1)}, u32[]{:S(2)}, u32[]{:S(2)}) collective-permute-start(bf16[128,1536]{1,0:T(8,128)(2,1)S(1)} %slice.15), channel_id=1, source_target_pairs={{0,24},{1,25},{2,26},{3,27},{4,28},{5,29},{6,30},{7,31},{8,0},{9,1... | collective-permute-start | bytes 1179656 | tf_op jit(solution)/shard_map/ppermute | solution.py:28
  94.2 11.2 %collective-permute-start.17 = (bf16[192,2304]{1,0:T(8,128)(2,1)S(1)}, bf16[192,2304]{1,0:T(8,128)(2,1)S(1)}, u32[]{:S(2)}, u32[]{:S(2)}) collective-permute-start(bf16[192,2304]{1,0:T(8,128)(2,1)S(1)} %copy-done.1), channel_id=1, source_target_pairs={{0,32},{32,0},{64,96},{96,64},{128,160},{160,128},{192,224},{224,1... | collective-permute-start | bytes 2654216 | tf_op jit(solution)/shard_map/ppermute | solution.py:42
  104.1 3.0 %collective-permute-start.18 = (bf16[192,2304]{1,0:T(8,128)(2,1)}, bf16[192,2304]{1,0:T(8,128)(2,1)S(1)}, u32[]{:S(2)}, u32[]{:S(2)}) collective-permute-start(bf16[192,2304]{1,0:T(8,128)(2,1)} %collective-permute-done.6.refs_12_), channel_id=1, source_target_pairs={{0,32},{32,0},{64,96},{96,64},{128,160},{160,128},{192,224},{224,1... | collective-permute-start | bytes 2654216 | tf_op jit(solution)/shard_map/ppermute | solution.py:42
  104.7 3.3 %collective-permute-start.19 = (bf16[192,2304]{1,0:T(8,128)(2,1)S(1)}, bf16[192,2304]{1,0:T(8,128)(2,1)S(1)}, u32[]{:S(2)}, u32[]{:S(2)}) collective-permute-start(bf16[192,2304]{1,0:T(8,128)(2,1)S(1)} %collective-permute-done.11.refs_13_), channel_id=1, source_target_pairs={{0,32},{32,0},{64,96},{96,64},{128,160},{160,128},{192,224},{224,1... | collective-permute-start | bytes 2654216 | tf_op jit(solution)/shard_map/ppermute | solution.py:42
  104.8 4.5 %collective-permute-start.20 = (bf16[192,2304]{1,0:T(8,128)(2,1)S(1)}, bf16[192,2304]{1,0:T(8,128)(2,1)S(1)}, u32[]{:S(2)}, u32[]{:S(2)}) collective-permute-start(bf16[192,2304]{1,0:T(8,128)(2,1)S(1)} %collective-permute-done.12.refs_14_), channel_id=1, source_target_pairs={{0,32},{32,0},{64,96},{96,64},{128,160},{160,128},{192,224},{224,1... | collective-permute-start | bytes 2654216 | tf_op jit(solution)/shard_map/ppermute | solution.py:42
  105.3 28.9 %collective-permute-start.22 = (bf16[2,96,1536]{2,1,0:T(8,128)(2,1)S(1)}, bf16[2,96,1536]{2,1,0:T(8,128)(2,1)S(1)}, u32[]{:S(2)}, u32[]{:S(2)}) collective-permute-start(bf16[2,96,1536]{2,1,0:T(8,128)(2,1)S(1)} %pad_maximum_fusion.refs_0_), channel_id=1, source_target_pairs={{0,64},{32,96},{64,128},{96,160},{128,192},{160,224},{192,0},{224,... | collective-permute-start | bytes 1769480 | tf_op jit(solution)/shard_map/ppermute | solution.py:33
  105.4 28.9 %collective-permute-start.23 = (bf16[2,96,1536]{2,1,0:T(8,128)(2,1)S(1)}, bf16[2,96,1536]{2,1,0:T(8,128)(2,1)S(1)}, u32[]{:S(2)}, u32[]{:S(2)}) collective-permute-start(bf16[2,96,1536]{2,1,0:T(8,128)(2,1)S(1)} %pad_maximum_fusion.refs_0_), channel_id=1, source_target_pairs={{0,192},{32,224},{64,0},{96,32},{128,64},{160,96},{192,128},{224,1... | collective-permute-start | bytes 1769480 | tf_op jit(solution)/shard_map/ppermute | solution.py:33
  107.2 27.1 %collective-permute-start.24 = (bf16[2,96,1536]{2,1,0:T(8,128)(2,1)S(1)}, bf16[2,96,1536]{2,1,0:T(8,128)(2,1)S(1)}, u32[]{:S(2)}, u32[]{:S(2)}) collective-permute-start(bf16[2,96,1536]{2,1,0:T(8,128)(2,1)S(1)} %pad_maximum_fusion.refs_0_), channel_id=1, source_target_pairs={{0,128},{32,160},{64,192},{96,224},{128,0},{160,32},{192,64},{224,... | collective-permute-start | bytes 1769480 | tf_op jit(solution)/shard_map/ppermute | solution.py:33
  133.7 1.6 collective-permute-start.21
  137.3 5.7 %collective-permute-start.26 = (bf16[128,1536]{1,0:T(8,128)(2,1)S(1)}, bf16[128,1536]{1,0:T(8,128)(2,1)S(1)}, u32[]{:S(2)}, u32[]{:S(2)}) collective-permute-start(bf16[128,1536]{1,0:T(8,128)(2,1)S(1)} %get-tuple-element.67), channel_id=1, source_target_pairs={{0,32},{32,0},{64,96},{96,64},{128,160},{160,128},{192,224},{224,1... | collective-permute-start | bytes 1179656 | tf_op jit(solution)/shard_map/ppermute | solution.py:42
  137.7 14.0 %collective-permute-start.25 = (bf16[128,1536]{1,0:T(8,128)(2,1)S(1)}, bf16[128,1536]{1,0:T(8,128)(2,1)S(1)}, u32[]{:S(2)}, u32[]{:S(2)}) collective-permute-start(bf16[128,1536]{1,0:T(8,128)(2,1)S(1)} %get-tuple-element.65), channel_id=1, source_target_pairs={{0,128},{32,160},{64,192},{96,224},{1,129},{33,161},{65,193},{97,2... | collective-permute-start | bytes 1179656 | tf_op jit(solution)/shard_map/ppermute | solution.py:38
  139.0 12.7 %collective-permute-start.27 = (bf16[128,1536]{1,0:T(8,128)(2,1)S(1)}, bf16[128,1536]{1,0:T(8,128)(2,1)S(1)}, u32[]{:S(2)}, u32[]{:S(2)}) collective-permute-start(bf16[128,1536]{1,0:T(8,128)(2,1)S(1)} %get-tuple-element.65), channel_id=1, source_target_pairs={{0,64},{32,96},{64,128},{96,160},{128,192},{160,224},{1,65},{33,97... | collective-permute-start | bytes 1179656 | tf_op jit(solution)/shard_map/ppermute | solution.py:38
  140.3 20.3 %collective-permute-start.28 = (bf16[128,1536]{1,0:T(8,128)(2,1)S(1)}, bf16[128,1536]{1,0:T(8,128)(2,1)S(1)}, u32[]{:S(2)}, u32[]{:S(2)}) collective-permute-start(bf16[128,1536]{1,0:T(8,128)(2,1)S(1)} %get-tuple-element.65), channel_id=1, source_target_pairs={{0,192},{32,224},{1,193},{33,225},{2,194},{34,226},{3,195},{35,227... | collective-permute-start | bytes 1179656 | tf_op jit(solution)/shard_map/ppermute | solution.py:38
  160.9 1.9 %collective-permute-start.29 = (bf16[128,1536]{1,0:T(8,128)(2,1)S(1)}, bf16[128,1536]{1,0:T(8,128)(2,1)S(1)}, u32[]{:S(2)}, u32[]{:S(2)}) collective-permute-start(bf16[128,1536]{1,0:T(8,128)(2,1)S(1)} %add_convert_fusion), channel_id=1, source_target_pairs={{0,32},{32,0},{64,96},{96,64},{128,160},{160,128},{192,224},{224,1... | collective-permute-start | bytes 1179656 | tf_op jit(solution)/shard_map/ppermute | solution.py:42
  162.3 1.4 copy-start.12

commit v7 on v6

--- a/solution.py
+++ b/solution.py
@@ -358,7 +358,8 @@
     near_half = (jnp.arange(2, dtype=jnp.int32) == core)[:, None, None]
     own32 = own.astype(F32)
     velocity = jnp.where(near_half, own[None], rest[None]).reshape(rows, width)
-    two, velocity = lax.optimization_barrier((two, velocity))
+    rest_part = size_own * rest.astype(F32)
+    two, velocity, rest_part = lax.optimization_barrier((two, velocity, rest_part))
     even = jnp.where(core == 0, size_own, 0.0)
     odd = jnp.where(core == 1, size_other, 0.0)
     sums = one.astype(F32) + two.astype(F32) + three.astype(F32)
@@ -366,7 +367,7 @@
     one, two, three, own = lax.optimization_barrier((one, two, three, own))
     sums = one.astype(F32) + two.astype(F32) + three.astype(F32)
     own_part = sums + odd * other.astype(F32) + size_own * own.astype(F32)
-    rest_part = earlier.astype(F32) + size_own * rest.astype(F32)
+    rest_part = earlier.astype(F32) + rest_part
     advanced = anchor.reshape(parts) + jnp.where(near_half, own_part[None], rest_part[None])
     advanced = advanced.reshape(rows, width)
     return (velocity[None], advanced[None])

time: 166 us -> 167 us (level)
  transfers between devices with their start and end apart: 31 -> 31, of which waited for: 17 -> 17; matrix products, arithmetic and copies ran while one was open for 9% -> 10% of each run, Pallas kernels for 16% -> 16%
where the time goes in v7:
time: 167 us
  waiting for transfers between devices  63.8 us (38%)
  starting transfers between devices  43.1 us (26%)
  Pallas kernels  28.8 us (17%)
  local copies, waits for them, and re-layouts  18.1 us (11%)
  other arithmetic  6.83 us (4%)
  between operations  6 us (4%)
    ppermute x6, waiting for transfers between devices, z_shift(): return lax.ppermute(block, 'frame', pairs)  29.5 us
    pallas_call x1, Pallas kernels, attend(): pl.pallas_call(attend_kernel, in_specs=[smem, smem, pl.BlockSpec(memory_s...  24.4 us
    ppermute x3, waiting for transfers between devices, x_later(): return lax.ppermute(block, 'step', pairs)  17.2 us
    ppermute x7, waiting for transfers between devices, y_shift(): return lax.ppermute(block, 'frame', pairs)  14 us
    ppermute x8, starting transfers between devices, core_swap(): return lax.ppermute(block, 'step', [(i, i ^ 1) for i in range(2 * NX)])  9.96 us
    ppermute x7, starting transfers between devices, y_shift(): return lax.ppermute(block, 'frame', pairs)  9.91 us
    all_to_all x1, starting transfers between devices, on_device(): column = lax.all_to_all(packed, 'frame', 0, 0, axis_index_groups=columns_z)  7.56 us
    ppermute x6, starting transfers between devices, z_shift(): return lax.ppermute(block, 'frame', pairs)  6.52 us
  transfers between devices with their start and end apart: 31, of which 17 were waited for; matrix products, arithmetic and copies ran while one was open for 10% of the time, Pallas kernels for 16%

profile of v7, /device:TPU:79, one launch (start us, length us, event | category | flops | bytes accessed | tf_op | source)
XLA Modules:
  0.0 166.6 jit_solution(1235074544581900216)
XLA Ops:
  0.7 2.1 %collective-permute-start = (bf16[256,1536]{1,0:T(8,128)(2,1)}, bf16[256,1536]{1,0:T(8,128)(2,1)S(1)}, u32[]{:S(2)}, u32[]{:S(2)}) collective-permute-start(bf16[256,1536]{1,0:T(8,128)(2,1)} %bitcast.39), channel_id=1, source_target_pairs={{0,2},{1,3},{2,0},{3,1},{4,6},{5,7},{6,4},{7,5},{8,10},{9,11},{10,... | collective-permute-start | bytes 2359304 | tf_op jit(solution)/shard_map/ppermute | solution.py:23
  2.8 0.7 reshape.54
  3.5 0.8 pad_maximum_fusion.1
  4.3 0.7 broadcast_in_dim.75
  5.0 7.6 %all-to-all-start = ((bf16[8,8,2304]{2,1,0:T(8,128)(2,1)}), bf16[8,8,2304]{2,1,0:T(8,128)(2,1)}, u32[]{:S(2)}, u32[]{:S(2)}) async-start(bf16[8,8,2304]{2,1,0:T(8,128)(2,1)} %broadcast_in_dim.75), calls=%async_computation | async-start | bytes 589824 | tf_op jit(solution)/shard_map/all_to_all | solution.py:312
  12.6 1.4 fusion.2
  17.9 1.1 copy-done.2
  19.0 1.2 modulate.2.refs_0_
  20.2 0.6 fusion.1
  21.0 0.9 copy-done.3
  21.8 1.0 collective-permute-start.1
  22.8 1.5 collective-permute-start.2
  24.3 1.6 collective-permute-start.3
  25.9 1.6 collective-permute-start.4
  27.6 1.0 bitcast_dynamic-update-slice_fusion.3
  28.7 7.8 %collective-permute-done.2 = bf16[64,2304]{1,0:T(8,128)(2,1)S(1)} collective-permute-done((bf16[64,2304]{1,0:T(8,128)(2,1)}, bf16[64,2304]{1,0:T(8,128)(2,1)S(1)}, u32[]{:S(2)}, u32[]{:S(2)}) %collective-permute-start.2) | collective-permute-done | bytes 294944 | tf_op jit(solution)/shard_map/ppermute | solution.py:23
  36.5 1.2 collective-permute-done.3
  37.7 4.7 %collective-permute-done.4.refs_1_ = bf16[256,1536]{1,0:T(8,128)(2,1)S(1)} collective-permute-done((bf16[256,1536]{1,0:T(8,128)(2,1)S(1)}, bf16[256,1536]{1,0:T(8,128)(2,1)S(1)}, u32[]{:S(2)}, u32[]{:S(2)}) %collective-permute-start.4) | collective-permute-done | bytes 786464 | tf_op jit(solution)/shard_map/ppermute | solution.py:28
  42.4 3.1 %collective-permute-done.5.refs_2_ = bf16[256,1536]{1,0:T(8,128)(2,1)S(1)} collective-permute-done((bf16[256,1536]{1,0:T(8,128)(2,1)S(1)}, bf16[256,1536]{1,0:T(8,128)(2,1)S(1)}, u32[]{:S(2)}, u32[]{:S(2)}) %collective-permute-start.5) | collective-permute-done | bytes 786464 | tf_op jit(solution)/shard_map/ppermute | solution.py:28
  45.5 2.2 %reshape.60.refs_11_ = bf16[192,2304]{1,0:T(8,128)(2,1)} reshape(bf16[8,4,6,2304]{3,2,1,0:T(8,128)(2,1)} %bitcast.41) | data formatting | bytes 1769472 | tf_op jit(solution)/shard_map/reshape | solution.py:322
  47.9 1.4 broadcast_select_fusion.1
  49.3 1.5 collective-permute-start.9
  50.8 2.4 %collective-permute-start.7 = (bf16[256,1536]{1,0:T(8,128)(2,1)S(1)}, bf16[256,1536]{1,0:T(8,128)(2,1)}, u32[]{:S(2)}, u32[]{:S(2)}) collective-permute-start(bf16[256,1536]{1,0:T(8,128)(2,1)S(1)} %collective-permute-done.4.refs_1_), channel_id=1, source_target_pairs={{0,4},{1,5},{2,6},{3,7},{4,8},{5,9},{6,10},{7,11},{8,12},{9,13},{1... | collective-permute-start | bytes 2359304 | tf_op jit(solution)/shard_map/ppermute | solution.py:28
  53.2 1.1 copy-done.4
  54.3 1.2 modulate.3.refs_3_
  55.5 0.9 copy-done.5
  56.4 2.3 %slice.13 = bf16[8,4,2,2304]{3,2,1,0:T(2,128)(2,1)} slice(bf16[8,4,8,2304]{3,2,1,0:T(8,128)(2,1)} %copy-done.11), slice={[0:8], [0:4], [6:8], [0:2304]} | slice | bytes 589824 | tf_op jit(solution)/shard_map/slice | solution.py:323
  58.7 1.9 %reshape.61 = bf16[96,1536]{1,0:T(8,128)(2,1)} reshape(bf16[8,4,2,2304]{3,2,1,0:T(2,128)(2,1)} %slice.13) | data formatting | bytes 589824 | tf_op jit(solution)/shard_map/reshape | solution.py:323
  60.5 4.5 %collective-permute-done.10.refs_7_ = bf16[256,1536]{1,0:T(8,128)(2,1)} collective-permute-done((bf16[256,1536]{1,0:T(8,128)(2,1)}, bf16[256,1536]{1,0:T(8,128)(2,1)}, u32[]{:S(2)}, u32[]{:S(2)}) %collective-permute-start.10) | collective-permute-done | bytes 786464 | tf_op jit(solution)/shard_map/ppermute | solution.py:23
  65.1 0.4 collective-permute-done.9.refs_6_
  65.8 1.8 %collective-permute-done.8.refs_5_ = bf16[256,1536]{1,0:T(8,128)(2,1)} collective-permute-done((bf16[256,1536]{1,0:T(8,128)(2,1)S(1)}, bf16[256,1536]{1,0:T(8,128)(2,1)}, u32[]{:S(2)}, u32[]{:S(2)}) %collective-permute-start.8) | collective-permute-done | bytes 786464 | tf_op jit(solution)/shard_map/ppermute | solution.py:28
  67.6 1.3 collective-permute-start.11
  68.9 1.4 collective-permute-start.12
  70.4 2.3 %collective-permute-start.15 = (bf16[256,1536]{1,0:T(8,128)(2,1)S(1)}, bf16[256,1536]{1,0:T(8,128)(2,1)S(1)}, u32[]{:S(2)}, u32[]{:S(2)}) collective-permute-start(bf16[256,1536]{1,0:T(8,128)(2,1)S(1)} %broadcast_select_fusion), channel_id=1, source_target_pairs={{0,2},{1,3},{2,0},{3,1},{4,6},{5,7},{6,4},{7,5},{8,10},{9,11},{10,... | collective-permute-start | bytes 2359304 | tf_op jit(solution)/shard_map/ppermute | solution.py:23
  72.6 6.5 %collective-permute-start.16 = (bf16[96,1536]{1,0:T(8,128)(2,1)S(1)}, bf16[96,1536]{1,0:T(8,128)(2,1)S(1)}, u32[]{:S(2)}, u32[]{:S(2)}) collective-permute-start(bf16[96,1536]{1,0:T(8,128)(2,1)S(1)} %copy-done.13), channel_id=1, source_target_pairs={{0,32},{32,0},{64,96},{96,64},{128,160},{160,128},{192,224},{224,1... | collective-permute-start | bytes 884744 | tf_op jit(solution)/shard_map/ppermute | solution.py:42
  79.1 1.0 slice.14
  80.2 1.3 collective-permute-start.13
  81.5 1.0 slice.15
  82.5 1.2 collective-permute-start.14
  83.8 10.4 %collective-permute-done.13.refs_9_ = bf16[128,1536]{1,0:T(8,128)(2,1)S(1)} collective-permute-done((bf16[128,1536]{1,0:T(8,128)(2,1)S(1)}, bf16[128,1536]{1,0:T(8,128)(2,1)S(1)}, u32[]{:S(2)}, u32[]{:S(2)}) %collective-permute-start.13) | collective-permute-done | bytes 393248 | tf_op jit(solution)/shard_map/ppermute | solution.py:28
  94.2 0.8 collective-permute-start.17
  95.0 9.2 %collective-permute-done.14.refs_10_ = bf16[128,1536]{1,0:T(8,128)(2,1)S(1)} collective-permute-done((bf16[128,1536]{1,0:T(8,128)(2,1)S(1)}, bf16[128,1536]{1,0:T(8,128)(2,1)S(1)}, u32[]{:S(2)}, u32[]{:S(2)}) %collective-permute-start.14) | collective-permute-done | bytes 393248 | tf_op jit(solution)/shard_map/ppermute | solution.py:28
  104.1 0.6 collective-permute-start.18
  104.8 0.5 collective-permute-start.20
  105.4 1.5 collective-permute-start.23
  107.2 0.9 collective-permute-start.24
  108.1 1.2 collective-permute-done.20.refs_18_
  109.3 24.4 %attend.1 = (bf16[128,768]{1,0:T(8,128)(2,1)S(1)}, bf16[128,768]{1,0:T(8,128)(2,1)S(1)}) custom-call(s32[4]{0:T(128)S(1)} %pad_add_fusion.where_ref, s32[2,64]{1,0:T(2,128)S(1)} %copy-done.10, f32[2,768]{1,0:T(2,128)S(1)} %copy-done.9, bf16[256,1536]{1,0:T(8,128)(2,1)S(1)} %modulate.2.refs_0_, bf16[256,1536]{1,0:T(8,128)(2,1)S(1)} %collective-permute-done.4.refs_1_, ...), custom_call_target="tpu_custom_call" | custom-call | flops 16000000000 | bytes 16000000 | tf_op jit(solution)/shard_map/attend/pallas_call | solution.py:190
  133.7 0.5 collective-permute-start.21
  134.2 1.1 collective-permute-done.21.got_ref
  135.3 2.0 %output.1 = (bf16[128,1536]{1,0:T(8,128)(2,1)S(1)}, bf16[128,1536]{1,0:T(8,128)(2,1)S(1)}, bf16[128,1536]{1,0:T(8,128)(2,1)S(1)}) custom-call(s32[4]{0:T(128)S(1)} %pad_add_fusion.where_ref, s32[8]{0:T(128)S(1)} %copy-done.7, f32[50]{0:T(128)S(1)} %copy-done.8, bf16[128,768]{1,0:T(8,128)(2,1)S(1)} %get-tuple-element.63.keep_ref, ...), custom_call_target="tpu_custom_call" | custom-call | tf_op jit(solution)/shard_map/output/pallas_call | solution.py:258
  137.3 0.5 collective-permute-start.26
  139.1 1.3 collective-permute-start.25
  140.4 1.3 collective-permute-start.27
  141.7 1.3 collective-permute-start.28
  143.0 1.0 bitcast_select_fusion.1
  144.0 0.7 convert_multiply_fusion
  144.7 8.4 %collective-permute-done.25 = bf16[128,1536]{1,0:T(8,128)(2,1)S(1)} collective-permute-done((bf16[128,1536]{1,0:T(8,128)(2,1)S(1)}, bf16[128,1536]{1,0:T(8,128)(2,1)S(1)}, u32[]{:S(2)}, u32[]{:S(2)}) %collective-permute-start.25) | collective-permute-done | bytes 393248 | tf_op jit(solution)/shard_map/ppermute | solution.py:38
  153.1 8.9 %collective-permute-done.28 = bf16[128,1536]{1,0:T(8,128)(2,1)S(1)} collective-permute-done((bf16[128,1536]{1,0:T(8,128)(2,1)S(1)}, bf16[128,1536]{1,0:T(8,128)(2,1)S(1)}, u32[]{:S(2)}, u32[]{:S(2)}) %collective-permute-start.28) | collective-permute-done | bytes 393248 | tf_op jit(solution)/shard_map/ppermute | solution.py:38
  162.2 0.6 collective-permute-start.29
  162.7 0.9 multiply_add_fusion
  163.7 0.4 collective-permute-done.29
  164.2 0.9 copy-done.12
  165.1 1.5 fusion
  (57 shorter events, 1.9 us)
Async XLA Ops:
  0.6 17.2 %copy-start.7 = (s32[8]{0:T(128)S(1)}, s32[8]{0:T(128)}, u32[]{:S(2)}) copy-start(s32[8]{0:T(128)} %index_ref.5) | copy-start | bytes 100
  0.6 17.2 %copy-start = (f32[50,3,1536]{2,0,1:T(8,128)S(1)}, f32[50,3,1536]{2,0,1:T(8,128)}, u32[]{:S(2)}) copy-start(f32[50,3,1536]{2,0,1:T(8,128)} %param.12) | copy-start | bytes 2764804
  0.7 20.3 %collective-permute-start = (bf16[256,1536]{1,0:T(8,128)(2,1)}, bf16[256,1536]{1,0:T(8,128)(2,1)S(1)}, u32[]{:S(2)}, u32[]{:S(2)}) collective-permute-start(bf16[256,1536]{1,0:T(8,128)(2,1)} %bitcast.39), channel_id=1, source_target_pairs={{0,2},{1,3},{2,0},{3,1},{4,6},{5,7},{6,4},{7,5},{8,10},{9,11},{10,... | collective-permute-start | bytes 2359304 | tf_op jit(solution)/shard_map/ppermute | solution.py:23
  5.0 15.8 %all-to-all-start = ((bf16[8,8,2304]{2,1,0:T(8,128)(2,1)}), bf16[8,8,2304]{2,1,0:T(8,128)(2,1)}, u32[]{:S(2)}, u32[]{:S(2)}) async-start(bf16[8,8,2304]{2,1,0:T(8,128)(2,1)} %broadcast_in_dim.75), calls=%async_computation | async-start | bytes 589824 | tf_op jit(solution)/shard_map/all_to_all | solution.py:312
  17.9 1.1 copy-start.2
  19.0 1.2 copy-start.8
  21.0 0.9 copy-start.3
  21.8 6.8 %collective-permute-start.1 = (bf16[64,2304]{1,0:T(8,128)(2,1)}, bf16[64,2304]{1,0:T(8,128)(2,1)S(1)}, u32[]{:S(2)}, u32[]{:S(2)}) collective-permute-start(bf16[64,2304]{1,0:T(8,128)(2,1)} %bitcast.5), channel_id=1, source_target_pairs={{0,3},{1,0},{2,1},{3,2},{4,7},{5,4},{6,5},{7,6},{8,11},{9,8},{10,9... | collective-permute-start | bytes 884744 | tf_op jit(solution)/shard_map/ppermute | solution.py:23
  22.8 13.6 %collective-permute-start.2 = (bf16[64,2304]{1,0:T(8,128)(2,1)}, bf16[64,2304]{1,0:T(8,128)(2,1)S(1)}, u32[]{:S(2)}, u32[]{:S(2)}) collective-permute-start(bf16[64,2304]{1,0:T(8,128)(2,1)} %bitcast.5), channel_id=1, source_target_pairs={{0,2},{1,3},{2,0},{3,1},{4,6},{5,7},{6,4},{7,5},{8,10},{9,11},{10,... | collective-permute-start | bytes 884744 | tf_op jit(solution)/shard_map/ppermute | solution.py:23
  24.3 13.4 %collective-permute-start.3 = (bf16[64,2304]{1,0:T(8,128)(2,1)}, bf16[64,2304]{1,0:T(8,128)(2,1)S(1)}, u32[]{:S(2)}, u32[]{:S(2)}) collective-permute-start(bf16[64,2304]{1,0:T(8,128)(2,1)} %bitcast.5), channel_id=1, source_target_pairs={{0,1},{1,2},{2,3},{3,0},{4,5},{5,6},{6,7},{7,4},{8,9},{9,10},{10,1... | collective-permute-start | bytes 884744 | tf_op jit(solution)/shard_map/ppermute | solution.py:23
  25.9 16.5 %collective-permute-start.4 = (bf16[256,1536]{1,0:T(8,128)(2,1)S(1)}, bf16[256,1536]{1,0:T(8,128)(2,1)S(1)}, u32[]{:S(2)}, u32[]{:S(2)}) collective-permute-start(bf16[256,1536]{1,0:T(8,128)(2,1)S(1)} %modulate.2.refs_0_), channel_id=1, source_target_pairs={{0,4},{1,5},{2,6},{3,7},{4,8},{5,9},{6,10},{7,11},{8,12},{9,13},{1... | collective-permute-start | bytes 2359304 | tf_op jit(solution)/shard_map/ppermute | solution.py:28
  27.5 18.0 %collective-permute-start.5 = (bf16[256,1536]{1,0:T(8,128)(2,1)S(1)}, bf16[256,1536]{1,0:T(8,128)(2,1)S(1)}, u32[]{:S(2)}, u32[]{:S(2)}) collective-permute-start(bf16[256,1536]{1,0:T(8,128)(2,1)S(1)} %modulate.2.refs_0_), channel_id=1, source_target_pairs={{0,28},{1,29},{2,30},{3,31},{4,0},{5,1},{6,2},{7,3},{8,4},{9,5},{1... | collective-permute-start | bytes 2359304 | tf_op jit(solution)/shard_map/ppermute | solution.py:28
  37.7 7.8 %copy-start.11 = (bf16[8,4,8,2304]{3,2,1,0:T(8,128)(2,1)}, bf16[8,4,8,2304]{3,2,1,0:T(8,128)(2,1)S(1)}, u32[]{:S(2)}) copy-start(bf16[8,4,8,2304]{3,2,1,0:T(8,128)(2,1)S(1)} %bitcast_dynamic-update-slice_fusion) | copy-start | bytes 3538948
  47.7 19.9 %collective-permute-start.6 = (bf16[192,2304]{1,0:T(8,128)(2,1)}, bf16[192,2304]{1,0:T(8,128)(2,1)}, u32[]{:S(2)}, u32[]{:S(2)}) collective-permute-start(bf16[192,2304]{1,0:T(8,128)(2,1)} %reshape.60.refs_11_), channel_id=1, source_target_pairs={{0,64},{32,96},{64,128},{96,160},{128,192},{160,224},{192,0},{224,... | collective-permute-start | bytes 2654216 | tf_op jit(solution)/shard_map/ppermute | solution.py:33
  49.3 15.8 %collective-permute-start.10 = (bf16[256,1536]{1,0:T(8,128)(2,1)}, bf16[256,1536]{1,0:T(8,128)(2,1)}, u32[]{:S(2)}, u32[]{:S(2)}) collective-permute-start(bf16[256,1536]{1,0:T(8,128)(2,1)} %get-tuple-element.78), channel_id=1, source_target_pairs={{0,3},{1,0},{2,1},{3,2},{4,7},{5,4},{6,5},{7,6},{8,11},{9,8},{10,9... | collective-permute-start | bytes 2359304 | tf_op jit(solution)/shard_map/ppermute | solution.py:23
  49.3 16.1 %collective-permute-start.9 = (bf16[256,1536]{1,0:T(8,128)(2,1)}, bf16[256,1536]{1,0:T(8,128)(2,1)}, u32[]{:S(2)}, u32[]{:S(2)}) collective-permute-start(bf16[256,1536]{1,0:T(8,128)(2,1)} %get-tuple-element.79), channel_id=1, source_target_pairs={{0,1},{1,2},{2,3},{3,0},{4,5},{5,6},{6,7},{7,4},{8,9},{9,10},{10,1... | collective-permute-start | bytes 2359304 | tf_op jit(solution)/shard_map/ppermute | solution.py:23
  50.8 15.0 %collective-permute-start.7 = (bf16[256,1536]{1,0:T(8,128)(2,1)S(1)}, bf16[256,1536]{1,0:T(8,128)(2,1)}, u32[]{:S(2)}, u32[]{:S(2)}) collective-permute-start(bf16[256,1536]{1,0:T(8,128)(2,1)S(1)} %collective-permute-done.4.refs_1_), channel_id=1, source_target_pairs={{0,4},{1,5},{2,6},{3,7},{4,8},{5,9},{6,10},{7,11},{8,12},{9,13},{1... | collective-permute-start | bytes 2359304 | tf_op jit(solution)/shard_map/ppermute | solution.py:28
  53.2 14.4 %collective-permute-start.8 = (bf16[256,1536]{1,0:T(8,128)(2,1)S(1)}, bf16[256,1536]{1,0:T(8,128)(2,1)}, u32[]{:S(2)}, u32[]{:S(2)}) collective-permute-start(bf16[256,1536]{1,0:T(8,128)(2,1)S(1)} %collective-permute-done.5.refs_2_), channel_id=1, source_target_pairs={{0,28},{1,29},{2,30},{3,31},{4,0},{5,1},{6,2},{7,3},{8,4},{9,5},{1... | collective-permute-start | bytes 2359304 | tf_op jit(solution)/shard_map/ppermute | solution.py:28
  53.2 1.1 copy-start.4
  55.5 0.9 copy-start.5
  60.5 12.1 %copy-start.13 = (bf16[96,1536]{1,0:T(8,128)(2,1)S(1)}, bf16[96,1536]{1,0:T(8,128)(2,1)}, u32[]{:S(2)}) copy-start(bf16[96,1536]{1,0:T(8,128)(2,1)} %reshape.61) | copy-start | bytes 884740
  67.6 37.1 %collective-permute-start.11 = (bf16[192,2304]{1,0:T(8,128)(2,1)}, bf16[192,2304]{1,0:T(8,128)(2,1)S(1)}, u32[]{:S(2)}, u32[]{:S(2)}) collective-permute-start(bf16[192,2304]{1,0:T(8,128)(2,1)} %reshape.60.refs_11_), channel_id=1, source_target_pairs={{0,192},{32,224},{64,0},{96,32},{128,64},{160,96},{192,128},{224,1... | collective-permute-start | bytes 2654216 | tf_op jit(solution)/shard_map/ppermute | solution.py:33
  68.9 35.9 %collective-permute-start.12 = (bf16[192,2304]{1,0:T(8,128)(2,1)}, bf16[192,2304]{1,0:T(8,128)(2,1)S(1)}, u32[]{:S(2)}, u32[]{:S(2)}) collective-permute-start(bf16[192,2304]{1,0:T(8,128)(2,1)} %collective-permute-done.6.refs_12_), channel_id=1, source_target_pairs={{0,64},{32,96},{64,128},{96,160},{128,192},{160,224},{192,0},{224,... | collective-permute-start | bytes 2654216 | tf_op jit(solution)/shard_map/ppermute | solution.py:33
  70.4 34.4 %collective-permute-start.15 = (bf16[256,1536]{1,0:T(8,128)(2,1)S(1)}, bf16[256,1536]{1,0:T(8,128)(2,1)S(1)}, u32[]{:S(2)}, u32[]{:S(2)}) collective-permute-start(bf16[256,1536]{1,0:T(8,128)(2,1)S(1)} %broadcast_select_fusion), channel_id=1, source_target_pairs={{0,2},{1,3},{2,0},{3,1},{4,6},{5,7},{6,4},{7,5},{8,10},{9,11},{10,... | collective-permute-start | bytes 2359304 | tf_op jit(solution)/shard_map/ppermute | solution.py:23
  72.6 9.9 %collective-permute-start.16 = (bf16[96,1536]{1,0:T(8,128)(2,1)S(1)}, bf16[96,1536]{1,0:T(8,128)(2,1)S(1)}, u32[]{:S(2)}, u32[]{:S(2)}) collective-permute-start(bf16[96,1536]{1,0:T(8,128)(2,1)S(1)} %copy-done.13), channel_id=1, source_target_pairs={{0,32},{32,0},{64,96},{96,64},{128,160},{160,128},{192,224},{224,1... | collective-permute-start | bytes 884744 | tf_op jit(solution)/shard_map/ppermute | solution.py:42
  80.1 14.1 %copy-start.1 = (bf16[192,2304]{1,0:T(8,128)(2,1)S(1)}, bf16[192,2304]{1,0:T(8,128)(2,1)}, u32[]{:S(2)}) copy-start(bf16[192,2304]{1,0:T(8,128)(2,1)} %reshape.60.refs_11_) | copy-start | bytes 2654212
  80.1 29.2 %copy-start.6 = (bf16[256,1536]{1,0:T(8,128)(2,1)S(1)}, bf16[256,1536]{1,0:T(8,128)(2,1)}, u32[]{:S(2)}) copy-start(bf16[256,1536]{1,0:T(8,128)(2,1)} %copy-done.5) | copy-start | bytes 2359300
  80.1 29.2 %copy-start.9 = (f32[2,768]{1,0:T(2,128)S(1)}, f32[2,768]{1,0:T(2,128)}, u32[]{:S(2)}) copy-start(f32[2,768]{1,0:T(2,128)} %gain_ref.1) | copy-start | bytes 18436
  80.2 29.2 %copy-start.10 = (s32[2,64]{1,0:T(2,128)S(1)}, s32[2,64]{1,0:T(2,128)}, u32[]{:S(2)}) copy-start(s32[2,64]{1,0:T(2,128)} %mask_ref.1) | copy-start | bytes 1540
  80.2 14.0 %collective-permute-start.13 = (bf16[128,1536]{1,0:T(8,128)(2,1)S(1)}, bf16[128,1536]{1,0:T(8,128)(2,1)S(1)}, u32[]{:S(2)}, u32[]{:S(2)}) collective-permute-start(bf16[128,1536]{1,0:T(8,128)(2,1)S(1)} %slice.14), channel_id=1, source_target_pairs={{0,8},{1,9},{2,10},{3,11},{4,12},{5,13},{6,14},{7,15},{8,16},{9,17... | collective-permute-start | bytes 1179656 | tf_op jit(solution)/shard_map/ppermute | solution.py:28
  82.5 21.6 %collective-permute-start.14 = (bf16[128,1536]{1,0:T(8,128)(2,1)S(1)}, bf16[128,1536]{1,0:T(8,128)(2,1)S(1)}, u32[]{:S(2)}, u32[]{:S(2)}) collective-permute-start(bf16[128,1536]{1,0:T(8,128)(2,1)S(1)} %slice.15), channel_id=1, source_target_pairs={{0,24},{1,25},{2,26},{3,27},{4,28},{5,29},{6,30},{7,31},{8,0},{9,1... | collective-permute-start | bytes 1179656 | tf_op jit(solution)/shard_map/ppermute | solution.py:28
  94.2 11.2 %collective-permute-start.17 = (bf16[192,2304]{1,0:T(8,128)(2,1)S(1)}, bf16[192,2304]{1,0:T(8,128)(2,1)S(1)}, u32[]{:S(2)}, u32[]{:S(2)}) collective-permute-start(bf16[192,2304]{1,0:T(8,128)(2,1)S(1)} %copy-done.1), channel_id=1, source_target_pairs={{0,32},{32,0},{64,96},{96,64},{128,160},{160,128},{192,224},{224,1... | collective-permute-start | bytes 2654216 | tf_op jit(solution)/shard_map/ppermute | solution.py:42
  104.1 3.0 %collective-permute-start.18 = (bf16[192,2304]{1,0:T(8,128)(2,1)}, bf16[192,2304]{1,0:T(8,128)(2,1)S(1)}, u32[]{:S(2)}, u32[]{:S(2)}) collective-permute-start(bf16[192,2304]{1,0:T(8,128)(2,1)} %collective-permute-done.6.refs_12_), channel_id=1, source_target_pairs={{0,32},{32,0},{64,96},{96,64},{128,160},{160,128},{192,224},{224,1... | collective-permute-start | bytes 2654216 | tf_op jit(solution)/shard_map/ppermute | solution.py:42
  104.7 3.3 %collective-permute-start.19 = (bf16[192,2304]{1,0:T(8,128)(2,1)S(1)}, bf16[192,2304]{1,0:T(8,128)(2,1)S(1)}, u32[]{:S(2)}, u32[]{:S(2)}) collective-permute-start(bf16[192,2304]{1,0:T(8,128)(2,1)S(1)} %collective-permute-done.11.refs_13_), channel_id=1, source_target_pairs={{0,32},{32,0},{64,96},{96,64},{128,160},{160,128},{192,224},{224,1... | collective-permute-start | bytes 2654216 | tf_op jit(solution)/shard_map/ppermute | solution.py:42
  104.8 4.5 %collective-permute-start.20 = (bf16[192,2304]{1,0:T(8,128)(2,1)S(1)}, bf16[192,2304]{1,0:T(8,128)(2,1)S(1)}, u32[]{:S(2)}, u32[]{:S(2)}) collective-permute-start(bf16[192,2304]{1,0:T(8,128)(2,1)S(1)} %collective-permute-done.12.refs_14_), channel_id=1, source_target_pairs={{0,32},{32,0},{64,96},{96,64},{128,160},{160,128},{192,224},{224,1... | collective-permute-start | bytes 2654216 | tf_op jit(solution)/shard_map/ppermute | solution.py:42
  105.3 28.9 %collective-permute-start.22 = (bf16[2,96,1536]{2,1,0:T(8,128)(2,1)S(1)}, bf16[2,96,1536]{2,1,0:T(8,128)(2,1)S(1)}, u32[]{:S(2)}, u32[]{:S(2)}) collective-permute-start(bf16[2,96,1536]{2,1,0:T(8,128)(2,1)S(1)} %pad_maximum_fusion.refs_0_), channel_id=1, source_target_pairs={{0,64},{32,96},{64,128},{96,160},{128,192},{160,224},{192,0},{224,... | collective-permute-start | bytes 1769480 | tf_op jit(solution)/shard_map/ppermute | solution.py:33
  105.4 28.9 %collective-permute-start.23 = (bf16[2,96,1536]{2,1,0:T(8,128)(2,1)S(1)}, bf16[2,96,1536]{2,1,0:T(8,128)(2,1)S(1)}, u32[]{:S(2)}, u32[]{:S(2)}) collective-permute-start(bf16[2,96,1536]{2,1,0:T(8,128)(2,1)S(1)} %pad_maximum_fusion.refs_0_), channel_id=1, source_target_pairs={{0,192},{32,224},{64,0},{96,32},{128,64},{160,96},{192,128},{224,1... | collective-permute-start | bytes 1769480 | tf_op jit(solution)/shard_map/ppermute | solution.py:33
  107.2 27.1 %collective-permute-start.24 = (bf16[2,96,1536]{2,1,0:T(8,128)(2,1)S(1)}, bf16[2,96,1536]{2,1,0:T(8,128)(2,1)S(1)}, u32[]{:S(2)}, u32[]{:S(2)}) collective-permute-start(bf16[2,96,1536]{2,1,0:T(8,128)(2,1)S(1)} %pad_maximum_fusion.refs_0_), channel_id=1, source_target_pairs={{0,128},{32,160},{64,192},{96,224},{128,0},{160,32},{192,64},{224,... | collective-permute-start | bytes 1769480 | tf_op jit(solution)/shard_map/ppermute | solution.py:33
  133.7 1.6 collective-permute-start.21
  137.3 5.7 %collective-permute-start.26 = (bf16[128,1536]{1,0:T(8,128)(2,1)S(1)}, bf16[128,1536]{1,0:T(8,128)(2,1)S(1)}, u32[]{:S(2)}, u32[]{:S(2)}) collective-permute-start(bf16[128,1536]{1,0:T(8,128)(2,1)S(1)} %get-tuple-element.68), channel_id=1, source_target_pairs={{0,32},{32,0},{64,96},{96,64},{128,160},{160,128},{192,224},{224,1... | collective-permute-start | bytes 1179656 | tf_op jit(solution)/shard_map/ppermute | solution.py:42
  139.1 14.0 %collective-permute-start.25 = (bf16[128,1536]{1,0:T(8,128)(2,1)S(1)}, bf16[128,1536]{1,0:T(8,128)(2,1)S(1)}, u32[]{:S(2)}, u32[]{:S(2)}) collective-permute-start(bf16[128,1536]{1,0:T(8,128)(2,1)S(1)} %get-tuple-element.66), channel_id=1, source_target_pairs={{0,128},{32,160},{64,192},{96,224},{1,129},{33,161},{65,193},{97,2... | collective-permute-start | bytes 1179656 | tf_op jit(solution)/shard_map/ppermute | solution.py:38
  140.4 12.7 %collective-permute-start.27 = (bf16[128,1536]{1,0:T(8,128)(2,1)S(1)}, bf16[128,1536]{1,0:T(8,128)(2,1)S(1)}, u32[]{:S(2)}, u32[]{:S(2)}) collective-permute-start(bf16[128,1536]{1,0:T(8,128)(2,1)S(1)} %get-tuple-element.66), channel_id=1, source_target_pairs={{0,64},{32,96},{64,128},{96,160},{128,192},{160,224},{1,65},{33,97... | collective-permute-start | bytes 1179656 | tf_op jit(solution)/shard_map/ppermute | solution.py:38
  141.7 20.3 %collective-permute-start.28 = (bf16[128,1536]{1,0:T(8,128)(2,1)S(1)}, bf16[128,1536]{1,0:T(8,128)(2,1)S(1)}, u32[]{:S(2)}, u32[]{:S(2)}) collective-permute-start(bf16[128,1536]{1,0:T(8,128)(2,1)S(1)} %get-tuple-element.66), channel_id=1, source_target_pairs={{0,192},{32,224},{1,193},{33,225},{2,194},{34,226},{3,195},{35,227... | collective-permute-start | bytes 1179656 | tf_op jit(solution)/shard_map/ppermute | solution.py:38
  162.2 1.9 %collective-permute-start.29 = (bf16[128,1536]{1,0:T(8,128)(2,1)S(1)}, bf16[128,1536]{1,0:T(8,128)(2,1)S(1)}, u32[]{:S(2)}, u32[]{:S(2)}) collective-permute-start(bf16[128,1536]{1,0:T(8,128)(2,1)S(1)} %add_convert_fusion), channel_id=1, source_target_pairs={{0,32},{32,0},{64,96},{96,64},{128,160},{160,128},{192,224},{224,1... | collective-permute-start | bytes 1179656 | tf_op jit(solution)/shard_map/ppermute | solution.py:42
  163.6 1.4 copy-start.12
